TPU v7x, 32 devices: a whole 2x2x4 slice. The times are simulated.
32 devices in a mesh: expert: 8 (over z, y), dp: 4 (over x, core).
Axes of the slice: x: 2, y: 2, z: 4, core: 2. Of those that a mesh axis runs over, the one named last changes fastest.
Arguments:
- block_input: bfloat16 [4, 12288, 1024], P('dp', 'expert'), may hold values from -6 to 6
- expert_ids: int32 [4, 8192], P('dp', 'expert'), may hold values from 0 to 7, as said below
- ln1_gain: float32 [1024], replicated, may hold values from 0.1 to 1.9
- ln1_bias: float32 [1024], replicated, may hold values from -3 to 3
- w_qkv: bfloat16 [1024, 3072], replicated, may hold values from -0.1875 to 0.1875
- w_o: bfloat16 [1024, 1024], replicated, may hold values from -2 to 2
- ln2_gain: float32 [1024], replicated, may hold values from 0.1 to 1.9
- ln2_bias: float32 [1024], replicated, may hold values from -3 to 3
- w_in: bfloat16 [8, 4096, 1024], P('expert', 'dp'), may hold values from -0.1875 to 0.1875
- b_in: bfloat16 [8, 4096], P('expert', 'dp'), may hold values from -4 to 4
- w_out: bfloat16 [8, 4096, 1024], P('expert', 'dp'), may hold values from -0.09375 to 0.09375
- b_out: bfloat16 [8, 1024], P('expert', 'dp'), may hold values from -3 to 3
- cotangent: bfloat16 [4, 12288, 1024], P('dp', 'expert'), may hold values from -6 to 6
Outputs:
- out: bfloat16 [4, 12288, 1024], P('dp', 'expert')
- grad_input: bfloat16 [4, 12288, 1024], P('dp', 'expert')
- grad_ln1_gain: float32 [1024], replicated
- grad_ln1_bias: float32 [1024], replicated
- grad_w_qkv: float32 [1024, 3072], replicated
- grad_w_o: float32 [1024, 1024], replicated
- grad_ln2_gain: float32 [1024], replicated
- grad_ln2_bias: float32 [1024], replicated
- grad_w_in: float32 [8, 4096, 1024], P('expert', 'dp')
- grad_b_in: float32 [8, 4096], P('expert', 'dp')
- grad_w_out: float32 [8, 4096, 1024], P('expert', 'dp')
- grad_b_out: float32 [8, 1024], P('expert', 'dp')
Inputs may be any that keep to these rules, and one draw needn't show every extreme that they name: `expert_ids`: in each group every expert takes exactly 640 tokens of one sequence of the group and at least 1 but fewer than 640 tokens of each other sequence; one expert, drawn from the seed, takes exactly 1536 tokens of the group in all, every other expert fewer.
All inputs are finite; a program needn't handle non-finite values.
Results may differ from a plain program's by a relative error of at most 0.012.
Values may be sent and summed in bfloat16 or wider, within the bound.
A program may use at most 384 MiB of HBM per device.

v0:
```python
import jax
import jax.numpy as jnp
from jax import lax
from jax.sharding import PartitionSpec as P

HEADS = 16
HEAD_DIM = 64


epsilon = 1e-05
gelu_c = 0.7978845608028654
contract_last = (((1,), (1,)), ((), ()))
contract_first = (((0,), (0,)), ((), ()))


def normalize(values_in, gains, offsets):
    centre = jnp.mean(values_in, axis=-1, keepdims=True)
    centred = values_in - centre
    spread = jnp.mean(centred * centred, axis=-1, keepdims=True)
    inverse = lax.rsqrt(spread + epsilon)
    scaled = centred * inverse
    return (scaled * gains + offsets, scaled, inverse)


def normalize_back(grad_output, scaled, inverse, gains):
    grad_scaled = grad_output * gains
    first_mean = jnp.mean(grad_scaled, axis=-1, keepdims=True)
    second_mean = jnp.mean(grad_scaled * scaled, axis=-1, keepdims=True)
    grad_values = inverse * (grad_scaled - first_mean - scaled * second_mean)
    return (grad_values, jnp.sum(grad_output * scaled, axis=0), jnp.sum(grad_output, axis=0))


def smooth_gelu(pre_act):
    inner_arg = gelu_c * (pre_act + 0.044715 * pre_act * pre_act * pre_act)
    return 0.5 * pre_act * (1.0 + jnp.tanh(inner_arg))


def gelu_slope(pre_act):
    tangent = jnp.tanh(gelu_c * (pre_act + 0.044715 * pre_act * pre_act * pre_act))
    return 0.5 * (1.0 + tangent) + 0.5 * pre_act * (1.0 - tangent * tangent) * gelu_c * (
        1.0 + 3.0 * 0.044715 * pre_act * pre_act
    )


def causal_mask(first_row, height, breadth):
    row_pos = first_row + lax.broadcasted_iota(jnp.int32, (height, breadth), 0)
    col_pos = lax.broadcasted_iota(jnp.int32, (height, breadth), 1)
    return col_pos <= row_pos


def block_scores(block_queries, keys_part, first_row):
    scores = (
        jnp.einsum("qhd,khd->hqk", block_queries, keys_part, preferred_element_type=jnp.float32)
        * 0.125
    )
    allowed = causal_mask(first_row, block_queries.shape[0], keys_part.shape[0])
    return jnp.where(allowed[None], scores, -1e30)


def attend_forward(queries, keys_all, values_all):
    length = queries.shape[0]
    step_rows = min(512, length)
    outputs = []
    log_totals = []
    for first_row in range(0, length, step_rows):
        last_row = first_row + step_rows
        scores = block_scores(queries[first_row:last_row], keys_all[:last_row], first_row)
        row_peak = jnp.max(scores, axis=-1, keepdims=True)
        exponent = jnp.exp(scores - row_peak)
        row_total = jnp.sum(exponent, axis=-1, keepdims=True)
        weights_low = (exponent / row_total).astype(jnp.bfloat16)
        outputs.append(
            jnp.einsum(
                "hqk,khd->qhd",
                weights_low,
                values_all[:last_row],
                preferred_element_type=jnp.float32,
            )
        )
        log_totals.append(row_peak + jnp.log(row_total))
    return (jnp.concatenate(outputs, axis=0), log_totals)


def attend_backward(queries, keys_all, values_all, grad_context, log_totals):
    length = queries.shape[0]
    step_rows = min(512, length)
    grad_queries = []
    grad_keys = jnp.zeros(keys_all.shape, jnp.float32)
    grad_values = jnp.zeros(values_all.shape, jnp.float32)
    for index_block, first_row in enumerate(range(0, length, step_rows)):
        last_row = first_row + step_rows
        block_queries = queries[first_row:last_row]
        block_grad = grad_context[first_row:last_row]
        scores = block_scores(block_queries, keys_all[:last_row], first_row)
        weights_f = jnp.exp(scores - log_totals[index_block])
        weights_low = weights_f.astype(jnp.bfloat16)
        grad_weights = jnp.einsum(
            "qhd,khd->hqk", block_grad, values_all[:last_row], preferred_element_type=jnp.float32
        )
        row_centre = jnp.sum(weights_f * grad_weights, axis=-1, keepdims=True)
        grad_scores = (weights_f * (grad_weights - row_centre)).astype(jnp.bfloat16)
        grad_queries.append(
            jnp.einsum(
                "hqk,khd->qhd", grad_scores, keys_all[:last_row], preferred_element_type=jnp.float32
            )
            * 0.125
        )
        grad_keys = grad_keys.at[:last_row].add(
            jnp.einsum(
                "hqk,qhd->khd", grad_scores, block_queries, preferred_element_type=jnp.float32
            )
            * 0.125
        )
        grad_values = grad_values.at[:last_row].add(
            jnp.einsum("hqk,qhd->khd", weights_low, block_grad, preferred_element_type=jnp.float32)
        )
    return (jnp.concatenate(grad_queries, axis=0), grad_keys, grad_values)


def pad_row(matrix):
    return jnp.concatenate([matrix, jnp.zeros((1, matrix.shape[1]), matrix.dtype)], axis=0)


def pack_experts(matrix, send_rows):
    return pad_row(matrix)[send_rows]


def unpack_sequence(received, pick_sequence):
    return received.reshape(-1, received.shape[-1])[pick_sequence]


def pack_sequence(matrix, send_tokens, expert_count):
    return pad_row(matrix)[send_tokens].reshape(expert_count, -1, matrix.shape[1])


def unpack_experts(received, pick_expert):
    return pad_row(received.reshape(-1, received.shape[-1]))[pick_expert]


def body(
    block_input,
    expert_ids,
    ln1_gain,
    ln1_bias,
    w_qkv,
    w_o,
    ln2_gain,
    ln2_bias,
    w_in,
    b_in,
    w_out,
    b_out,
    cotangent,
):
    expert_count = lax.axis_size("expert")
    own_expert = lax.axis_index("expert")
    slot_rows = block_input.shape[1]
    model_width = block_input.shape[2]
    seq_ids = expert_ids[0]
    seq_length = seq_ids.shape[0]
    capacity = 5 * seq_length // expert_count
    every_id = lax.all_gather(expert_ids, "expert", axis=1, tiled=True)[0]
    from_each = jnp.sum(
        (every_id == own_expert).astype(jnp.int32).reshape(expert_count, seq_length), axis=1
    )
    ends_at = jnp.cumsum(from_each)
    starts_at = ends_at - from_each
    slot_index = jnp.arange(slot_rows, dtype=jnp.int32)
    source = jnp.minimum(
        jnp.sum((ends_at[None, :] <= slot_index[:, None]).astype(jnp.int32), axis=1),
        expert_count - 1,
    )
    occupied = slot_index < ends_at[-1]
    pick_expert = jnp.where(
        occupied, source * capacity + slot_index - starts_at[source], expert_count * capacity
    )
    position = jnp.arange(capacity, dtype=jnp.int32)
    send_rows = jnp.where(
        position[None, :] < from_each[:, None], starts_at[:, None] + position[None, :], slot_rows
    )
    choose = (seq_ids[:, None] == jnp.arange(expert_count, dtype=jnp.int32)[None, :]).astype(
        jnp.int32
    )
    rank_in = jnp.sum((jnp.cumsum(choose, axis=0) - 1) * choose, axis=1)
    pick_sequence = seq_ids * capacity + rank_in
    send_tokens = (
        jnp.full((expert_count * capacity,), seq_length, jnp.int32)
        .at[pick_sequence]
        .set(jnp.arange(seq_length, dtype=jnp.int32))
    )
    arrived = lax.all_to_all(
        pack_experts(block_input[0], send_rows), "expert", split_axis=0, concat_axis=0, tiled=True
    )
    tokens_in = unpack_sequence(arrived, pick_sequence).astype(jnp.float32)
    normed, scaled_one, inverse_one = normalize(tokens_in, ln1_gain, ln1_bias)
    normed_low = normed.astype(jnp.bfloat16)
    mixed_qkv = jnp.dot(normed_low, w_qkv, preferred_element_type=jnp.float32).astype(jnp.bfloat16)
    heads_shape = (seq_length, HEADS, HEAD_DIM)
    queries = mixed_qkv[:, :model_width].reshape(heads_shape)
    keys_all = mixed_qkv[:, model_width : 2 * model_width].reshape(heads_shape)
    values_all = mixed_qkv[:, 2 * model_width :].reshape(heads_shape)
    context, log_totals = attend_forward(queries, keys_all, values_all)
    context_low = context.reshape(seq_length, model_width).astype(jnp.bfloat16)
    hidden = tokens_in + jnp.dot(context_low, w_o, preferred_element_type=jnp.float32)
    returned = lax.all_to_all(
        pack_sequence(hidden.astype(jnp.bfloat16), send_tokens, expert_count),
        "expert",
        split_axis=0,
        concat_axis=0,
        tiled=True,
    )
    placed = unpack_experts(returned, pick_expert).astype(jnp.float32)
    normed_two, scaled_two, inverse_two = normalize(placed, ln2_gain, ln2_bias)
    inputs_low = normed_two.astype(jnp.bfloat16)
    live = occupied[:, None]
    grad_low = jnp.where(live, cotangent[0], jnp.zeros((), jnp.bfloat16))
    full_in, full_out, full_bias_in, full_bias_out = (
        lax.all_gather(w_in, "dp", axis=1, tiled=True),
        lax.all_gather(w_out, "dp", axis=1, tiled=True),
        lax.all_gather(b_in, "dp", axis=1, tiled=True),
        lax.all_gather(b_out, "dp", axis=1, tiled=True),
    )
    weight_in = full_in[0]
    weight_out = full_out[0]
    pre_act = lax.dot_general(
        inputs_low, weight_in, contract_last, preferred_element_type=jnp.float32
    ) + full_bias_in[0].astype(jnp.float32)
    act_low = smooth_gelu(pre_act).astype(jnp.bfloat16)
    expert_out = jnp.dot(act_low, weight_out, preferred_element_type=jnp.float32) + full_bias_out[
        0
    ].astype(jnp.float32)
    result = jnp.where(live, placed + expert_out, 0.0).astype(jnp.bfloat16)
    grad_act = lax.dot_general(
        grad_low, weight_out, contract_last, preferred_element_type=jnp.float32
    )
    grad_pre = (grad_act * gelu_slope(pre_act)).astype(jnp.bfloat16)
    grad_normed = jnp.dot(grad_pre, weight_in, preferred_element_type=jnp.float32)
    local_w_in = lax.dot_general(
        grad_pre, inputs_low, contract_first, preferred_element_type=jnp.float32
    )
    local_w_out = lax.dot_general(
        act_low, grad_low, contract_first, preferred_element_type=jnp.float32
    )
    local_b_in = jnp.sum(grad_pre.astype(jnp.float32), axis=0)
    local_b_out = jnp.sum(grad_low.astype(jnp.float32), axis=0)
    grad_w_in, grad_w_out, grad_b_in, grad_b_out = (
        lax.psum_scatter(
            local_w_in[None].astype(jnp.bfloat16), "dp", scatter_dimension=1, tiled=True
        ).astype(jnp.float32),
        lax.psum_scatter(
            local_w_out[None].astype(jnp.bfloat16), "dp", scatter_dimension=1, tiled=True
        ).astype(jnp.float32),
        lax.psum_scatter(
            local_b_in[None].astype(jnp.bfloat16), "dp", scatter_dimension=1, tiled=True
        ).astype(jnp.float32),
        lax.psum_scatter(
            local_b_out[None].astype(jnp.bfloat16), "dp", scatter_dimension=1, tiled=True
        ).astype(jnp.float32),
    )
    grad_placed_norm, local_ln2_gain, local_ln2_bias = normalize_back(
        grad_normed, scaled_two, inverse_two, ln2_gain
    )
    grad_placed = grad_low.astype(jnp.float32) + grad_placed_norm
    back_arrived = lax.all_to_all(
        pack_experts(grad_placed.astype(jnp.bfloat16), send_rows),
        "expert",
        split_axis=0,
        concat_axis=0,
        tiled=True,
    )
    grad_hidden = unpack_sequence(back_arrived, pick_sequence)
    local_w_o = lax.dot_general(
        context_low, grad_hidden, contract_first, preferred_element_type=jnp.float32
    )
    grad_context = (
        lax.dot_general(grad_hidden, w_o, contract_last, preferred_element_type=jnp.float32)
        .astype(jnp.bfloat16)
        .reshape(heads_shape)
    )
    grad_queries, grad_keys, grad_values = attend_backward(
        queries, keys_all, values_all, grad_context, log_totals
    )
    grad_mixed = jnp.concatenate(
        [
            grad_queries.reshape(seq_length, model_width),
            grad_keys.reshape(seq_length, model_width),
            grad_values.reshape(seq_length, model_width),
        ],
        axis=1,
    ).astype(jnp.bfloat16)
    local_w_qkv = lax.dot_general(
        normed_low, grad_mixed, contract_first, preferred_element_type=jnp.float32
    )
    grad_normed_one = lax.dot_general(
        grad_mixed, w_qkv, contract_last, preferred_element_type=jnp.float32
    )
    grad_tokens_norm, local_ln1_gain, local_ln1_bias = normalize_back(
        grad_normed_one, scaled_one, inverse_one, ln1_gain
    )
    grad_tokens = grad_hidden.astype(jnp.float32) + grad_tokens_norm
    sent_back = lax.all_to_all(
        pack_sequence(grad_tokens.astype(jnp.bfloat16), send_tokens, expert_count),
        "expert",
        split_axis=0,
        concat_axis=0,
        tiled=True,
    )
    grad_input = unpack_experts(sent_back, pick_expert)
    grad_w_qkv, grad_w_o, grad_ln1_gain, grad_ln1_bias, grad_ln2_gain, grad_ln2_bias = lax.psum(
        (local_w_qkv, local_w_o, local_ln1_gain, local_ln1_bias, local_ln2_gain, local_ln2_bias),
        ("expert", "dp"),
    )
    return (
        result[None],
        grad_input[None],
        grad_ln1_gain,
        grad_ln1_bias,
        grad_w_qkv,
        grad_w_o,
        grad_ln2_gain,
        grad_ln2_bias,
        grad_w_in,
        grad_b_in,
        grad_w_out,
        grad_b_out,
    )


def solution(mesh):
    placed = (
        P("dp", "expert", None),
        P("dp", "expert"),
        P(),
        P(),
        P(),
        P(),
        P(),
        P(),
        P("expert", "dp", None),
        P("expert", "dp"),
        P("expert", "dp", None),
        P("expert", "dp"),
        P("dp", "expert", None),
    )
    return jax.shard_map(
        body,
        mesh=mesh,
        in_specs=placed,
        out_specs=(
            P("dp", "expert", None),
            P("dp", "expert", None),
            P(),
            P(),
            P(),
            P(),
            P(),
            P(),
            P("expert", "dp", None),
            P("expert", "dp"),
            P("expert", "dp", None),
            P("expert", "dp"),
        ),
        check_vma=False,
    )
```

profile of v0, /device:TPU:24, one launch (start us, length us, event | category | flops | bytes accessed | tf_op | source)
XLA Modules:
  0.0 1773.9 jit_solution(6524035785267862154)
XLA Ops:
  7.2 28.0 %all_gather.15 = s32[1,8192]{1,0:T(1,128)S(1)} all-gather(s32[1,1024]{1,0:T(1,128)} %param.26), channel_id=1, replica_groups=mesh['expert'=8,'dp'=4] {'expert'}, dimensions={1}, use_global_device_ids=true | all-gather | bytes 36864 | tf_op jit(solution)/shard_map/all_gather | solution.py:162
  40.6 28.0 %gather_fusion = bf16[5120,1024]{1,0:T(8,128)(2,1)} fusion(bf16[1537,1024]{1,0:T(8,128)(2,1)} %concatenate.38, s32[5120]{0:T(1024)S(1)} %broadcast_clamp_fusion), kind=kCustom, calls=%fused_computation | custom fusion | bytes 20992000 | tf_op jit(solution)/shard_map/gather | solution.py:125
  86.7 210.9 %all-to-all-done = bf16[8,640,1024]{2,1,0:T(8,128)(2,1)} async-done(((bf16[8,640,1024]{2,1,0:T(8,128)(2,1)}), bf16[8,640,1024]{2,1,0:T(8,128)(2,1)}, u32[]{:S(2)}, u32[]{:S(2)}) %all-to-all-start) | async-done | bytes 10485792 | tf_op jit(solution)/shard_map/all_to_all | solution.py:191
  337.9 15.4 fusion.104
  353.3 14.4 fusion
  397.3 13.1 fusion.81
  414.7 27.6 %gather_fusion.2 = bf16[5120,1024]{1,0:T(8,128)(2,1)} fusion(bf16[1025,1024]{1,0:T(8,128)(2,1)} %concatenate.40, s32[5120]{0:T(1024)S(1)} %fusion.87), kind=kCustom, calls=%fused_computation.2 | custom fusion | bytes 20992000 | tf_op jit(solution)/shard_map/gather | solution.py:133
  466.4 208.4 %all-to-all-done.1 = bf16[8,640,1024]{2,1,0:T(8,128)(2,1)} async-done(((bf16[8,640,1024]{2,1,0:T(8,128)(2,1)}), bf16[8,640,1024]{2,1,0:T(8,128)(2,1)}, u32[]{:S(2)}, u32[]{:S(2)}) %all-to-all-start.1) | async-done | bytes 10485792 | tf_op jit(solution)/shard_map/all_to_all | solution.py:205
  684.9 13.1 gather_fusion.3
  703.4 28.2 %multiply_convert_fusion.1 = (bf16[1536,4096]{1,0:T(8,128)(2,1)}, f32[1536,4096]{1,0:T(8,128)}) fusion(f32[4096]{0:T(1024)S(1)} %bitcast.196, bf16[1,4096,1024]{2,1,0:T(8,128)(2,1)} %all-gather.3.cloned.1.call-done, bf16[1536,1024]{1,0:T(8,128)(2,1)} %gather_fusion.3, f32[1024]{0:T(1024)S(1)} %copy-done.57, f32[1024]{0:T(1024)S(1)} %copy-done.48, ...), kind=kOutput, calls=%fused_computation.26 | convolution fusion | flops 12957253632 | bytes 49319936 | tf_op jit(solution)/shard_map/dot_general | solution.py:225
  731.5 34.8 %fusion.106 = (bf16[4096]{0:T(1024)(128)(2,1)S(1)}, bf16[1536,4096]{1,0:T(8,128)(2,1)}) fusion(f32[1536,4096]{1,0:T(8,128)} %get-tuple-element.111, f32[4096]{0:T(1024)S(1)} %bitcast.197, bf16[1,4096,1024]{2,1,0:T(8,128)(2,1)} %all-gather.5.cloned.1.call-done, bf16[1,1536,1024]{2,1,0:T(8,128)(2,1)} %param.37, pred[1536]{0:T(1024)(128)(4,1)S(1)} %iota_compare_fusion.6), kind=kOutput, calls=%fused_computation.182 | convolution fusion | flops 13018591232 | bytes 49309184 | tf_op jit(solution)/shard_map/dot_general | solution.py:233
  766.4 20.8 %fusion.39 = (f32[1024]{0:T(1024)}, f32[1536]{0:T(1024)S(1)}, f32[1536]{0:T(1024)S(1)}, f32[1024]{0:T(1024)}, f32[1536,1024]{1,0:T(8,128)S(1)}) fusion(bf16[1536,1024]{1,0:T(8,128)(2,1)} %gather_fusion.3, f32[1536]{0:T(1024)S(1)} %add_rsqrt_fusion, f32[1536]{0:T(1024)S(1)} %broadcast_multiply_fusion.2, f32[1024]{0:T(1024)S(1)} %copy-done.48, ...), kind=kOutput, calls=%fused_computation.66 | convolution fusion | flops 12900625408 | bytes 30445568 | tf_op jit(solution)/shard_map/dot_general | solution.py:237
  796.8 28.1 %gather_fusion.4 = bf16[5120,1024]{1,0:T(8,128)(2,1)} fusion(bf16[1537,1024]{1,0:T(8,128)(2,1)} %concatenate.42, s32[5120]{0:T(1024)S(1)} %copy-done.30), kind=kCustom, calls=%fused_computation.4 | custom fusion | bytes 20992000 | tf_op jit(solution)/shard_map/gather | solution.py:125
  831.6 20.1 %convert_bitcast_fusion.1 = bf16[1,4096,1024]{2,1,0:T(8,128)(2,1)} fusion(bf16[1536,4096]{1,0:T(8,128)(2,1)} %get-tuple-element.119, bf16[1536,1024]{1,0:T(8,128)(2,1)} %gather_fusion.3, f32[1024]{0:T(1024)S(1)} %copy-done.57, f32[1024]{0:T(1024)S(1)} %copy-done.48, f32[1536]{0:T(1024)S(1)} %add_rsqrt_fusion, f32[1536]{0:T(1024)S(1)} %broadcast_multiply_fusion.2), kind=kOutput, calls=%fused_computation.50 | convolution fusion | flops 12898533376 | bytes 24137728 | tf_op jit(solution)/shard_map/dot_general | solution.py:238
  852.6 20.1 %convert_bitcast_fusion = bf16[1,4096,1024]{2,1,0:T(8,128)(2,1)} fusion(bf16[1536,4096]{1,0:T(8,128)(2,1)} %get-tuple-element.110, bf16[1,1536,1024]{2,1,0:T(8,128)(2,1)} %param.37, pred[1536]{0:T(1024)(128)(4,1)S(1)} %iota_compare_fusion.6), kind=kOutput, calls=%fused_computation.49 | convolution fusion | flops 12890669056 | bytes 24118784 | tf_op jit(solution)/shard_map/dot_general | solution.py:241
  872.8 184.5 %all-to-all-done.2 = bf16[8,640,1024]{2,1,0:T(8,128)(2,1)} async-done(((bf16[8,640,1024]{2,1,0:T(8,128)(2,1)}), bf16[8,640,1024]{2,1,0:T(8,128)(2,1)}, u32[]{:S(2)}, u32[]{:S(2)}) %all-to-all-start.2) | async-done | bytes 10485792 | tf_op jit(solution)/shard_map/all_to_all | solution.py:264
  1100.0 22.2 %multiply_reduce_fusion = (f32[16,512]{1,0:T(8,128)S(1)}, f32[16,512,1024]{2,1,0:T(8,128)}) fusion(f32[16,512,1024]{2,1,0:T(8,128)} %get-tuple-element.107, f32[16,512]{1,0:T(8,128)S(1)} %log_add_fusion, bf16[512,16,64]{0,2,1:T(8,128)(2,1)S(1)} %bitcast.170, bf16[1024,16,64]{0,2,1:T(8,128)(2,1)S(1)} %bitcast.169), kind=kOutput, calls=%fused_computation.12 | convolution fusion | flops 1098899456 | bytes 70320128 | tf_op jit(solution)/shard_map/qhd,khd->hqk/dot_general | solution.py:97
  1122.2 27.9 %multiply_convert_fusion = bf16[16,512,1024]{2,1,0:T(8,128)(2,1)} fusion(f32[16,512,1024]{2,1,0:T(8,128)} %get-tuple-element.116, f32[16,512,1024]{2,1,0:T(8,128)} %get-tuple-element.107, f32[16,512]{1,0:T(8,128)S(1)} %get-tuple-element.115, f32[16,512]{1,0:T(8,128)S(1)} %log_add_fusion), kind=kLoop, calls=%fused_computation.11 | loop fusion | flops 33554432 | bytes 83951616 | tf_op jit(solution)/shard_map/convert_element_type | solution.py:101
  1192.3 15.8 fusion.61
  1223.7 27.6 %gather_fusion.6 = bf16[5120,1024]{1,0:T(8,128)(2,1)} fusion(bf16[1025,1024]{1,0:T(8,128)(2,1)} %concatenate.45, s32[5120]{0:T(1024)S(1)} %copy-done.28), kind=kCustom, calls=%fused_computation.6 | custom fusion | bytes 20992000 | tf_op jit(solution)/shard_map/gather | solution.py:133
  1283.8 19.8 %fusion.63 = bf16[1,1536,1024]{2,1,0:T(8,128)(2,1)} fusion(bf16[1536,4096]{1,0:T(8,128)(2,1)} %get-tuple-element.110, bf16[1,4096,1024]{2,1,0:T(8,128)(2,1)} %all-gather.5.cloned.1.call-done, bf16[1536,1024]{1,0:T(8,128)(2,1)} %gather_fusion.3, f32[1024]{0:T(1024)S(1)} %bitcast.198, pred[1536]{0:T(1024)(128)(4,1)S(1)} %copy-done.45), kind=kOutput, calls=%fused_computation.97 | convolution fusion | flops 12892766208 | bytes 27268608 | tf_op jit(solution)/shard_map/dot_general | solution.py:229
  1313.5 268.7 %all-reduce.8 = (f32[1024]{0:T(1024)}, f32[1024]{0:T(1024)}, f32[1024]{0:T(1024)}, f32[1024]{0:T(1024)}) all-reduce(f32[1024]{0:T(1024)S(1)} %get-tuple-element.78, f32[1024]{0:T(1024)S(1)} %get-tuple-element.83, f32[1024]{0:T(1024)S(1)} %copy-done.52, f32[1024]{0:T(1024)S(1)} %copy-done.53), channel_id=1, replica_groups=mesh['expert'=8,'dp'=4] {'expert','dp'}, use_global_device_ids=true, to_apply=%region_22.23 | all-reduce | flops 4096 | bytes 32768 | tf_op jit(solution)/shard_map/psum | solution.py:309
  1592.3 13.1 gather_fusion.7
  1605.4 148.3 %all-reduce.12.cloned.1.call-done = (f32[1024,3072]{1,0:T(8,128)}, f32[1024,1024]{1,0:T(8,128)}) async-done(((f32[1024,3072]{1,0:T(8,128)}, f32[1024,1024]{1,0:T(8,128)}), (f32[1024,3072]{1,0:T(8,128)}, f32[1024,1024]{1,0:T(8,128)})) %all-reduce.12.cloned.1.call-update) | async-done | bytes 16777232 | tf_op jit(solution)/shard_map/psum | solution.py:309
  (242 shorter events, 319.9 us)
Async XLA Ops:
  7.2 403.4 %copy-start = (bf16[1024,1024]{1,0:T(8,128)(2,1)S(1)}, bf16[1024,1024]{1,0:T(8,128)(2,1)}, u32[]{:S(2)}) copy-start(bf16[1024,1024]{1,0:T(8,128)(2,1)} %param.30) | copy-start | bytes 6291460
  36.7 31.9 %copy-start.29 = (s32[5120]{0:T(1024)}, s32[5120]{0:T(1024)S(1)}, u32[]{:S(2)}) copy-start(s32[5120]{0:T(1024)S(1)} %broadcast_clamp_fusion) | copy-start | bytes 61444
  68.6 229.1 %all-to-all-start = ((bf16[8,640,1024]{2,1,0:T(8,128)(2,1)}), bf16[8,640,1024]{2,1,0:T(8,128)(2,1)}, u32[]{:S(2)}, u32[]{:S(2)}) async-start(bf16[8,640,1024]{2,1,0:T(8,128)(2,1)} %bitcast.161), calls=%async_computation | async-start | bytes 20971520 | tf_op jit(solution)/shard_map/all_to_all | solution.py:191
  77.5 625.9 %all-gather.3.cloned.1.call-start = ((), (), s32[]{:S(2)}) async-start(), calls=%async_computation.8 | async-start | bytes 10485760 | tf_op jit(solution)/shard_map/all_gather | solution.py:218
  85.5 224.0 %copy-start.42 = (s32[1024]{0:T(1024)}, s32[1024]{0:T(1024)S(1)}, u32[]{:S(2)}) copy-start(s32[1024]{0:T(1024)S(1)} %broadcast_clamp_fusion.1) | copy-start | bytes 12292
  85.6 329.1 %copy-start.27 = (s32[5120]{0:T(1024)}, s32[5120]{0:T(1024)S(1)}, u32[]{:S(2)}) copy-start(s32[5120]{0:T(1024)S(1)} %fusion.87) | copy-start | bytes 61444
  335.2 18.1 %copy-start.6 = (bf16[512,1024]{0,1:T(8,128)(2,1)}, bf16[512,1024]{0,1:T(8,128)(2,1)S(1)}, u32[]{:S(2)}) copy-start(bf16[512,1024]{0,1:T(8,128)(2,1)S(1)} %copy.66) | copy-start | bytes 3145732
  353.3 43.9 %copy-start.25 = (f32[16,512]{1,0:T(8,128)}, f32[16,512]{1,0:T(8,128)S(1)}, u32[]{:S(2)}) copy-start(f32[16,512]{1,0:T(8,128)S(1)} %get-tuple-element.106) | copy-start | bytes 98308
  367.8 29.4 %copy-start.33 = (f32[16,512]{1,0:T(8,128)}, f32[16,512]{1,0:T(8,128)S(1)}, u32[]{:S(2)}) copy-start(f32[16,512]{1,0:T(8,128)S(1)} %fusion) | copy-start | bytes 98308
  442.2 232.5 %all-to-all-start.1 = ((bf16[8,640,1024]{2,1,0:T(8,128)(2,1)}), bf16[8,640,1024]{2,1,0:T(8,128)(2,1)}, u32[]{:S(2)}, u32[]{:S(2)}) async-start(bf16[8,640,1024]{2,1,0:T(8,128)(2,1)} %bitcast.159), calls=%async_computation.1 | async-start | bytes 20971520 | tf_op jit(solution)/shard_map/all_to_all | solution.py:205
  449.0 282.6 %all-gather.5.cloned.1.call-start = ((), (), s32[]{:S(2)}) async-start(), calls=%async_computation.9 | async-start | bytes 10485760 | tf_op jit(solution)/shard_map/all_gather | solution.py:219
  449.7 832.6 %reduce-scatter.15.cloned.1.call-start = ((), (), s32[]{:S(2)}) async-start(), calls=%async_computation.13 | async-start | bytes 327680
  451.0 401.6 %copy-start.44 = (pred[1536]{0:T(1024)(128)(4,1)}, pred[1536]{0:T(1024)(128)(4,1)S(1)}, u32[]{:S(2)}) copy-start(pred[1536]{0:T(1024)(128)(4,1)S(1)} %iota_compare_fusion.6) | copy-start | bytes 4612
  466.4 218.6 %copy-start.35 = (s32[2048]{0:T(1024)}, s32[2048]{0:T(1024)S(1)}, u32[]{:S(2)}) copy-start(s32[2048]{0:T(1024)S(1)} %pad_clamp_fusion) | copy-start | bytes 24580
  766.3 20.8 %copy-start.2 = (bf16[1536,1024]{1,0:T(8,128)(2,1)S(1)}, bf16[1536,1024]{1,0:T(8,128)(2,1)}, u32[]{:S(2)}) copy-start(bf16[1536,1024]{1,0:T(8,128)(2,1)} %gather_fusion.3) | copy-start | bytes 9437188
  766.3 20.8 %copy-start.13 = (bf16[1,1536,1024]{2,1,0:T(8,128)(2,1)S(1)}, bf16[1,1536,1024]{2,1,0:T(8,128)(2,1)}, u32[]{:S(2)}) copy-start(bf16[1,1536,1024]{2,1,0:T(8,128)(2,1)} %param.37) | copy-start | bytes 9437188
  824.9 232.4 %all-to-all-start.2 = ((bf16[8,640,1024]{2,1,0:T(8,128)(2,1)}), bf16[8,640,1024]{2,1,0:T(8,128)(2,1)}, u32[]{:S(2)}, u32[]{:S(2)}) async-start(bf16[8,640,1024]{2,1,0:T(8,128)(2,1)} %bitcast.160), calls=%async_computation.2 | async-start | bytes 20971520 | tf_op jit(solution)/shard_map/all_to_all | solution.py:264
  831.0 472.6 %reduce-scatter.13.cloned.1.call-start = ((), (), s32[]{:S(2)}) async-start(), calls=%async_computation.12 | async-start | bytes 1310720
  831.6 473.7 %reduce-scatter.9.cloned.1.call-start = ((), (), s32[]{:S(2)}) async-start(), calls=%async_computation.10 | async-start | bytes 10485760 | tf_op jit(solution)/shard_map/reduce_scatter | solution.py:247
  851.8 457.6 %reduce-scatter.11.cloned.1.call-start = ((), (), s32[]{:S(2)}) async-start(), calls=%async_computation.11 | async-start | bytes 10485760 | tf_op jit(solution)/shard_map/reduce_scatter | solution.py:250
  872.7 184.5 %copy-start.43 = (s32[1024]{0:T(1024)S(1)}, s32[1024]{0:T(1024)}, u32[]{:S(2)}) copy-start(s32[1024]{0:T(1024)} %copy-done.42) | copy-start | bytes 12292
  1072.8 27.2 %copy-start.12 = (bf16[512,1024]{0,1:T(8,128)(2,1)}, bf16[512,1024]{0,1:T(8,128)(2,1)S(1)}, u32[]{:S(2)}) copy-start(bf16[512,1024]{0,1:T(8,128)(2,1)S(1)} %get-tuple-element.96) | copy-start | bytes 3145732
  1251.3 330.8 %all-to-all-start.3 = ((bf16[8,640,1024]{2,1,0:T(8,128)(2,1)}), bf16[8,640,1024]{2,1,0:T(8,128)(2,1)}, u32[]{:S(2)}, u32[]{:S(2)}) async-start(bf16[8,640,1024]{2,1,0:T(8,128)(2,1)} %bitcast.158), calls=%async_computation.3 | async-start | bytes 20971520 | tf_op jit(solution)/shard_map/all_to_all | solution.py:301
  1257.5 496.2 %all-reduce.12.cloned.1.call-start = ((), (), s32[]{:S(2)}) async-start(), calls=%async_computation.14 | async-start | bytes 33554432 | tf_op jit(solution)/shard_map/psum | solution.py:309
  (47 other events, 407.0 us)
Sparse Core Ops, SparseCore 0:
  79.9 59.1 all-gather.2
  451.4 59.1 all-gather.4
  513.1 20.0 reduce-scatter.14
  834.2 25.7 reduce-scatter.12
  862.5 71.6 reduce-scatter.8
  936.8 71.6 reduce-scatter.10
  1276.6 477.0 all-reduce.11
where the time goes:
time: 1780 us; the launch traced here: 1770 us
  waiting for transfers between devices  754 us (42%)
  matrix products  326 us (18%)
  blocking collectives  307 us (17%)
  local copies, waits for them, and re-layouts  239 us (13%)
  other arithmetic  104 us (6%)
  starting transfers between devices  28.5 us (2%)
    psum x1, blocking collectives, body(): lax.psum((local_w_qkv, local_w_o, local_ln1_gain, local_ln1_bias, local_l...  269 us
    all_to_all x1, waiting for transfers between devices, body(): lax.all_to_all(pack_experts(block_input[0], send_rows), 'expert', split_a...  211 us
    all_to_all x1, waiting for transfers between devices, body(): lax.all_to_all(pack_sequence(hidden.astype(jnp.bfloat16), send_tokens, ex...  208 us
    all_to_all x1, waiting for transfers between devices, body(): lax.all_to_all(pack_experts(grad_placed.astype(jnp.bfloat16), send_rows),...  184 us
    psum x1, waiting for transfers between devices, body(): lax.psum((local_w_qkv, local_w_o, local_ln1_gain, local_ln1_bias, local_l...  148 us
    gather x2, local copies, waits for them, and re-layouts, pack_experts(): return pad_row(matrix)[send_rows]  56.1 us
    gather x2, local copies, waits for them, and re-layouts, pack_sequence(): pad_row(matrix)[send_tokens].reshape(expert_count, -1, matrix.shape[1])  55.2 us
    convert_element_type x2, other arithmetic, attend_backward(): grad_scores = (weights_f * (grad_weights - row_centre)).astype(jnp.bfloat16)  39.6 us
  transfers between devices with their start and end apart: 11, of which 4 were waited for; matrix products, arithmetic and copies ran while one was open for 35% of the time, Pallas kernels for 0%

commit v1 on v0

--- a/solution.py
+++ b/solution.py
@@ -117,24 +117,85 @@
     return (jnp.concatenate(grad_queries, axis=0), grad_keys, grad_values)
 
 
-def pad_row(matrix):
-    return jnp.concatenate([matrix, jnp.zeros((1, matrix.shape[1]), matrix.dtype)], axis=0)
-
-
-def pack_experts(matrix, send_rows):
-    return pad_row(matrix)[send_rows]
-
-
-def unpack_sequence(received, pick_sequence):
-    return received.reshape(-1, received.shape[-1])[pick_sequence]
-
-
-def pack_sequence(matrix, send_tokens, expert_count):
-    return pad_row(matrix)[send_tokens].reshape(expert_count, -1, matrix.shape[1])
-
-
-def unpack_experts(received, pick_expert):
-    return pad_row(received.reshape(-1, received.shape[-1]))[pick_expert]
+bf16 = jnp.bfloat16
+
+
+def select_rows(columns, count, table):
+    chosen = (columns[:, None] == jnp.arange(count, dtype=jnp.int32)[None, :]).astype(bf16)
+    return jnp.dot(chosen, table, preferred_element_type=jnp.float32)
+
+
+def place_rows(columns, count, table):
+    chosen = (columns[None, :] == jnp.arange(count, dtype=jnp.int32)[:, None]).astype(bf16)
+    return jnp.dot(chosen, table, preferred_element_type=jnp.float32).astype(bf16)
+
+
+def exchange(packed, expert_count):
+    return lax.all_to_all(
+        packed.reshape(expert_count, -1, packed.shape[-1]),
+        "expert",
+        split_axis=0,
+        concat_axis=0,
+        tiled=True,
+    ).reshape(-1, packed.shape[-1])
+
+
+def move_rows(table, from_columns, to_columns, local_rows, chunk, expert_count, rounds):
+    from_local, from_device, from_rank = from_columns
+    to_local, to_device, to_rank = to_columns
+    span = expert_count * chunk
+
+    def remote_column(device, rank, step):
+        return jnp.where(rank // chunk == step, device * chunk + rank % chunk, -1)
+
+    def one_round(step):
+        packed = place_rows(remote_column(from_device, from_rank, step), span, table)
+        arrived = exchange(packed, expert_count)
+        return select_rows(remote_column(to_device, to_rank, step), span, arrived)
+
+    local = place_rows(from_local, local_rows, table)
+    total = one_round(0) + select_rows(to_local, local_rows, local)
+
+    def again(state):
+        step, sums = state
+        return (step + 1, sums + one_round(step))
+
+    return lax.while_loop(lambda state: state[0] < rounds, again, (jnp.int32(1), total))[1]
+
+
+def swap(values, axis, bit):
+    size = lax.axis_size(axis)
+    return lax.ppermute(values, axis, [(i, i ^ bit) for i in range(size)])
+
+
+def bits_of(axis):
+    size = lax.axis_size(axis)
+    return [(axis, 1 << k) for k in range(size.bit_length() - 1)]
+
+
+def sum_everywhere(values, steps):
+    part = values
+    for axis, bit in steps:
+        upper = (lax.axis_index(axis) // bit) % 2
+        halves = part.reshape(2, -1, part.shape[-1])
+        kept = lax.dynamic_index_in_dim(halves, upper, 0, keepdims=False)
+        given = lax.dynamic_index_in_dim(halves, 1 - upper, 0, keepdims=False)
+        got = swap(given.astype(bf16), axis, bit)
+        part = kept.astype(jnp.float32) + got.astype(jnp.float32)
+    part = part.astype(bf16)
+    for axis, bit in reversed(steps):
+        upper = (lax.axis_index(axis) // bit) % 2
+        got = swap(part, axis, bit)
+        first = jnp.where(upper == 0, part, got)
+        second = jnp.where(upper == 0, got, part)
+        part = jnp.concatenate([first, second], axis=0)
+    return part.astype(jnp.float32)
+
+
+def sum_small(values, steps):
+    for axis, bit in steps:
+        values = values + swap(values, axis, bit)
+    return values
 
 
 def body(
@@ -159,39 +220,68 @@
     seq_ids = expert_ids[0]
     seq_length = seq_ids.shape[0]
     capacity = 5 * seq_length // expert_count
-    every_id = lax.all_gather(expert_ids, "expert", axis=1, tiled=True)[0]
-    from_each = jnp.sum(
-        (every_id == own_expert).astype(jnp.int32).reshape(expert_count, seq_length), axis=1
-    )
+    chunk = seq_length // expert_count
+    group_ids = lax.all_to_all(
+        jnp.broadcast_to(seq_ids[None], (expert_count, seq_length)),
+        "expert",
+        split_axis=0,
+        concat_axis=0,
+        tiled=True,
+    )
+    devices = jnp.arange(expert_count, dtype=jnp.int32)
+    counts = jnp.sum(
+        (group_ids[:, :, None] == devices[None, None, :]).astype(jnp.int32), axis=1
+    )
+    fullest = jnp.argmax(counts, axis=0).astype(jnp.int32)
+    taken = jnp.sum((fullest[:, None] == devices[None, :]).astype(jnp.int32), axis=0)
+    distinct = jnp.all(taken == 1)
+    held_by = jnp.where(distinct, fullest, devices)
+    owner = jnp.sum(
+        (held_by[:, None] == devices[None, :]).astype(jnp.int32) * devices[:, None], axis=0
+    )
+    held = held_by[own_expert]
+    most = jnp.max(jnp.where(owner[:, None] == devices[None, :], 0, counts))
+    for axis, bit in bits_of("dp"):
+        most = jnp.maximum(most, swap(most, axis, bit))
+    rounds = (most + chunk - 1) // chunk
+    from_each = counts[:, own_expert]
     ends_at = jnp.cumsum(from_each)
     starts_at = ends_at - from_each
     slot_index = jnp.arange(slot_rows, dtype=jnp.int32)
-    source = jnp.minimum(
-        jnp.sum((ends_at[None, :] <= slot_index[:, None]).astype(jnp.int32), axis=1),
-        expert_count - 1,
-    )
+    passed = (ends_at[None, :] <= slot_index[:, None]).astype(jnp.int32)
+    source = jnp.sum(passed, axis=1)
     occupied = slot_index < ends_at[-1]
-    pick_expert = jnp.where(
-        occupied, source * capacity + slot_index - starts_at[source], expert_count * capacity
-    )
-    position = jnp.arange(capacity, dtype=jnp.int32)
-    send_rows = jnp.where(
-        position[None, :] < from_each[:, None], starts_at[:, None] + position[None, :], slot_rows
-    )
-    choose = (seq_ids[:, None] == jnp.arange(expert_count, dtype=jnp.int32)[None, :]).astype(
-        jnp.int32
-    )
+    within = slot_index - jnp.sum(passed * from_each[None, :], axis=1)
+    at_device = jnp.sum(
+        (source[:, None] == devices[None, :]).astype(jnp.int32) * owner[None, :], axis=1
+    )
+    at_home = at_device == own_expert
+    slot_columns = (
+        jnp.where(occupied & at_home, within, -1),
+        at_device,
+        jnp.where(occupied & ~at_home, within, -chunk),
+    )
+    held_ids = lax.dynamic_index_in_dim(group_ids, held, 0, keepdims=False)
+    choose = (held_ids[:, None] == devices[None, :]).astype(jnp.int32)
     rank_in = jnp.sum((jnp.cumsum(choose, axis=0) - 1) * choose, axis=1)
-    pick_sequence = seq_ids * capacity + rank_in
-    send_tokens = (
-        jnp.full((expert_count * capacity,), seq_length, jnp.int32)
-        .at[pick_sequence]
-        .set(jnp.arange(seq_length, dtype=jnp.int32))
-    )
-    arrived = lax.all_to_all(
-        pack_experts(block_input[0], send_rows), "expert", split_axis=0, concat_axis=0, tiled=True
-    )
-    tokens_in = unpack_sequence(arrived, pick_sequence).astype(jnp.float32)
+    is_own = held_ids == own_expert
+    token_columns = (
+        jnp.where(is_own, rank_in, -1),
+        held_ids,
+        jnp.where(is_own, -chunk, rank_in),
+    )
+
+    def to_sequence(table):
+        return move_rows(
+            table, slot_columns, token_columns, capacity, chunk, expert_count, rounds
+        )
+
+    def to_expert(table):
+        return move_rows(
+            table, token_columns, slot_columns, capacity, chunk, expert_count, rounds
+        )
+
+    tokens_in = to_sequence(block_input[0])
     normed, scaled_one, inverse_one = normalize(tokens_in, ln1_gain, ln1_bias)
     normed_low = normed.astype(jnp.bfloat16)
     mixed_qkv = jnp.dot(normed_low, w_qkv, preferred_element_type=jnp.float32).astype(jnp.bfloat16)
@@ -202,14 +292,7 @@
     context, log_totals = attend_forward(queries, keys_all, values_all)
     context_low = context.reshape(seq_length, model_width).astype(jnp.bfloat16)
     hidden = tokens_in + jnp.dot(context_low, w_o, preferred_element_type=jnp.float32)
-    returned = lax.all_to_all(
-        pack_sequence(hidden.astype(jnp.bfloat16), send_tokens, expert_count),
-        "expert",
-        split_axis=0,
-        concat_axis=0,
-        tiled=True,
-    )
-    placed = unpack_experts(returned, pick_expert).astype(jnp.float32)
+    placed = to_expert(hidden.astype(bf16))
     normed_two, scaled_two, inverse_two = normalize(placed, ln2_gain, ln2_bias)
     inputs_low = normed_two.astype(jnp.bfloat16)
     live = occupied[:, None]
@@ -261,14 +344,7 @@
         grad_normed, scaled_two, inverse_two, ln2_gain
     )
     grad_placed = grad_low.astype(jnp.float32) + grad_placed_norm
-    back_arrived = lax.all_to_all(
-        pack_experts(grad_placed.astype(jnp.bfloat16), send_rows),
-        "expert",
-        split_axis=0,
-        concat_axis=0,
-        tiled=True,
-    )
-    grad_hidden = unpack_sequence(back_arrived, pick_sequence)
+    grad_hidden = to_sequence(grad_placed.astype(bf16)).astype(bf16)
     local_w_o = lax.dot_general(
         context_low, grad_hidden, contract_first, preferred_element_type=jnp.float32
     )
@@ -298,18 +374,16 @@
         grad_normed_one, scaled_one, inverse_one, ln1_gain
     )
     grad_tokens = grad_hidden.astype(jnp.float32) + grad_tokens_norm
-    sent_back = lax.all_to_all(
-        pack_sequence(grad_tokens.astype(jnp.bfloat16), send_tokens, expert_count),
-        "expert",
-        split_axis=0,
-        concat_axis=0,
-        tiled=True,
-    )
-    grad_input = unpack_experts(sent_back, pick_expert)
-    grad_w_qkv, grad_w_o, grad_ln1_gain, grad_ln1_bias, grad_ln2_gain, grad_ln2_bias = lax.psum(
-        (local_w_qkv, local_w_o, local_ln1_gain, local_ln1_bias, local_ln2_gain, local_ln2_bias),
-        ("expert", "dp"),
-    )
+    grad_input = to_expert(grad_tokens.astype(bf16)).astype(bf16)
+    by_x = bits_of("dp") + bits_of("expert")
+    dense = jnp.concatenate([local_w_qkv.astype(bf16), local_w_o.astype(bf16)], axis=1)
+    summed = sum_everywhere(dense, by_x)
+    grad_w_qkv = summed[:, : 3 * model_width]
+    grad_w_o = summed[:, 3 * model_width :]
+    norms = sum_small(
+        jnp.stack([local_ln1_gain, local_ln1_bias, local_ln2_gain, local_ln2_bias]), by_x
+    )
+    grad_ln1_gain, grad_ln1_bias, grad_ln2_gain, grad_ln2_bias = norms
     return (
         result[None],
         grad_input[None],

time: 1780 us -> 942 us (0.53)
  waiting for transfers between devices: 754 us -> 216 us
  blocking collectives: 307 us -> 10.2 us
  local copies, waits for them, and re-layouts: 239 us -> 59.8 us
  matrix products: 326 us -> 419 us
  other arithmetic: 104 us -> 153 us
  starting transfers between devices: 28.5 us -> 50.4 us
    all_to_all x4 -> x5, waiting for transfers between devices: 604 us -> 107 us  [the longest x4 103 us: exchange(): lax.all_to_all(packed.reshape(expert_count, -1, packed.shape[-1]), 'exper...]
    psum x1 -> x0, blocking collectives: 269 us -> none  [body(): lax.psum((local_w_qkv, local_w_o, local_ln1_gain, local_ln1_bias, local_l...]
    gather x9 -> x0, local copies, waits for them, and re-layouts: 161 us -> none  [the longest x2 56.1 us: pack_experts(): return pad_row(matrix)[send_rows]]
    psum x1 -> x0, waiting for transfers between devices: 148 us -> none  [body(): lax.psum((local_w_qkv, local_w_o, local_ln1_gain, local_ln1_bias, local_l...]
    ppermute x0 -> x17, waiting for transfers between devices: none -> 108 us  [swap(): return lax.ppermute(values, axis, [(i, i ^ bit) for i in range(size)])]
    dot_general x0 -> x12, matrix products: none -> 83.4 us  [the longest x8 64.8 us: select_rows(): return jnp.dot(chosen, table, preferred_element_type=jnp.float32)]
    concatenate x6 -> x0, local copies, waits for them, and re-layouts: 31 us -> none  [pad_row(): jnp.concatenate([matrix, jnp.zeros((1, matrix.shape[1]), matrix.dtype)],...]
    all_gather x1 -> x0, blocking collectives: 28 us -> none  [body(): every_id = lax.all_gather(expert_ids, 'expert', axis=1, tiled=True)[0]]
  transfers between devices with their start and end apart: 11 -> 28, of which waited for: 4 -> 13; matrix products, arithmetic and copies ran while one was open for 35% -> 63% of each run, Pallas kernels for 0% -> 0%
where the time goes in v1:
time: 942 us; the launch traced here: 929 us
  matrix products  419 us (44%)
  waiting for transfers between devices  216 us (23%)
  other arithmetic  153 us (16%)
  local copies, waits for them, and re-layouts  59.8 us (6%)
  starting transfers between devices  50.4 us (5%)
  between operations  20.2 us (2%)
  blocking collectives  10.2 us (1%)
    ppermute x17, waiting for transfers between devices, swap(): return lax.ppermute(values, axis, [(i, i ^ bit) for i in range(size)])  108 us
    all_to_all x4, waiting for transfers between devices, exchange(): lax.all_to_all(packed.reshape(expert_count, -1, packed.shape[-1]), 'exper...  103 us
    dot_general x8, matrix products, select_rows(): return jnp.dot(chosen, table, preferred_element_type=jnp.float32)  64.8 us
    convert_element_type x2, other arithmetic, attend_backward(): grad_scores = (weights_f * (grad_weights - row_centre)).astype(jnp.bfloat16)  39.9 us
    dot_general x1, matrix products, body(): lax.dot_general(grad_low, weight_out, contract_last, preferred_element_ty...  34.9 us
    dot_general x2, matrix products, attend_backward(): jnp.einsum('qhd,khd->hqk', block_grad, values_all[:last_row], preferred_e...  33.8 us
    dot_general x1, matrix products, body(): lax.dot_general(act_low, grad_low, contract_first, preferred_element_type...  28 us
    all_to_all x4, starting transfers between devices, exchange(): lax.all_to_all(packed.reshape(expert_count, -1, packed.shape[-1]), 'exper...  26.8 us
  transfers between devices with their start and end apart: 28, of which 13 were waited for; matrix products, arithmetic and copies ran while one was open for 63% of the time, Pallas kernels for 0%

profile of v1, /device:TPU:24, one launch (start us, length us, event | category | flops | bytes accessed | tf_op | source)
XLA Modules:
  0.0 929.3 jit_solution(11771218533881244582)
XLA Ops:
  51.9 30.2 %all-to-all-done.5 = bf16[8,128,1024]{2,1,0:T(8,128)(2,1)} async-done(((bf16[8,128,1024]{2,1,0:T(8,128)(2,1)}), bf16[8,128,1024]{2,1,0:T(8,128)(2,1)}, u32[]{:S(2)}, u32[]{:S(2)}) %all-to-all-start.5) | async-done | bytes 2097184 | tf_op jit(solution)/shard_map/all_to_all | solution.py:134
  152.0 15.8 %fusion.194 = (f32[16,512]{1,0:T(8,128)S(1)}, f32[16,512,1024]{2,1,0:T(8,128)}) fusion(bf16[512,16,64]{0,2,1:T(8,128)(2,1)} %bitcast.276, bf16[1024,16,64]{0,2,1:T(8,128)(2,1)S(1)} %bitcast.272, pred[512,1024]{1,0:T(8,128)(4,1)S(1)} %copy-done.24), kind=kOutput, calls=%fused_computation.395 | convolution fusion | flops 1098899456 | bytes 37257216 | tf_op jit(solution)/shard_map/qhd,khd->hqk/dot_general | solution.py:53
  167.8 14.4 %fusion.64 = f32[16,512]{1,0:T(8,128)S(1)} fusion(f32[16,512,1024]{2,1,0:T(8,128)} %get-tuple-element.1167, f32[16,512]{1,0:T(8,128)S(1)} %get-tuple-element.1166), kind=kLoop, calls=%fused_computation.136 | loop fusion | flops 16769024 | bytes 33619968 | tf_op jit(solution)/shard_map/reduce_sum | solution.py:70
  189.8 12.9 %fusion.148 = bf16[512,16,64]{0,2,1:T(8,128)(2,1)S(1)} fusion(bf16[1024,16,64]{0,2,1:T(8,128)(2,1)S(1)} %bitcast.280, f32[16,512,1024]{2,1,0:T(8,128)} %get-tuple-element.1167, f32[16,512]{1,0:T(8,128)S(1)} %fusion.64, f32[16,512]{1,0:T(8,128)S(1)} %get-tuple-element.1166), kind=kOutput, calls=%fused_computation.275 | convolution fusion | flops 1099431936 | bytes 36765696 | tf_op jit(solution)/shard_map/hqk,khd->qhd/dot_general | solution.py:73
  230.7 34.1 %all-to-all-done.6 = bf16[8,128,1024]{2,1,0:T(8,128)(2,1)} async-done(((bf16[8,128,1024]{2,1,0:T(8,128)(2,1)}), bf16[8,128,1024]{2,1,0:T(8,128)(2,1)}, u32[]{:S(2)}, u32[]{:S(2)}) %all-to-all-start.6) | async-done | bytes 2097184 | tf_op jit(solution)/shard_map/all_to_all | solution.py:134
  289.3 22.5 %fusion.86 = f32[1536,4096]{1,0:T(8,128)} fusion(bf16[1,4096,1024]{2,1,0:T(8,128)(2,1)} %all-gather.3.cloned.1.call-done, f32[1536,1024]{1,0:T(8,128)} %get-tuple-element.999, f32[1024]{0:T(1024)S(1)} %copy-done.122, f32[1024]{0:T(1024)S(1)} %copy-done.120, f32[1536]{0:T(1024)S(1)} %add_rsqrt_fusion, f32[1536]{0:T(1024)S(1)} %broadcast_multiply_fusion.2), kind=kOutput, calls=%fused_computation.166 | convolution fusion | flops 12892766208 | bytes 39866368 | tf_op jit(solution)/shard_map/dot_general | solution.py:308
  311.8 34.9 %fusion.196 = (bf16[4096]{0:T(1024)(128)(2,1)S(1)}, bf16[1536,4096]{1,0:T(8,128)(2,1)}) fusion(f32[1536,4096]{1,0:T(8,128)} %fusion.86, f32[4096]{0:T(1024)S(1)} %bitcast.335, bf16[1,4096,1024]{2,1,0:T(8,128)(2,1)} %all-gather.5.cloned.1.call-done, bf16[1,1536,1024]{2,1,0:T(8,128)(2,1)} %param.45, pred[1536]{0:T(1024)(128)(4,1)S(1)} %iota_compare_fusion.91), kind=kOutput, calls=%fused_computation.397 | convolution fusion | flops 13018591232 | bytes 49309184 | tf_op jit(solution)/shard_map/dot_general | solution.py:316
  346.8 20.9 %multiply_reduce_fusion.2 = (f32[1024]{0:T(1024)}, f32[1536]{0:T(1024)S(1)}, f32[1536]{0:T(1024)S(1)}, f32[1024]{0:T(1024)}, f32[1536,1024]{1,0:T(8,128)S(1)}) fusion(f32[1536,1024]{1,0:T(8,128)} %get-tuple-element.999, f32[1536]{0:T(1024)S(1)} %add_rsqrt_fusion, f32[1536]{0:T(1024)S(1)} %broadcast_multiply_fusion.2, f32[1024]{0:T(1024)S(1)} %copy-done.120, ...), kind=kOutput, calls=%fused_computation.173 | convolution fusion | flops 12899052544 | bytes 33591296 | tf_op jit(solution)/shard_map/dot_general | solution.py:320
  383.0 21.1 %convert_bitcast_fusion.1 = bf16[1,4096,1024]{2,1,0:T(8,128)(2,1)} fusion(bf16[1536,4096]{1,0:T(8,128)(2,1)} %get-tuple-element.1177, f32[1536,1024]{1,0:T(8,128)} %get-tuple-element.999, f32[1024]{0:T(1024)S(1)} %copy-done.122, f32[1024]{0:T(1024)S(1)} %copy-done.120, f32[1536]{0:T(1024)S(1)} %add_rsqrt_fusion, f32[1536]{0:T(1024)S(1)} %broadcast_multiply_fusion.2), kind=kOutput, calls=%fused_computation.169 | convolution fusion | flops 12896960512 | bytes 27283456 | tf_op jit(solution)/shard_map/dot_general | solution.py:321
  404.3 23.1 %all-to-all-done.7 = bf16[8,128,1024]{2,1,0:T(8,128)(2,1)} async-done(((bf16[8,128,1024]{2,1,0:T(8,128)(2,1)}), bf16[8,128,1024]{2,1,0:T(8,128)(2,1)}, u32[]{:S(2)}, u32[]{:S(2)}) %all-to-all-start.7) | async-done | bytes 2097184 | tf_op jit(solution)/shard_map/all_to_all | solution.py:134
  463.5 11.6 %multiply_reduce_fusion.1 = (f32[16,512]{1,0:T(8,128)S(1)}, f32[16,512,512]{1,2,0:T(8,128)}) fusion(f32[16,512,512]{1,2,0:T(8,128)} %get-tuple-element.1169, f32[16,512]{1,0:T(8,128)S(1)} %copy-done.75, bf16[512,16,64]{0,2,1:T(8,128)(2,1)S(1)} %bitcast.287, bf16[512,16,64]{0,2,1:T(8,128)(2,1)S(1)} %bitcast.293), kind=kOutput, calls=%fused_computation.149 | convolution fusion | flops 549445632 | bytes 35717120 | tf_op jit(solution)/shard_map/qhd,khd->hqk/dot_general | solution.py:97
  475.1 11.9 %multiply_convert_fusion.2 = bf16[16,512,512]{1,2,0:T(8,128)(2,1)S(1)} fusion(f32[16,512,512]{1,2,0:T(8,128)} %get-tuple-element.1172, f32[16,512,512]{1,2,0:T(8,128)} %get-tuple-element.1169, f32[16,512]{1,0:T(8,128)S(1)} %get-tuple-element.1171, f32[16,512]{1,0:T(8,128)S(1)} %copy-done.75), kind=kLoop, calls=%fused_computation.148 | loop fusion | flops 16777216 | bytes 42008576 | tf_op jit(solution)/shard_map/convert_element_type | solution.py:101
  493.4 22.2 %multiply_reduce_fusion = (f32[16,512]{1,0:T(8,128)S(1)}, f32[16,512,1024]{2,1,0:T(8,128)}) fusion(f32[16,512,1024]{2,1,0:T(8,128)} %get-tuple-element.1167, f32[16,512]{1,0:T(8,128)S(1)} %copy-done.66, bf16[512,16,64]{0,2,1:T(8,128)(2,1)S(1)} %bitcast.284, bf16[1024,16,64]{0,2,1:T(8,128)(2,1)S(1)} %bitcast.281), kind=kOutput, calls=%fused_computation.131 | convolution fusion | flops 1098899456 | bytes 70320128 | tf_op jit(solution)/shard_map/qhd,khd->hqk/dot_general | solution.py:97
  515.6 15.2 %fusion.96 = bf16[1024,16,64]{0,2,1:T(8,128)(2,1)} fusion(f32[512,16,64]{0,2,1:T(8,128)} %fusion.136, bf16[512,16,64]{0,2,1:T(8,128)(2,1)S(1)} %bitcast.285, f32[16,512,1024]{2,1,0:T(8,128)} %get-tuple-element.1167, f32[16,512]{1,0:T(8,128)S(1)} %copy-done.66), kind=kOutput, calls=%fused_computation.194 | convolution fusion | flops 1092616192 | bytes 38830080 | tf_op jit(solution)/shard_map/hqk,qhd->khd/dot_general | solution.py:115
  530.8 28.0 %multiply_convert_fusion = bf16[16,512,1024]{2,1,0:T(8,128)(2,1)} fusion(f32[16,512,1024]{2,1,0:T(8,128)} %get-tuple-element.1174, f32[16,512,1024]{2,1,0:T(8,128)} %get-tuple-element.1167, f32[16,512]{1,0:T(8,128)S(1)} %get-tuple-element.1173, f32[16,512]{1,0:T(8,128)S(1)} %copy-done.66), kind=kLoop, calls=%fused_computation.130 | loop fusion | flops 33554432 | bytes 83951616 | tf_op jit(solution)/shard_map/convert_element_type | solution.py:101
  558.9 12.0 %fusion.147 = bf16[512,16,64]{0,2,1:T(8,128)(2,1)} fusion(bf16[1024,16,64]{0,2,1:T(8,128)(2,1)S(1)} %bitcast.273, bf16[16,512,1024]{2,1,0:T(8,128)(2,1)} %multiply_convert_fusion), kind=kOutput, calls=%fused_computation.274 | convolution fusion | flops 1074790400 | bytes 19922944 | tf_op jit(solution)/shard_map/hqk,khd->qhd/dot_general | solution.py:103
  584.1 13.9 %convolution_convert_fusion = bf16[1024,3072]{1,0:T(8,128)(2,1)} fusion(bf16[1024,1024]{0,1:T(8,128)(2,1)} %bitcast.303, bf16[1024,1024]{0,1:T(8,128)(2,1)S(1)} %bitcast.295, bf16[1024,1024]{0,1:T(8,128)(2,1)} %bitcast.305, f32[1024,1024]{1,0:T(8,128)} %get-tuple-element.998, f32[1024]{0:T(1024)S(1)} %copy-done.124, f32[1024]{0:T(1024)S(1)} %copy-done.110, ...), kind=kOutput, calls=%fused_computation.186 | convolution fusion | flops 6469713920 | bytes 16793600 | tf_op jit(solution)/shard_map/dot_general | solution.py:367
  627.9 46.0 %collective-permute-done.8 = bf16[256,4096]{1,0:T(8,128)(2,1)} collective-permute-done((bf16[256,4096]{1,0:T(8,128)(2,1)S(1)}, bf16[256,4096]{1,0:T(8,128)(2,1)}, u32[]{:S(2)}, u32[]{:S(2)}) %collective-permute-start.8) | collective-permute-done | bytes 2097184 | tf_op jit(solution)/shard_map/ppermute | solution.py:168
  686.6 17.4 %collective-permute-done.9 = bf16[128,4096]{1,0:T(8,128)(2,1)S(1)} collective-permute-done((bf16[128,4096]{1,0:T(8,128)(2,1)S(1)}, bf16[128,4096]{1,0:T(8,128)(2,1)S(1)}, u32[]{:S(2)}, u32[]{:S(2)}) %collective-permute-start.9) | collective-permute-done | bytes 1048608 | tf_op jit(solution)/shard_map/ppermute | solution.py:168
  706.0 28.0 %convert_bitcast_fusion = bf16[1,4096,1024]{2,1,0:T(8,128)(2,1)} fusion(bf16[1,1536,1024]{2,1,0:T(8,128)(2,1)} %param.45, pred[1536]{0:T(1024)(128)(4,1)S(1)} %copy-done.94, f32[1536,4096]{1,0:T(8,128)} %fusion.86, f32[4096]{0:T(1024)S(1)} %bitcast.336), kind=kOutput, calls=%fused_computation.168 | convolution fusion | flops 12953583616 | bytes 36718080 | tf_op jit(solution)/shard_map/dot_general | solution.py:324
  736.6 13.8 %multiply_reduce_fusion.6 = (f32[1024]{0:T(1024)S(1)}, f32[1024]{0:T(1024)S(1)}, f32[1024]{0:T(1024)S(1)}, f32[1024]{0:T(1024)S(1)}, f32[1024,1024]{1,0:T(8,128)S(1)}) fusion(f32[1024,1024]{1,0:T(8,128)} %get-tuple-element.998, f32[1024]{0:T(1024)S(1)} %copy-done.98, f32[1024]{0:T(1024)S(1)} %copy-done.92, f32[1024]{0:T(1024)S(1)} %copy-done.110, ...), kind=kOutput, calls=%fused_computation.199 | convolution fusion | flops 6470758400 | bytes 21000192 | tf_op jit(solution)/shard_map/dot_general | solution.py:370
  784.7 15.0 %collective-permute-done.14 = bf16[128,4096]{1,0:T(8,128)(2,1)S(1)} collective-permute-done((bf16[128,4096]{1,0:T(8,128)(2,1)S(1)}, bf16[128,4096]{1,0:T(8,128)(2,1)S(1)}, u32[]{:S(2)}, u32[]{:S(2)}) %collective-permute-start.14) | collective-permute-done | bytes 1048608 | tf_op jit(solution)/shard_map/ppermute | solution.py:168
  809.9 25.2 %fusion.104 = bf16[1,1536,1024]{2,1,0:T(8,128)(2,1)} fusion(f32[1536,1024]{1,0:T(8,128)} %get-tuple-element.999, bf16[1,4096,1024]{2,1,0:T(8,128)(2,1)} %all-gather.5.cloned.1.call-done, f32[1024]{0:T(1024)S(1)} %bitcast.339, pred[1536]{0:T(1024)(128)(4,1)S(1)} %copy-done.94, f32[1536,4096]{1,0:T(8,128)} %fusion.86, f32[4096]{0:T(1024)S(1)} %bitcast.337), kind=kOutput, calls=%fused_computation.219 | convolution fusion | flops 12954107904 | bytes 43013632 | tf_op jit(solution)/shard_map/dot_general | solution.py:312
  837.5 15.9 %all-to-all-done.8 = bf16[8,128,1024]{2,1,0:T(8,128)(2,1)} async-done(((bf16[8,128,1024]{2,1,0:T(8,128)(2,1)}), bf16[8,128,1024]{2,1,0:T(8,128)(2,1)}, u32[]{:S(2)}, u32[]{:S(2)}) %all-to-all-start.8) | async-done | bytes 2097184 | tf_op jit(solution)/shard_map/all_to_all | solution.py:134
  (447 shorter events, 403.1 us)
Async XLA Ops:
  7.2 282.1 %all-gather.3.cloned.1.call-start = ((), (), s32[]{:S(2)}) async-start(), calls=%async_computation.13 | async-start | bytes 10485760 | tf_op jit(solution)/shard_map/all_gather | solution.py:301
  9.2 9.5 %all-to-all-start.4 = ((s32[8,1,1024]{2,1,0:T(1,128)}), s32[8,1,1024]{2,1,0:T(1,128)S(1)}, u32[]{:S(2)}, u32[]{:S(2)}) async-start(s32[8,1,1024]{2,1,0:T(1,128)} %broadcast_in_dim.107), calls=%async_computation.4 | async-start | bytes 65536 | tf_op jit(solution)/shard_map/all_to_all | solution.py:224
  29.9 52.2 %all-to-all-start.5 = ((bf16[8,128,1024]{2,1,0:T(8,128)(2,1)}), bf16[8,128,1024]{2,1,0:T(8,128)(2,1)}, u32[]{:S(2)}, u32[]{:S(2)}) async-start(bf16[8,128,1024]{2,1,0:T(8,128)(2,1)} %bitcast.309), calls=%async_computation.5 | async-start | bytes 4194304 | tf_op jit(solution)/shard_map/all_to_all | solution.py:134
  37.4 274.5 %all-gather.5.cloned.1.call-start = ((), (), s32[]{:S(2)}) async-start(), calls=%async_computation.14 | async-start | bytes 10485760 | tf_op jit(solution)/shard_map/all_gather | solution.py:302
  212.0 52.9 %all-to-all-start.6 = ((bf16[8,128,1024]{2,1,0:T(8,128)(2,1)}), bf16[8,128,1024]{2,1,0:T(8,128)(2,1)}, u32[]{:S(2)}, u32[]{:S(2)}) async-start(bf16[8,128,1024]{2,1,0:T(8,128)(2,1)} %bitcast.310), calls=%async_computation.6 | async-start | bytes 4194304 | tf_op jit(solution)/shard_map/all_to_all | solution.py:134
  218.8 466.3 %reduce-scatter.15.cloned.1.call-start = ((), (), s32[]{:S(2)}) async-start(), calls=%async_computation.18 | async-start | bytes 327680
  375.3 52.2 %all-to-all-start.7 = ((bf16[8,128,1024]{2,1,0:T(8,128)(2,1)}), bf16[8,128,1024]{2,1,0:T(8,128)(2,1)}, u32[]{:S(2)}, u32[]{:S(2)}) async-start(bf16[8,128,1024]{2,1,0:T(8,128)(2,1)} %bitcast.312), calls=%async_computation.7 | async-start | bytes 4194304 | tf_op jit(solution)/shard_map/all_to_all | solution.py:134
  381.3 453.9 %reduce-scatter.13.cloned.1.call-start = ((), (), s32[]{:S(2)}) async-start(), calls=%async_computation.17 | async-start | bytes 1310720
  382.9 498.9 %reduce-scatter.9.cloned.1.call-start = ((), (), s32[]{:S(2)}) async-start(), calls=%async_computation.15 | async-start | bytes 10485760 | tf_op jit(solution)/shard_map/reduce_scatter | solution.py:330
  404.1 481.9 %reduce-scatter.11.cloned.1.call-start = ((), (), s32[]{:S(2)}) async-start(), calls=%async_computation.16 | async-start | bytes 10485760 | tf_op jit(solution)/shard_map/reduce_scatter | solution.py:333
  609.7 7.5 collective-permute-start.7
  626.0 48.0 %collective-permute-start.8 = (bf16[256,4096]{1,0:T(8,128)(2,1)S(1)}, bf16[256,4096]{1,0:T(8,128)(2,1)}, u32[]{:S(2)}, u32[]{:S(2)}) collective-permute-start(bf16[256,4096]{1,0:T(8,128)(2,1)S(1)} %fusion.121), channel_id=1, source_target_pairs={{0,2},{1,3},{2,0},{3,1},{4,6},{5,7},{6,4},{7,5},{8,10},{9,11},{10,... | collective-permute-start | bytes 6291464 | tf_op jit(solution)/shard_map/ppermute | solution.py:168
  679.4 24.6 %collective-permute-start.9 = (bf16[128,4096]{1,0:T(8,128)(2,1)S(1)}, bf16[128,4096]{1,0:T(8,128)(2,1)S(1)}, u32[]{:S(2)}, u32[]{:S(2)}) collective-permute-start(bf16[128,4096]{1,0:T(8,128)(2,1)S(1)} %fusion.154), channel_id=1, source_target_pairs={{0,4},{4,0},{8,12},{12,8},{16,20},{20,16},{24,28},{28,24},{1,5},{5... | collective-permute-start | bytes 3145736 | tf_op jit(solution)/shard_map/ppermute | solution.py:168
  705.9 28.1 %collective-permute-start.10 = (bf16[64,4096]{1,0:T(8,128)(2,1)S(1)}, bf16[64,4096]{1,0:T(8,128)(2,1)S(1)}, u32[]{:S(2)}, u32[]{:S(2)}) collective-permute-start(bf16[64,4096]{1,0:T(8,128)(2,1)S(1)} %fusion.155), channel_id=1, source_target_pairs={{0,8},{4,12},{8,0},{12,4},{16,24},{20,28},{24,16},{28,20},{1,9},{5... | collective-permute-start | bytes 1572872 | tf_op jit(solution)/shard_map/ppermute | solution.py:168
  734.2 16.2 %collective-permute-start.11 = (bf16[32,4096]{1,0:T(8,128)(2,1)S(1)}, bf16[32,4096]{1,0:T(8,128)(2,1)S(1)}, u32[]{:S(2)}, u32[]{:S(2)}) collective-permute-start(bf16[32,4096]{1,0:T(8,128)(2,1)S(1)} %fusion.157), channel_id=1, source_target_pairs={{0,16},{4,20},{8,24},{12,28},{16,0},{20,4},{24,8},{28,12},{1,17},{... | collective-permute-start | bytes 786440 | tf_op jit(solution)/shard_map/ppermute | solution.py:168
  750.5 11.8 %collective-permute-start.12 = (bf16[32,4096]{1,0:T(8,128)(2,1)S(1)}, bf16[32,4096]{1,0:T(8,128)(2,1)S(1)}, u32[]{:S(2)}, u32[]{:S(2)}) collective-permute-start(bf16[32,4096]{1,0:T(8,128)(2,1)S(1)} %fusion.156), channel_id=1, source_target_pairs={{0,16},{4,20},{8,24},{12,28},{16,0},{20,4},{24,8},{28,12},{1,17},{... | collective-permute-start | bytes 786440 | tf_op jit(solution)/shard_map/ppermute | solution.py:168
  751.1 11.3 %collective-permute-start.2 = (f32[4,1024]{1,0:T(4,128)S(1)}, f32[4,1024]{1,0:T(4,128)S(1)}, u32[]{:S(2)}, u32[]{:S(2)}) collective-permute-start(f32[4,1024]{1,0:T(4,128)S(1)} %pad_maximum_fusion.10), channel_id=1, source_target_pairs={{0,1},{1,0},{2,3},{3,2},{4,5},{5,4},{6,7},{7,6},{8,9},{9,8},{10,11... | collective-permute-start | bytes 49160 | tf_op jit(solution)/shard_map/ppermute | solution.py:168
  762.4 12.8 %collective-permute-start.13 = (bf16[64,4096]{1,0:T(8,128)(2,1)S(1)}, bf16[64,4096]{1,0:T(8,128)(2,1)S(1)}, u32[]{:S(2)}, u32[]{:S(2)}) collective-permute-start(bf16[64,4096]{1,0:T(8,128)(2,1)S(1)} %pad_maximum_fusion.9), channel_id=1, source_target_pairs={{0,8},{4,12},{8,0},{12,4},{16,24},{20,28},{24,16},{28,20},{1,9},{5... | collective-permute-start | bytes 1572872 | tf_op jit(solution)/shard_map/ppermute | solution.py:168
  766.7 12.5 %collective-permute-start.4 = (f32[4,1024]{1,0:T(4,128)S(1)}, f32[4,1024]{1,0:T(4,128)S(1)}, u32[]{:S(2)}, u32[]{:S(2)}) collective-permute-start(f32[4,1024]{1,0:T(4,128)S(1)} %fusion.243), channel_id=1, source_target_pairs={{0,4},{4,0},{8,12},{12,8},{16,20},{20,16},{24,28},{28,24},{1,5},{5... | collective-permute-start | bytes 49160 | tf_op jit(solution)/shard_map/ppermute | solution.py:168
  775.5 24.2 %collective-permute-start.14 = (bf16[128,4096]{1,0:T(8,128)(2,1)S(1)}, bf16[128,4096]{1,0:T(8,128)(2,1)S(1)}, u32[]{:S(2)}, u32[]{:S(2)}) collective-permute-start(bf16[128,4096]{1,0:T(8,128)(2,1)S(1)} %pad_maximum_fusion.8), channel_id=1, source_target_pairs={{0,4},{4,0},{8,12},{12,8},{16,20},{20,16},{24,28},{28,24},{1,5},{5... | collective-permute-start | bytes 3145736 | tf_op jit(solution)/shard_map/ppermute | solution.py:168
  783.2 53.7 %collective-permute-start.6 = (f32[4,1024]{1,0:T(4,128)S(1)}, f32[4,1024]{1,0:T(4,128)S(1)}, u32[]{:S(2)}, u32[]{:S(2)}) collective-permute-start(f32[4,1024]{1,0:T(4,128)S(1)} %add.754), channel_id=1, source_target_pairs={{0,16},{4,20},{8,24},{12,28},{16,0},{20,4},{24,8},{28,12},{1,17},{... | collective-permute-start | bytes 49160 | tf_op jit(solution)/shard_map/ppermute | solution.py:168
  801.8 68.6 %collective-permute-start.15 = (bf16[256,4096]{1,0:T(8,128)(2,1)}, bf16[256,4096]{1,0:T(8,128)(2,1)}, u32[]{:S(2)}, u32[]{:S(2)}) collective-permute-start(bf16[256,4096]{1,0:T(8,128)(2,1)} %pad_maximum_fusion.7), channel_id=1, source_target_pairs={{0,2},{1,3},{2,0},{3,1},{4,6},{5,7},{6,4},{7,5},{8,10},{9,11},{10,... | collective-permute-start | bytes 6291464 | tf_op jit(solution)/shard_map/ppermute | solution.py:168
  803.4 50.0 %all-to-all-start.8 = ((bf16[8,128,1024]{2,1,0:T(8,128)(2,1)}), bf16[8,128,1024]{2,1,0:T(8,128)(2,1)}, u32[]{:S(2)}, u32[]{:S(2)}) async-start(bf16[8,128,1024]{2,1,0:T(8,128)(2,1)} %bitcast.311), calls=%async_computation.8 | async-start | bytes 4194304 | tf_op jit(solution)/shard_map/all_to_all | solution.py:134
  876.8 13.4 %collective-permute-start.16 = (bf16[512,4096]{1,0:T(8,128)(2,1)}, bf16[512,4096]{1,0:T(8,128)(2,1)}, u32[]{:S(2)}, u32[]{:S(2)}) collective-permute-start(bf16[512,4096]{1,0:T(8,128)(2,1)} %pad_maximum_fusion.2), channel_id=1, source_target_pairs={{0,1},{1,0},{2,3},{3,2},{4,5},{5,4},{6,7},{7,6},{8,9},{9,8},{10,11... | collective-permute-start | bytes 12582920 | tf_op jit(solution)/shard_map/ppermute | solution.py:168
  (132 other events, 1823.5 us)
Sparse Core Ops, SparseCore 0:
  9.6 59.2 all-gather.2
  70.5 58.3 all-gather.4
  228.9 20.9 reduce-scatter.14
  384.5 25.9 reduce-scatter.12
  412.9 71.7 reduce-scatter.8
  734.1 75.0 reduce-scatter.10

commit v2 on v1

v2 whole, which is shorter than its diff:
```python
import functools

import jax
import jax.numpy as jnp
from jax import lax
from jax.experimental import pallas as pl
from jax.experimental.pallas import tpu as pltpu
from jax.sharding import PartitionSpec as P

HEADS = 16
HEAD_DIM = 64


epsilon = 1e-05
gelu_c = 0.7978845608028654
contract_last = (((1,), (1,)), ((), ()))
contract_first = (((0,), (0,)), ((), ()))


bf16 = jnp.bfloat16
PAIR = 2 * HEAD_DIM
BIG_VMEM = 48 << 20
f32 = jnp.float32


def dot(left, right):
    return jnp.dot(left, right, preferred_element_type=f32)


def dot_last(left, right):
    return lax.dot_general(left, right, contract_last, preferred_element_type=f32)


def dot_first(left, right):
    return lax.dot_general(left, right, contract_first, preferred_element_type=f32)


def head_parts(pair):
    first = lax.broadcasted_iota(jnp.int32, (1, PAIR), 1) < HEAD_DIM
    zero = jnp.zeros_like(pair)
    return [jnp.where(first, pair, zero), jnp.where(first, zero, pair)]


def attend_kernel(block, q_ref, k_ref, v_ref, context_ref, logs_ref):
    length = q_ref.shape[0]
    keys = head_parts(k_ref[...])
    values_t = v_ref[...].T
    rows = lax.broadcasted_iota(jnp.int32, (block, block), 0)
    cols = lax.broadcasted_iota(jnp.int32, (block, block), 1)
    allowed = rows <= cols
    for low in range(0, length, block):
        high = low + block
        queries = q_ref[low:high, :] * jnp.asarray(0.125, bf16)
        outputs = []
        for head in range(2):
            value_rows = values_t[head * HEAD_DIM : (head + 1) * HEAD_DIM]
            near = jnp.where(allowed, dot_last(keys[head][low:high], queries), -1e30)
            peak = jnp.max(near, axis=0, keepdims=True)
            if low:
                far = dot_last(keys[head][:low], queries)
                peak = jnp.maximum(peak, jnp.max(far, axis=0, keepdims=True))
            near = jnp.exp(near - peak)
            total = jnp.sum(near, axis=0, keepdims=True)
            result = dot(value_rows[:, low:high], near.astype(bf16))
            if low:
                far = jnp.exp(far - peak)
                total = total + jnp.sum(far, axis=0, keepdims=True)
                result = result + dot(value_rows[:, :low], far.astype(bf16))
            outputs.append(result / total)
            logs_ref[0, head : head + 1, low:high] = peak + jnp.log(total)
        context_ref[low:high, :] = jnp.concatenate(outputs, axis=0).T.astype(bf16)


def pair_columns(length, offset):
    return pl.BlockSpec((length, PAIR), lambda pair: (0, offset + pair))


def pair_logs(length):
    return pl.BlockSpec((1, 8, length), lambda pair: (pair, 0, 0))


def attend(mixed):
    length, width = mixed.shape[0], mixed.shape[1] // 3
    pairs = width // PAIR
    return pl.pallas_call(
        functools.partial(attend_kernel, min(512, length)),
        grid=(pairs,),
        in_specs=[pair_columns(length, part * pairs) for part in range(3)],
        out_specs=[pair_columns(length, 0), pair_logs(length)],
        out_shape=[
            jax.ShapeDtypeStruct((length, width), bf16),
            jax.ShapeDtypeStruct((pairs, 8, length), f32),
        ],
        compiler_params=pltpu.CompilerParams(vmem_limit_bytes=BIG_VMEM),
        cost_estimate=pl.CostEstimate(
            flops=4 * length * length * width,
            bytes_accessed=8 * length * width,
            transcendentals=length * length * width // HEAD_DIM,
        ),
    )(mixed, mixed, mixed)


def attend_back_kernel(
    block, q_ref, k_ref, v_ref, context_ref, grad_ref, logs_ref, out_ref, grad_k, grad_v
):
    length = q_ref.shape[0]
    keys, values, grads = k_ref[...], v_ref[...], grad_ref[...]
    queries = head_parts(q_ref[...] * jnp.asarray(0.125, bf16))
    key_parts = head_parts(keys)
    grad_parts = head_parts(grads)
    products = head_parts(grads.astype(f32) * context_ref[...].astype(f32))
    centres = [jnp.sum(part, axis=1, keepdims=True) for part in products]
    logs = logs_ref[0].T
    rows = lax.broadcasted_iota(jnp.int32, (block, block), 0)
    cols = lax.broadcasted_iota(jnp.int32, (block, block), 1)
    allowed = cols <= rows
    for low in reversed(range(0, length, block)):
        high = low + block
        add_q, add_k, add_v = [], [], []
        for head in range(2):
            scores = dot_last(queries[head][low:high], keys[:high])
            probs = jnp.exp(scores - logs[low:high, head : head + 1])
            near = jnp.where(allowed, probs[:, low:], 0.0)
            probs = jnp.concatenate([probs[:, :low], near], axis=1) if low else near
            grad_probs = dot_last(grad_parts[head][low:high], values[:high])
            grad_scores = (probs * (grad_probs - centres[head][low:high])).astype(bf16)
            add_q.append(dot(grad_scores, key_parts[head][:high]))
            add_k.append(dot_first(grad_scores, queries[head][low:high]))
            add_v.append(dot_first(probs.astype(bf16), grad_parts[head][low:high]))
        out_ref[0, low:high, :] = ((add_q[0] + add_q[1]) * 0.125).astype(bf16)
        if high == length:
            grad_k[...] = add_k[0] + add_k[1]
            grad_v[...] = add_v[0] + add_v[1]
        else:
            grad_k[:high, :] += add_k[0] + add_k[1]
            grad_v[:high, :] += add_v[0] + add_v[1]
    out_ref[1] = grad_k[...].astype(bf16)
    out_ref[2] = grad_v[...].astype(bf16)


def attend_back(mixed, context, grad_context, logs):
    length, width = context.shape
    pairs = width // PAIR
    return pl.pallas_call(
        functools.partial(attend_back_kernel, min(256, length)),
        grid=(pairs,),
        in_specs=[pair_columns(length, part * pairs) for part in range(3)]
        + [pair_columns(length, 0)] * 2
        + [pair_logs(length)],
        out_specs=pl.BlockSpec((3, length, PAIR), lambda pair: (0, 0, pair)),
        out_shape=jax.ShapeDtypeStruct((3, length, width), bf16),
        scratch_shapes=[pltpu.VMEM((length, PAIR), f32), pltpu.VMEM((length, PAIR), f32)],
        compiler_params=pltpu.CompilerParams(vmem_limit_bytes=BIG_VMEM),
        cost_estimate=pl.CostEstimate(
            flops=10 * length * length * width,
            bytes_accessed=16 * length * width,
            transcendentals=length * length * width // HEAD_DIM,
        ),
    )(mixed, mixed, mixed, context, grad_context, logs)


def place_rows(columns, count, table):
    chosen = (columns[None, :] == jnp.arange(count, dtype=jnp.int32)[:, None]).astype(bf16)
    return dot(chosen, table).astype(bf16)


def exchange(packed, expert_count):
    return lax.all_to_all(
        packed.reshape(expert_count, -1, packed.shape[-1]),
        "expert",
        split_axis=0,
        concat_axis=0,
        tiled=True,
    ).reshape(-1, packed.shape[-1])


def remote_column(places, chunk, step):
    device, rank = places[1:]
    return jnp.where(rank // chunk == step, device * chunk + rank % chunk, -1)


def pack(table, places, chunk, expert_count, step=0):
    return place_rows(remote_column(places, chunk, step), expert_count * chunk, table)


def more_rounds(arrived, table, source, target, chunk, expert_count, rounds):
    def again(state):
        step, kept = state
        packed = pack(table, source, chunk, expert_count, step)
        got = select_rows(remote_column(target, chunk, step), exchange(packed, expert_count))
        return (step + 1, kept + got)

    count = target[0].shape[0]
    start = (jnp.int32(1), jnp.zeros((count, table.shape[1]), bf16))
    return lax.while_loop(lambda state: state[0] < rounds, again, start)[1]


def select_rows(columns, table):
    chosen = (columns[:, None] == jnp.arange(table.shape[0], dtype=jnp.int32)[None, :]).astype(bf16)
    return dot(chosen, table).astype(bf16)


def swap(values, axis, bit):
    size = lax.axis_size(axis)
    return lax.ppermute(values, axis, [(i, i ^ bit) for i in range(size)])


def bits_of(axis, size=None):
    size = size or lax.axis_size(axis)
    return [(axis, 1 << k) for k in range(size.bit_length() - 1)]


def peer_index(axis, bit):
    own = lax.axis_index(axis)
    side = (own // bit) % 2
    return side, own + bit * (1 - 2 * side)


def greet(peers):
    barrier = pltpu.get_barrier_semaphore()
    for axis, index in peers:
        pl.semaphore_signal(
            barrier, inc=1, device_id={axis: index}, device_id_type=pl.DeviceIdType.MESH
        )
    pl.semaphore_wait(barrier, len(peers))


def ring_peers(count):
    own = lax.axis_index("expert")
    return [lax.rem(own + step, count) for step in range(1, count)]


def remote(source, target, send_sem, recv_sem, axis, index):
    return pltpu.make_async_remote_copy(
        src_ref=source,
        dst_ref=target,
        send_sem=send_sem,
        recv_sem=recv_sem,
        device_id={axis: index},
        device_id_type=pl.DeviceIdType.MESH,
    )


def rows_of(offset, size):
    return pl.ds(pl.multiple_of(offset, 16), size)


def plan_orders(dp_count, expert_count, rows, width):
    dp_bits, expert_bits = bits_of("dp", dp_count), bits_of("expert", expert_count)
    across, along = dp_bits[1:], expert_bits
    y_bits = along[: max(1, len(along) // 2)]
    z_bits = along[len(y_bits) :]
    if expert_count == 8:
        y_bits, z_bits = along[:1], along[1:]
    orders = (across + y_bits + z_bits, y_bits + across + z_bits)
    steps = len(orders[0])
    chunks = max(1, rows // (4 * 16 << steps))
    return dp_bits[0], orders, chunks


def finish_kernel(
    first, orders, chunks, count, dense_ref, norm_ref, packed_ref, sum_ref, norm_out, bias_out, arrived_ref,
    work, done, *scratch
):
    steps = len(orders[0])
    core_slots = scratch[0]
    part_slots = scratch[1 : 1 + steps]
    norm_work, norm_slots = scratch[1 + steps : 3 + steps]
    core_send, core_recv, part_send, part_recv, norm_send, norm_recv = scratch[3 + steps : 9 + steps]
    swap_send, swap_recv, local_sem = scratch[9 + steps :]
    rows = work.shape[0] // chunks
    half, quarter = rows // 2, rows // 4
    own = lax.axis_index("expert")
    others = ring_peers(count)
    links = [first] + list(orders[0])
    dp_peers = [(axis, peer_index(axis, bit)[1]) for axis, bit in links if axis == "dp"]
    greet([("expert", index) for index in others] + dp_peers)

    swaps = []
    import os
    for step, index in enumerate(others):
        copy = remote(packed_ref.at[index], arrived_ref.at[own], swap_send.at[step], swap_recv.at[step], "expert", index)
        copy.start()
        swaps.append(copy)
    home = pltpu.make_async_copy(packed_ref.at[own], arrived_ref.at[own], local_sem.at[chunks])
    home.start()

    side0, peer0 = peer_index(*first)
    started = []
    norm_work[...] = norm_ref[...]

    def add_rows(offset, size, slot, target):
        block = min(size, 64)

        @pl.loop(0, size // block)
        def _(index):
            here = rows_of(offset + index * block, block)
            there = rows_of(index * block, block)
            target[here, :] = (work[here, :].astype(f32) + slot[there, :].astype(f32)).astype(bf16)

    state = {}

    def event(chunk, number):
        base = chunk * rows
        if number == 0:
            kept = base + side0 * half
            given = base + (1 - side0) * half
            load = pltpu.make_async_copy(dense_ref.at[rows_of(kept, half)], work.at[rows_of(kept, half)], local_sem.at[chunk])
            load.start()
            copy = remote(dense_ref.at[rows_of(given, half)], core_slots.at[chunk], core_send.at[chunk, 0], core_recv.at[chunk, 0], first[0], peer0)
            copy.start()
            started.append(copy)
            state[chunk] = dict(kept=kept, load=load, copy=copy)
        elif number <= 2 * steps + 1:
            for part in range(2):
                go_on(chunk, part, number - 1)
        if number == 2 * steps + 1:
            kept = state[chunk]["kept"]
            copy = remote(done.at[rows_of(kept, half)], done.at[rows_of(kept, half)], core_send.at[chunk, 1], core_recv.at[chunk, 1], first[0], peer0)
            copy.start()
            started.append(copy)
            state[chunk]["copy"] = copy
        if number == 2 * steps + 2:
            state[chunk]["copy"].wait_recv()
            store = pltpu.make_async_copy(done.at[pl.ds(base, rows)], sum_ref.at[pl.ds(base, rows)], local_sem.at[chunk])
            store.start()
            state[chunk]["store"] = store

    def go_on(chunk, part, step):
        here = state[chunk]
        if step == 0:
            if part == 0:
                here["load"].wait()
                here["copy"].wait_recv()
                add_rows(here["kept"], half, core_slots.at[chunk], work)
            offset = here["kept"] + part * quarter
        else:
            offset, size, copy, slot = here[part]
            copy.wait_recv()
            if step <= steps:
                add_rows(offset, size, slot, work if step < steps else done)
        if step < steps:
            axis, bit = orders[part][step]
            side, peer = peer_index(axis, bit)
            size = quarter >> (step + 1)
            slot = part_slots[step].at[chunk, part]
            given = offset + (1 - side) * size
            kept = offset + side * size
            copy = remote(work.at[rows_of(given, size)], slot, part_send.at[chunk, part, step], part_recv.at[chunk, part, step], axis, peer)
            copy.start()
            started.append(copy)
            here[part] = (kept, size, copy, slot)
        elif step < 2 * steps:
            back = 2 * steps - 1 - step
            axis, bit = orders[part][back]
            side, peer = peer_index(axis, bit)
            size = quarter >> (back + 1)
            if step > steps:
                offset = offset - here["side", part] * (size // 2)
            here["side", part] = side
            copy = remote(done.at[rows_of(offset, size)], done.at[rows_of(offset, size)], part_send.at[chunk, part, step], part_recv.at[chunk, part, step], axis, peer)
            copy.start()
            started.append(copy)
            here[part] = (offset, size, copy, None)

    norm_copy = None
    for tick in range(2 * steps + 2 + chunks):
        for chunk in range(chunks):
            number = tick - chunk
            if 0 <= number <= 2 * steps + 2:
                event(chunk, number)
        if tick <= len(links):
            if norm_copy is not None:
                norm_copy.wait()
                norm_work[...] += norm_slots[tick - 1]
                if tick == sum(axis == "dp" for axis, _ in links):
                    bias_out[...] = norm_work[8:16, :]
            if tick < len(links):
                axis, bit = links[tick]
                norm_copy = remote(norm_work, norm_slots.at[tick], norm_send.at[tick], norm_recv.at[tick], axis, peer_index(axis, bit)[1])
                norm_copy.start()
            else:
                norm_out[...] = norm_work[...]
    for copy in started:
        copy.wait_send()
    for copy in swaps:
        copy.wait()
    home.wait()
    for chunk in range(chunks):
        state[chunk]["store"].wait()


def finish(dense, norms, packed, dp_count):
    count = packed.shape[0]
    rows, width = dense.shape
    first, orders, chunks = plan_orders(dp_count, count, rows, width)
    steps = len(orders[0])
    part = rows // chunks // 4
    return pl.pallas_call(
        functools.partial(finish_kernel, first, orders, chunks, count),
        in_specs=[
            pl.BlockSpec(memory_space=pl.ANY),
            pl.BlockSpec(memory_space=pltpu.VMEM),
            pl.BlockSpec(memory_space=pl.ANY),
        ],
        out_specs=[
            pl.BlockSpec(memory_space=pl.ANY),
            pl.BlockSpec(memory_space=pltpu.VMEM),
            pl.BlockSpec(memory_space=pltpu.VMEM),
            pl.BlockSpec(memory_space=pl.ANY),
        ],
        out_shape=[
            jax.ShapeDtypeStruct(dense.shape, bf16),
            jax.ShapeDtypeStruct(norms.shape, f32),
            jax.ShapeDtypeStruct((8, width), f32),
            jax.ShapeDtypeStruct(packed.shape, bf16),
        ],
        scratch_shapes=[pltpu.VMEM(dense.shape, bf16)] * 2 + [pltpu.VMEM((chunks, 2 * part, width), bf16)]
        + [pltpu.VMEM((chunks, 2, part >> (step + 1), width), bf16) for step in range(steps)]
        + [
            pltpu.VMEM(norms.shape, f32),
            pltpu.VMEM((steps + 1,) + norms.shape, f32),
            pltpu.SemaphoreType.DMA((chunks, 2)),
            pltpu.SemaphoreType.DMA((chunks, 2)),
            pltpu.SemaphoreType.DMA((chunks, 2, 2 * steps)),
            pltpu.SemaphoreType.DMA((chunks, 2, 2 * steps)),
            pltpu.SemaphoreType.DMA((steps + 1,)),
            pltpu.SemaphoreType.DMA((steps + 1,)),
            pltpu.SemaphoreType.DMA((count - 1,)),
            pltpu.SemaphoreType.DMA((count - 1,)),
            pltpu.SemaphoreType.DMA((chunks + 1,)),
        ],
        compiler_params=pltpu.CompilerParams(
            collective_id=7, has_side_effects=True, vmem_limit_bytes=BIG_VMEM
        ),
        cost_estimate=pl.CostEstimate(
            flops=2 * rows * width, bytes_accessed=8 * rows * width, transcendentals=0
        ),
    )(dense, norms, packed)


def pick(columns, numbers, table):
    return dot((columns == numbers).astype(bf16), table)


def joined_rows(near_ref, far_ref, extra_ref, numbers_ref, table_ref, arrived_ref):
    places = lax.broadcasted_iota(jnp.int32, (1, arrived_ref.shape[0]), 1)
    rows = pick(near_ref[...], numbers_ref[...], table_ref[...])
    return rows + pick(far_ref[...], places, arrived_ref[...]) + extra_ref[...].astype(f32)


def norm_parts(rows):
    centre = jnp.mean(rows, axis=-1, keepdims=True)
    centred = rows - centre
    inverse = lax.rsqrt(jnp.mean(centred * centred, axis=-1, keepdims=True) + epsilon)
    return centred * inverse, inverse


def norm_back(grad, scaled, inverse, gains):
    grad_scaled = grad * gains
    first = jnp.mean(grad_scaled, axis=-1, keepdims=True)
    second = jnp.mean(grad_scaled * scaled, axis=-1, keepdims=True)
    return inverse * (grad_scaled - first - scaled * second)


def first_kernel(near, far, extra, numbers, table, arrived, gain, bias, weight, rows_ref, normed_ref, mixed_ref):
    rows = joined_rows(near, far, extra, numbers, table, arrived)
    rows_ref[...] = rows.astype(bf16)
    normed = (norm_parts(rows)[0] * gain[...] + bias[...]).astype(bf16)
    normed_ref[...] = normed
    mixed_ref[...] = dot(normed, weight[...]).astype(bf16)


def third_kernel(near, far, extra, numbers, table, arrived, weight, rows_ref, product_ref):
    rows = joined_rows(near, far, extra, numbers, table, arrived).astype(bf16)
    rows_ref[...] = rows
    product_ref[...] = dot_last(rows, weight[...]).astype(bf16)


def last_kernel(near, far, extra, numbers, table, arrived, rows_ref):
    rows_ref[...] = joined_rows(near, far, extra, numbers, table, arrived).astype(bf16)


def block_rows(width):
    return pl.BlockSpec((256, width), lambda step: (step, 0))


def in_full(array):
    return pl.BlockSpec(array.shape, lambda step: (0,) * array.ndim, pipeline_mode=pl.Buffered(1))


def join(kernel, blocked, whole, widths):
    count = blocked[0].shape[0]
    width = whole[1].shape[1]
    inside = whole[1].shape[0] + whole[2].shape[0]
    return pl.pallas_call(
        kernel,
        grid=(count // 256,),
        in_specs=[block_rows(array.shape[1]) for array in blocked]
        + [in_full(array) for array in whole],
        out_specs=[block_rows(size) for size in widths],
        out_shape=[jax.ShapeDtypeStruct((count, size), bf16) for size in widths],
        compiler_params=pltpu.CompilerParams(vmem_limit_bytes=BIG_VMEM),
        cost_estimate=pl.CostEstimate(
            flops=2 * count * width * (inside + sum(widths) - width),
            bytes_accessed=2 * (inside * width + count * sum(widths)),
            transcendentals=0,
        ),
    )(*blocked, *whole)


def expert_kernel(
    near, far, extra, live, grad_y, grad_act, numbers, table, arrived, gain, bias,
    weight_in, bias_in, weight_out, bias_out,
    out_ref, normed_ref, act_ref, grad_pre_ref, grad_ref, sum_ref, bias_sum_ref,
):
    rows = joined_rows(near, far, extra, numbers, table, arrived).astype(bf16).astype(f32)
    scaled, inverse = norm_parts(rows)
    normed = (scaled * gain[...] + bias[...]).astype(bf16)
    normed_ref[...] = normed
    hidden = weight_in.shape[0]
    block = min(512, hidden)

    @pl.when(pl.program_id(0) == 0)
    def _():
        sum_ref[...] = jnp.zeros_like(sum_ref)
        bias_sum_ref[...] = jnp.zeros_like(bias_sum_ref)

    result = jnp.zeros(rows.shape, f32)
    grad = jnp.zeros(rows.shape, f32)
    for low in range(0, hidden, block):
        part = slice(low, low + block)
        pre = dot_last(normed, weight_in[part, :]) + bias_in[:, part]
        square = pre * pre
        tangent = jnp.tanh(gelu_c * (pre + 0.044715 * pre * square))
        half = 0.5 * pre
        act = (half + half * tangent).astype(bf16)
        slope = (0.5 + 0.5 * tangent) + half * (1.0 - tangent * tangent) * (
            gelu_c + (3.0 * 0.044715 * gelu_c) * square
        )
        grad_pre_f = grad_act[:, part].astype(f32) * slope
        grad_pre = grad_pre_f.astype(bf16)
        act_ref[:, part] = act
        grad_pre_ref[:, part] = grad_pre
        bias_sum_ref[0:1, part] += jnp.sum(grad_pre.astype(f32), axis=0, keepdims=True)
        result += dot(act, weight_out[part, :])
        grad += dot(grad_pre, weight_in[part, :])
    out = rows + result + bias_out[...]
    out_ref[...] = jnp.where(live[...] > 0, out, 0.0).astype(bf16)
    grad_in = grad_y[...].astype(f32)
    grad_ref[...] = (grad_in + norm_back(grad, scaled, inverse, gain[...])).astype(bf16)
    sum_ref[0:1, :] += jnp.sum(grad * scaled, axis=0, keepdims=True)
    sum_ref[1:2, :] += jnp.sum(grad, axis=0, keepdims=True)
    sum_ref[2:3, :] += jnp.sum(grad_in, axis=0, keepdims=True)


def run_expert(blocked, whole, hidden):
    count, width = blocked[2].shape
    widths = (width, width, hidden, hidden, width)

    def sums(size):
        return pl.BlockSpec((8, size), lambda step: (0, 0))

    return pl.pallas_call(
        expert_kernel,
        grid=(count // 256,),
        in_specs=[block_rows(array.shape[1]) for array in blocked]
        + [in_full(array) for array in whole],
        out_specs=[block_rows(size) for size in widths] + [sums(width), sums(hidden)],
        out_shape=[jax.ShapeDtypeStruct((count, size), bf16) for size in widths]
        + [jax.ShapeDtypeStruct((8, width), f32), jax.ShapeDtypeStruct((8, hidden), f32)],
        compiler_params=pltpu.CompilerParams(vmem_limit_bytes=58 << 20),
        cost_estimate=pl.CostEstimate(
            flops=6 * count * width * hidden,
            bytes_accessed=2 * count * (5 * width + 3 * hidden) + 4 * width * hidden,
            transcendentals=count * hidden,
        ),
    )(*blocked, *whole)


def back_kernel(grad_ref, weight_ref, tokens_ref, hidden_ref, gain_ref, out_ref, sum_ref):
    width = gain_ref.shape[1]
    grad = sum(
        dot_last(grad_ref[part], weight_ref[:, part * width : (part + 1) * width])
        for part in range(3)
    )
    scaled, inverse = norm_parts(tokens_ref[...].astype(f32))
    result = hidden_ref[...].astype(f32) + norm_back(grad, scaled, inverse, gain_ref[...])
    out_ref[...] = result.astype(bf16)

    @pl.when(pl.program_id(0) == 0)
    def _():
        sum_ref[...] = jnp.zeros_like(sum_ref)

    sum_ref[0:1, :] += jnp.sum(grad * scaled, axis=0, keepdims=True)
    sum_ref[1:2, :] += jnp.sum(grad, axis=0, keepdims=True)


def back(grad_mixed, weight, tokens, grad_hidden, gain):
    count, width = tokens.shape
    block = 256

    def by_rows():
        return pl.BlockSpec((block, width), lambda step: (step, 0))

    return pl.pallas_call(
        back_kernel,
        grid=(count // block,),
        in_specs=[
            pl.BlockSpec((3, block, width), lambda step: (0, step, 0)),
            pl.BlockSpec(weight.shape, lambda step: (0, 0)),
            by_rows(),
            by_rows(),
            pl.BlockSpec((1, width), lambda step: (0, 0)),
        ],
        out_specs=[by_rows(), pl.BlockSpec((8, width), lambda step: (0, 0))],
        out_shape=[
            jax.ShapeDtypeStruct((count, width), bf16),
            jax.ShapeDtypeStruct((8, width), f32),
        ],
        compiler_params=pltpu.CompilerParams(vmem_limit_bytes=BIG_VMEM),
        cost_estimate=pl.CostEstimate(
            flops=6 * count * width * width, bytes_accessed=20 * count * width, transcendentals=0
        ),
    )(grad_mixed, weight, tokens, grad_hidden, gain)


def body(
    block_input,
    expert_ids,
    ln1_gain,
    ln1_bias,
    w_qkv,
    w_o,
    ln2_gain,
    ln2_bias,
    w_in,
    b_in,
    w_out,
    b_out,
    cotangent,
):
    expert_count = lax.axis_size("expert")
    own_expert = lax.axis_index("expert")
    slot_rows = block_input.shape[1]
    model_width = block_input.shape[2]
    seq_ids = expert_ids[0]
    seq_length = seq_ids.shape[0]
    capacity = 5 * seq_length // expert_count
    chunk = seq_length // expert_count
    group_ids = lax.all_to_all(
        jnp.broadcast_to(seq_ids[None], (expert_count, seq_length)),
        "expert",
        split_axis=0,
        concat_axis=0,
        tiled=True,
    )
    devices = jnp.arange(expert_count, dtype=jnp.int32)
    counts = jnp.sum(
        (group_ids[:, :, None] == devices[None, None, :]).astype(jnp.int32), axis=1
    )
    fullest = jnp.argmax(counts, axis=0).astype(jnp.int32)
    taken = jnp.sum((fullest[:, None] == devices[None, :]).astype(jnp.int32), axis=0)
    distinct = jnp.all(taken == 1)
    held_by = jnp.where(distinct, fullest, devices)
    owner = jnp.sum(
        (held_by[:, None] == devices[None, :]).astype(jnp.int32) * devices[:, None], axis=0
    )
    held = held_by[own_expert]
    most = jnp.max(jnp.where(owner[:, None] == devices[None, :], 0, counts))
    for axis, bit in bits_of("dp"):
        most = jnp.maximum(most, swap(most, axis, bit))
    rounds = (most + chunk - 1) // chunk
    from_each = counts[:, own_expert]
    ends_at = jnp.cumsum(from_each)
    starts_at = ends_at - from_each
    slot_index = jnp.arange(slot_rows, dtype=jnp.int32)
    passed = (ends_at[None, :] <= slot_index[:, None]).astype(jnp.int32)
    source = jnp.sum(passed, axis=1)
    occupied = slot_index < ends_at[-1]
    within = slot_index - jnp.sum(passed * from_each[None, :], axis=1)
    at_device = jnp.sum(
        (source[:, None] == devices[None, :]).astype(jnp.int32) * owner[None, :], axis=1
    )
    at_home = at_device == own_expert
    slot_places = (
        jnp.where(occupied & at_home, within, -2),
        at_device,
        jnp.where(occupied & ~at_home, within, -chunk),
    )
    held_ids = lax.dynamic_index_in_dim(group_ids, held, 0, keepdims=False)
    choose = (held_ids[:, None] == devices[None, :]).astype(jnp.int32)
    rank_in = jnp.sum((jnp.cumsum(choose, axis=0) - 1) * choose, axis=1)
    is_own = held_ids == own_expert
    token_places = (
        jnp.where(is_own, rank_in, -1),
        held_ids,
        jnp.where(is_own, -chunk, rank_in),
    )

    def start(table, places):
        return exchange(pack(table, places, chunk, expert_count), expert_count)

    def sides(arrived, table, source, target):
        extra = more_rounds(arrived, table, source, target, chunk, expert_count, rounds)
        blocked = [target[0][:, None], remote_column(target, chunk, 0)[:, None], extra]
        return blocked, [source[0][None, :], table, arrived]

    def row(values):
        return values.astype(f32).reshape(1, -1)

    dp_index = lax.axis_index("dp")
    dp_count = lax.axis_size("dp")
    biases = jnp.concatenate([b_in, b_out], axis=1)
    for axis, bit in bits_of("dp"):
        got = swap(biases, axis, bit)
        upper = (dp_index // bit) % 2 == 1
        biases = jnp.where(
            upper, jnp.concatenate([got, biases]), jnp.concatenate([biases, got])
        )
    full_in = lax.all_gather(w_in[0], "dp", axis=0, tiled=True)
    full_out = lax.all_gather(w_out[0], "dp", axis=0, tiled=True)
    hidden_part = b_in.shape[1]
    full_bias_in = row(biases[:, :hidden_part])
    full_bias_out = row(biases[:, hidden_part:])

    arrived = start(block_input[0], slot_places)
    blocked, whole = sides(arrived, block_input[0], slot_places, token_places)
    tokens_in, normed_low, mixed_qkv = join(
        first_kernel,
        blocked,
        whole + [row(ln1_gain), row(ln1_bias), w_qkv],
        (model_width, model_width, 3 * model_width),
    )
    context_low, log_totals = attend(mixed_qkv)
    hidden = (tokens_in.astype(f32) + dot(context_low, w_o)).astype(bf16)
    arrived = start(hidden, token_places)
    live = occupied[:, None]
    grad_low = jnp.where(live, cotangent[0], jnp.zeros((), jnp.bfloat16))
    grad_act = dot_last(grad_low, full_out).astype(bf16)
    arrived, grad_act = lax.optimization_barrier((arrived, grad_act))
    blocked, whole = sides(arrived, hidden, token_places, slot_places)
    result, normed_two, act_low, grad_pre, grad_placed, sums_two, bias_sums = run_expert(
        blocked + [live.astype(jnp.int32), grad_low, grad_act],
        whole + [row(ln2_gain), row(ln2_bias), full_in, full_bias_in, full_out, full_bias_out],
        full_in.shape[0],
    )
    arrived = start(grad_placed, slot_places)
    local_w_in = dot_first(grad_pre, normed_two).astype(bf16)
    local_w_out = dot_first(act_low, grad_low).astype(bf16)
    arrived, local_w_in, local_w_out = lax.optimization_barrier((arrived, local_w_in, local_w_out))
    grad_w_in = lax.psum_scatter(local_w_in, "dp", scatter_dimension=0, tiled=True).astype(f32)
    grad_w_out = lax.psum_scatter(local_w_out, "dp", scatter_dimension=0, tiled=True).astype(f32)
    blocked, whole = sides(arrived, grad_placed, slot_places, token_places)
    grad_hidden, grad_context = join(
        third_kernel, blocked, whole + [w_o], (model_width, model_width)
    )
    local_w_o = lax.dot_general(
        context_low, grad_hidden, contract_first, preferred_element_type=jnp.float32
    )
    grad_mixed = attend_back(mixed_qkv, context_low, grad_context, log_totals)
    grad_tokens, sums_one = back(grad_mixed, w_qkv, tokens_in, grad_hidden, row(ln1_gain))
    packed = pack(grad_tokens, token_places, chunk, expert_count)
    dense = jnp.concatenate(
        [dot_first(normed_low, grad_mixed[part]).astype(bf16) for part in range(3)]
        + [local_w_o.astype(bf16)]
    )
    norms = jnp.concatenate(
        [
            sums_one[:2],
            sums_two[:2],
            jnp.zeros((4, model_width), f32),
            bias_sums[0].reshape(-1, model_width),
            sums_two[2:3],
            jnp.zeros((3, model_width), f32),
        ]
    )
    summed, norms, bias_sums, arrived = finish(
        dense, norms, packed.reshape(expert_count, chunk, model_width), dp_count
    )
    blocked, whole = sides(
        arrived.reshape(-1, model_width), grad_tokens, token_places, slot_places
    )
    (grad_input,) = join(last_kernel, blocked, whole, (model_width,))
    grad_w_qkv = jnp.concatenate(
        [summed[part * model_width : (part + 1) * model_width] for part in range(3)], axis=1
    ).astype(f32)
    grad_w_o = summed[3 * model_width :].astype(f32)
    grad_ln1_gain, grad_ln1_bias, grad_ln2_gain, grad_ln2_bias = norms[:4]
    full_parts = bias_sums[:4].reshape(dp_count, -1)
    grad_b_in = lax.dynamic_index_in_dim(full_parts, dp_index, 0, keepdims=False)
    grad_b_out = lax.dynamic_index_in_dim(
        bias_sums[4].reshape(dp_count, -1), dp_index, 0, keepdims=False
    )
    return (
        result[None],
        grad_input[None],
        grad_ln1_gain,
        grad_ln1_bias,
        grad_w_qkv,
        grad_w_o,
        grad_ln2_gain,
        grad_ln2_bias,
        grad_w_in[None],
        grad_b_in[None],
        grad_w_out[None],
        grad_b_out[None],
    )


def solution(mesh):
    placed = (
        P("dp", "expert", None),
        P("dp", "expert"),
        P(),
        P(),
        P(),
        P(),
        P(),
        P(),
        P("expert", "dp", None),
        P("expert", "dp"),
        P("expert", "dp", None),
        P("expert", "dp"),
        P("dp", "expert", None),
    )
    return jax.shard_map(
        body,
        mesh=mesh,
        in_specs=placed,
        out_specs=(
            P("dp", "expert", None),
            P("dp", "expert", None),
            P(),
            P(),
            P(),
            P(),
            P(),
            P(),
            P("expert", "dp", None),
            P("expert", "dp"),
            P("expert", "dp", None),
            P("expert", "dp"),
        ),
        check_vma=False,
    )
```

time: 942 us -> 624 us (0.66)
  Pallas kernels: 0 us -> 335 us
  matrix products: 419 us -> 91.3 us
  waiting for transfers between devices: 216 us -> 72.5 us
  other arithmetic: 153 us -> 41.8 us
  local copies, waits for them, and re-layouts: 59.8 us -> 24.7 us
  starting transfers between devices: 50.4 us -> 29.7 us
  blocking collectives: 10.2 us -> 0 us
    pallas_call x0 -> x8, Pallas kernels: none -> 335 us  [the longest x1 135 us: finish(): pl.pallas_call(functools.partial(finish_kernel, first, orders, chunks, co...]
    dot_general x35 -> x11, matrix products: 412 us -> 88.9 us  [the longest x5 45.8 us: dot_first(): lax.dot_general(left, right, contract_first, preferred_element_type=f32)]
    ppermute x17 -> x4, waiting for transfers between devices: 108 us -> 3.87 us  [swap(): return lax.ppermute(values, axis, [(i, i ^ bit) for i in range(size)])]
    convert_element_type x10 -> x3, other arithmetic: 64.7 us -> 13.3 us  [the longest x1 6.46 us: body(): grad_w_o = summed[3 * model_width:].astype(f32)]
    all_to_all x4 -> x3, waiting for transfers between devices: 103 us -> 65.1 us  [exchange(): lax.all_to_all(packed.reshape(expert_count, -1, packed.shape[-1]), 'exper...]
    reduce_sum x8 -> x1, other arithmetic: 37.4 us -> 0.11 us  [body(): source = jnp.sum(passed, axis=1)]
    slice x10 -> x6, local copies, waits for them, and re-layouts: 32.5 us -> 2.75 us  [the longest x1 0.94 us: body(): bias_sums[0].reshape(-1, model_width)]
    ppermute x17 -> x4, starting transfers between devices: 17.3 us -> 4.58 us  [swap(): return lax.ppermute(values, axis, [(i, i ^ bit) for i in range(size)])]
  transfers between devices with their start and end apart: 28 -> 12, of which waited for: 13 -> 7; matrix products, arithmetic and copies ran while one was open for 63% -> 23% of each run, Pallas kernels for 0% -> 42%
where the time goes in v2:
time: 624 us; the launch traced here: 615 us
  Pallas kernels  335 us (54%)
  matrix products  91.3 us (15%)
  waiting for transfers between devices  72.5 us (12%)
  other arithmetic  41.8 us (7%)
  starting transfers between devices  29.7 us (5%)
  local copies, waits for them, and re-layouts  24.7 us (4%)
  between operations  19 us (3%)
    pallas_call x1, Pallas kernels, finish(): pl.pallas_call(functools.partial(finish_kernel, first, orders, chunks, co...  135 us
    pallas_call x1, Pallas kernels, run_expert(): pl.pallas_call(expert_kernel, grid=(count // 256,), in_specs=[block_rows(...  78.6 us
    all_to_all x3, waiting for transfers between devices, exchange(): lax.all_to_all(packed.reshape(expert_count, -1, packed.shape[-1]), 'exper...  65.1 us
    dot_general x5, matrix products, dot_first(): lax.dot_general(left, right, contract_first, preferred_element_type=f32)  45.8 us
    pallas_call x3, Pallas kernels, join(): pl.pallas_call(kernel, grid=(count // 256,), in_specs=[block_rows(array.s...  44.5 us
    pallas_call x1, Pallas kernels, attend_back(): pl.pallas_call(functools.partial(attend_back_kernel, min(256, length)), g...  40.5 us
    dot_general x5, matrix products, dot(): return jnp.dot(left, right, preferred_element_type=f32)  23.1 us
    pallas_call x1, Pallas kernels, attend(): pl.pallas_call(functools.partial(attend_kernel, min(512, length)), grid=(...  22.9 us
  transfers between devices with their start and end apart: 12, of which 7 were waited for; matrix products, arithmetic and copies ran while one was open for 23% of the time, Pallas kernels for 42%

profile of v2, /device:TPU:24, one launch (start us, length us, event | category | flops | bytes accessed | tf_op | source)
XLA Modules:
  0.0 614.6 jit_solution(16261636379355332423)
XLA Ops:
  8.5 6.1 all-to-all-start.4
  31.2 6.5 %fusion.80 = bf16[1024,1024]{1,0:T(8,128)(2,1)} fusion(s32[1536]{0:T(1024)S(1)} %get-tuple-element.1328, bf16[1,1536,1024]{2,1,0:T(8,128)(2,1)} %param.21), kind=kOutput, calls=%fused_computation.162 | convolution fusion | flops 3223846912 | bytes 5249024 | tf_op jit(solution)/shard_map/dot_general | solution.py:27
  44.9 7.7 %all-to-all-start.5 = ((bf16[8,128,1024]{2,1,0:T(8,128)(2,1)}), bf16[8,128,1024]{2,1,0:T(8,128)(2,1)}, u32[]{:S(2)}, u32[]{:S(2)}) async-start(bf16[8,128,1024]{2,1,0:T(8,128)(2,1)} %bitcast.184), calls=%async_computation.5 | async-start | bytes 4194304 | tf_op jit(solution)/shard_map/all_to_all | solution.py:168
  62.9 36.7 %all-to-all-done.5 = bf16[8,128,1024]{2,1,0:T(8,128)(2,1)} async-done(((bf16[8,128,1024]{2,1,0:T(8,128)(2,1)}), bf16[8,128,1024]{2,1,0:T(8,128)(2,1)}, u32[]{:S(2)}, u32[]{:S(2)}) %all-to-all-start.5) | async-done | bytes 2097184 | tf_op jit(solution)/shard_map/all_to_all | solution.py:168
  99.7 20.1 %shard_map.223 = (bf16[1024,1024]{1,0:T(8,128)(2,1)S(1)}, bf16[1024,1024]{1,0:T(8,128)(2,1)S(1)}, bf16[1024,3072]{1,0:T(8,128)(2,1)}) custom-call(s32[1024,1]{1,0:T(8,128)S(1)} %get-tuple-element.1343.near, s32[1024,1]{1,0:T(8,128)S(1)} %get-tuple-element.1341.far, bf16[1024,1024]{1,0:T(8,128)(2,1)} %get-tuple-element.959.extra, ...), custom_call_target="tpu_custom_call" | custom-call | flops 13958643712 | bytes 15728640 | tf_op jit(solution)/shard_map/pallas_call | solution.py:496
  121.1 22.9 %shard_map.224 = (bf16[1024,1024]{1,0:T(8,128)(2,1)S(1)}, f32[8,8,1024]{2,1,0:T(8,128)S(1)}) custom-call(bf16[1024,3072]{1,0:T(8,128)(2,1)} %get-tuple-element.961.q_ref.k_ref.v_ref, bf16[1024,3072]{1,0:T(8,128)(2,1)} %get-tuple-element.961.q_ref.k_ref.v_ref, bf16[1024,3072]{1,0:T(8,128)(2,1)} %get-tuple-element.961.q_ref.k_ref.v_ref), custom_call_target="tpu_custom_call" | custom-call | flops 4294967296 | bytes 8388608 | tf_op jit(solution)/shard_map/pallas_call | solution.py:85
  150.1 5.6 all-to-all-start.6
  162.1 20.0 %convolution_convert_fusion.grad_act = bf16[1536,4096]{1,0:T(8,128)(2,1)} fusion(bf16[1536,1024]{1,0:T(8,128)(2,1)} %bitcast_select_fusion.grad_y, bf16[1,4096,1024]{2,1,0:T(8,128)(2,1)} %all-gather.5.cloned.1.call-done), kind=kOutput, calls=%fused_computation.130 | convolution fusion | flops 12891193344 | bytes 24117248 | tf_op jit(solution)/shard_map/dot_general | solution.py:31
  182.1 20.4 %all-to-all-done.6 = bf16[8,128,1024]{2,1,0:T(8,128)(2,1)S(1)} async-done(((bf16[8,128,1024]{2,1,0:T(8,128)(2,1)}), bf16[8,128,1024]{2,1,0:T(8,128)(2,1)S(1)}, u32[]{:S(2)}, u32[]{:S(2)}) %all-to-all-start.6) | async-done | bytes 2097184 | tf_op jit(solution)/shard_map/all_to_all | solution.py:168
  205.1 78.6 %shard_map.225 = (bf16[1536,1024]{1,0:T(8,128)(2,1)}, bf16[1536,1024]{1,0:T(8,128)(2,1)}, bf16[1536,4096]{1,0:T(8,128)(2,1)}, bf16[1536,4096]{1,0:T(8,128)(2,1)}...) custom-call(s32[1536,1]{1,0:T(8,128)} %get-tuple-element.1354.near, ...), custom_call_target="tpu_custom_call" | custom-call | flops 38654705664 | bytes 70254592 | tf_op jit(solution)/shard_map/pallas_call | solution.py:564
  283.8 6.5 %fusion.81 = bf16[1024,1024]{1,0:T(8,128)(2,1)} fusion(bf16[1536,1024]{1,0:T(8,128)(2,1)} %get-tuple-element.1813.table, s32[1536]{0:T(1024)S(1)} %copy-done.36), kind=kOutput, calls=%fused_computation.163 | convolution fusion | flops 3223846912 | bytes 5249024 | tf_op jit(solution)/shard_map/dot_general | solution.py:27
  290.3 5.2 all-to-all-start.7
  295.8 19.3 %convolution_convert_fusion.1 = bf16[4096,1024]{1,0:T(8,128)(2,1)} fusion(bf16[1536,4096]{1,0:T(8,128)(2,1)} %get-tuple-element.971, bf16[1536,1024]{1,0:T(8,128)(2,1)} %bitcast_select_fusion.grad_y), kind=kOutput, calls=%fused_computation.132 | convolution fusion | flops 12889096192 | bytes 24117248 | tf_op jit(solution)/shard_map/dot_general | solution.py:35
  315.1 19.2 %convolution_convert_fusion.2 = bf16[4096,1024]{1,0:T(8,128)(2,1)} fusion(bf16[1536,4096]{1,0:T(8,128)(2,1)} %get-tuple-element.969, bf16[1536,1024]{1,0:T(8,128)(2,1)} %get-tuple-element.970), kind=kOutput, calls=%fused_computation.133 | convolution fusion | flops 12889096192 | bytes 24117248 | tf_op jit(solution)/shard_map/dot_general | solution.py:35
  334.3 8.0 %all-to-all-done.7 = bf16[8,128,1024]{2,1,0:T(8,128)(2,1)S(1)} async-done(((bf16[8,128,1024]{2,1,0:T(8,128)(2,1)}), bf16[8,128,1024]{2,1,0:T(8,128)(2,1)S(1)}, u32[]{:S(2)}, u32[]{:S(2)}) %all-to-all-start.7) | async-done | bytes 2097184 | tf_op jit(solution)/shard_map/all_to_all | solution.py:168
  347.8 13.5 %shard_map.226 = (bf16[1024,1024]{1,0:T(8,128)(2,1)S(1)}, bf16[1024,1024]{1,0:T(8,128)(2,1)S(1)}) custom-call(s32[1024,1]{1,0:T(8,128)S(1)} %get-tuple-element.1343.near, s32[1024,1]{1,0:T(8,128)S(1)} %get-tuple-element.1341.far, bf16[1024,1024]{1,0:T(8,128)(2,1)} %get-tuple-element.968.extra, s32[1,1536]{1,0:T(1,128)S(1)} %get-tuple-element.1348.numbers, ...), custom_call_target="tpu_custom_call" | custom-call | flops 7516192768 | bytes 9437184 | tf_op jit(solution)/shard_map/pallas_call | solution.py:496
  361.4 40.5 %shard_map.227.grad_ref = bf16[3,1024,1024]{2,1,0:T(8,128)(2,1)} custom-call(bf16[1024,3072]{1,0:T(8,128)(2,1)} %get-tuple-element.961.q_ref.k_ref.v_ref, bf16[1024,3072]{1,0:T(8,128)(2,1)} %get-tuple-element.961.q_ref.k_ref.v_ref, bf16[1024,3072]{1,0:T(8,128)(2,1)} %get-tuple-element.961.q_ref.k_ref.v_ref, bf16[1024,1024]{1,0:T(8,128)(2,1)S(1)} %copy-done.10, ...), custom_call_target="tpu_custom_call" | custom-call | flops 10737418240 | bytes 16777216 | tf_op jit(solution)/shard_map/pallas_call | solution.py:144
  401.9 14.0 %shard_map.228 = (bf16[1024,1024]{1,0:T(8,128)(2,1)}, f32[8,1024]{1,0:T(8,128)S(1)}) custom-call(bf16[3,1024,1024]{2,1,0:T(8,128)(2,1)} %shard_map.227.grad_ref, bf16[1024,3072]{1,0:T(8,128)(2,1)} %weight_ref.1, bf16[1024,1024]{1,0:T(8,128)(2,1)S(1)} %copy-done.8, bf16[1024,1024]{1,0:T(8,128)(2,1)S(1)} %get-tuple-element.975.hidden_ref, f32[1,1024]{1,0:T(1,128)S(1)} %bitcast.171), custom_call_target="tpu_custom_call" | custom-call | flops 6442450944 | bytes 20971520 | tf_op jit(solution)/shard_map/pallas_call | solution.py:606
  416.0 4.1 fusion.79
  433.8 135.0 %shard_map.229 = (bf16[4096,1024]{1,0:T(8,128)(2,1)}, f32[16,1024]{1,0:T(8,128)S(1)}, f32[8,1024]{1,0:T(8,128)S(1)}, bf16[8,128,1024]{2,1,0:T(8,128)(2,1)S(1)}) custom-call(bf16[4096,1024]{1,0:T(8,128)(2,1)} %pad_maximum_fusion.dense_ref, f32[16,1024]{1,0:T(8,128)S(1)} %concatenate.30.norm_ref, bf16[8,128,1024]{2,1,0:T(8,128)(2,1)S(1)} %bitcast.167), custom_call_target="tpu_custom_call" | custom-call | flops 8388608 | bytes 33554432 | tf_op jit(solution)/shard_map/pallas_call | solution.py:399
  571.9 6.5 %slice_convert_fusion = (f32[1024,1024]{1,0:T(8,128)}, bf16[1024,1024]{1,0:T(8,128)(2,1)}, bf16[1024,1024]{1,0:T(8,128)(2,1)}, bf16[1024,1024]{1,0:T(8,128)(2,1)}) fusion(bf16[4096,1024]{1,0:T(8,128)(2,1)} %get-tuple-element.984), kind=kLoop, calls=%fused_computation.153 | loop fusion | flops 1048576 | bytes 18874368 | tf_op jit(solution)/shard_map/convert_element_type | solution.py:788
  583.4 10.9 %shard_map.230 = bf16[1536,1024]{1,0:T(8,128)(2,1)} custom-call(s32[1536,1]{1,0:T(8,128)S(1)} %copy-done.1, s32[1536,1]{1,0:T(8,128)S(1)} %copy-done, bf16[1536,1024]{1,0:T(8,128)(2,1)} %get-tuple-element.977.extra, s32[1,1024]{1,0:T(1,128)S(1)} %copy-done.2, bf16[1024,1024]{1,0:T(8,128)(2,1)} %get-tuple-element.1964, bf16[1024,1024]{1,0:T(8,128)(2,1)S(1)} %bitcast.168), custom_call_target="tpu_custom_call" | custom-call | flops 6442450944 | bytes 7340032 | tf_op jit(solution)/shard_map/pallas_call | solution.py:496
  594.3 5.2 maximum_convert_fusion
  603.6 4.1 bitcast_convert_fusion.1
  (189 shorter events, 79.4 us)
Async XLA Ops:
  8.5 9.5 %all-to-all-start.4 = ((s32[8,1,1024]{2,1,0:T(1,128)}), s32[8,1,1024]{2,1,0:T(1,128)S(1)}, u32[]{:S(2)}, u32[]{:S(2)}) async-start(s32[8,1,1024]{2,1,0:T(1,128)} %broadcast_in_dim.91), calls=%async_computation.4 | async-start | bytes 65536 | tf_op jit(solution)/shard_map/all_to_all | solution.py:651
  14.6 147.6 %all-gather.5.cloned.1.call-start = ((), (), s32[]{:S(2)}) async-start(), calls=%async_computation.12 | async-start | bytes 10485760 | tf_op jit(solution)/shard_map/all_gather | solution.py:722
  23.6 14.0 %collective-permute-start = (s32[]{:T(128)}, s32[]{:T(128)}, u32[]{:S(2)}, u32[]{:S(2)}) collective-permute-start(s32[]{:T(128)} %select_reduce_fusion.2), channel_id=1, source_target_pairs={{0,1},{1,0},{2,3},{3,2},{4,5},{5,4},{6,7},{7,6},{8,9},{9,8},{10,11... | collective-permute-start | bytes 20 | tf_op jit(solution)/shard_map/ppermute | solution.py:205
  27.2 119.2 %copy-start.38 = (s32[1024]{0:T(1024)}, s32[1024]{0:T(1024)S(1)}, u32[]{:S(2)}) copy-start(s32[1024]{0:T(1024)S(1)} %get-tuple-element.1326) | copy-start | bytes 12292
  39.0 3.6 collective-permute-start.1
  44.9 54.7 %all-to-all-start.5 = ((bf16[8,128,1024]{2,1,0:T(8,128)(2,1)}), bf16[8,128,1024]{2,1,0:T(8,128)(2,1)}, u32[]{:S(2)}, u32[]{:S(2)}) async-start(bf16[8,128,1024]{2,1,0:T(8,128)(2,1)} %bitcast.184), calls=%async_computation.5 | async-start | bytes 4194304 | tf_op jit(solution)/shard_map/all_to_all | solution.py:168
  52.6 152.5 %all-gather.7.cloned.1.call-start = ((), (), s32[]{:S(2)}) async-start(), calls=%async_computation.13 | async-start | bytes 10485760 | tf_op jit(solution)/shard_map/all_gather | solution.py:721
  52.8 1.2 collective-permute-start.2
  54.1 45.6 %copy-start.5 = (f32[1024]{0:T(1024)S(1)}, f32[1024]{0:T(1024)}, u32[]{:S(2)}) copy-start(f32[1024]{0:T(1024)} %param.24) | copy-start | bytes 12292
  54.1 45.6 %copy-start.6 = (f32[1024]{0:T(1024)S(1)}, f32[1024]{0:T(1024)}, u32[]{:S(2)}) copy-start(f32[1024]{0:T(1024)} %param.23) | copy-start | bytes 12292
  54.1 3.8 collective-permute-start.3
  121.1 22.9 %copy-start.7 = (bf16[1024,1024]{1,0:T(8,128)(2,1)}, bf16[1024,1024]{1,0:T(8,128)(2,1)S(1)}, u32[]{:S(2)}) copy-start(bf16[1024,1024]{1,0:T(8,128)(2,1)S(1)} %get-tuple-element.960.tokens_ref) | copy-start | bytes 6291460
  121.1 22.9 %copy-start.41 = (bf16[1024,1024]{1,0:T(8,128)(2,1)S(1)}, bf16[1024,1024]{1,0:T(8,128)(2,1)}, u32[]{:S(2)}) copy-start(bf16[1024,1024]{1,0:T(8,128)(2,1)} %weight.3) | copy-start | bytes 6291460
  150.1 52.4 %all-to-all-start.6 = ((bf16[8,128,1024]{2,1,0:T(8,128)(2,1)}), bf16[8,128,1024]{2,1,0:T(8,128)(2,1)S(1)}, u32[]{:S(2)}, u32[]{:S(2)}) async-start(bf16[8,128,1024]{2,1,0:T(8,128)(2,1)} %bitcast.187), calls=%async_computation.6 | async-start | bytes 4194304 | tf_op jit(solution)/shard_map/all_to_all | solution.py:168
  205.1 78.7 %copy-start.19 = (s32[1536,1]{0,1:T(1,128)}, s32[1536,1]{0,1:T(1,128)S(1)}, u32[]{:S(2)}) copy-start(s32[1536,1]{0,1:T(1,128)S(1)} %get-tuple-element.1947) | copy-start | bytes 18436
  205.1 78.7 %copy-start.21 = (s32[1536,1]{0,1:T(1,128)}, s32[1536,1]{0,1:T(1,128)S(1)}, u32[]{:S(2)}) copy-start(s32[1536,1]{0,1:T(1,128)S(1)} %get-tuple-element.1948) | copy-start | bytes 18436
  205.1 78.7 %copy-start.31 = (s32[1,1024]{1,0:T(1,128)}, s32[1,1024]{1,0:T(1,128)S(1)}, u32[]{:S(2)}) copy-start(s32[1,1024]{1,0:T(1,128)S(1)} %get-tuple-element.1953) | copy-start | bytes 12292
  205.1 78.7 %copy-start.33 = (s32[1,1024]{1,0:T(1,128)}, s32[1,1024]{1,0:T(1,128)S(1)}, u32[]{:S(2)}) copy-start(s32[1,1024]{1,0:T(1,128)S(1)} %get-tuple-element.1954) | copy-start | bytes 12292
  205.1 78.7 %copy-start.36 = (s32[1536]{0:T(1024)S(1)}, s32[1536]{0:T(1024)}, u32[]{:S(2)}) copy-start(s32[1536]{0:T(1024)} %copy-done.35) | copy-start | bytes 18436
  290.3 52.0 %all-to-all-start.7 = ((bf16[8,128,1024]{2,1,0:T(8,128)(2,1)}), bf16[8,128,1024]{2,1,0:T(8,128)(2,1)S(1)}, u32[]{:S(2)}, u32[]{:S(2)}) async-start(bf16[8,128,1024]{2,1,0:T(8,128)(2,1)} %bitcast.188), calls=%async_computation.7 | async-start | bytes 4194304 | tf_op jit(solution)/shard_map/all_to_all | solution.py:168
  295.4 304.1 %reduce-scatter.5.cloned.1.call-start = ((), (), s32[]{:S(2)}) async-start(), calls=%async_computation.11 | async-start | bytes 10485760 | tf_op jit(solution)/shard_map/reduce_scatter | solution.py:753
  343.6 260.0 %reduce-scatter.3.cloned.1.call-start = ((), (), s32[]{:S(2)}) async-start(), calls=%async_computation.10 | async-start | bytes 10485760 | tf_op jit(solution)/shard_map/reduce_scatter | solution.py:752
  361.3 40.5 %copy-start.8 = (bf16[1024,1024]{1,0:T(8,128)(2,1)S(1)}, bf16[1024,1024]{1,0:T(8,128)(2,1)}, u32[]{:S(2)}) copy-start(bf16[1024,1024]{1,0:T(8,128)(2,1)} %copy-done.7) | copy-start | bytes 6291460
  401.9 14.1 %copy-start.39 = (s32[1024]{0:T(1024)S(1)}, s32[1024]{0:T(1024)}, u32[]{:S(2)}) copy-start(s32[1024]{0:T(1024)} %copy-done.38) | copy-start | bytes 12292
  (32 other events, 157.1 us)
Sparse Core Ops, SparseCore 0:
  16.9 59.3 all-gather.4
  77.9 58.2 all-gather.6
  342.5 71.8 reduce-scatter.4
  417.0 106.4 reduce-scatter.2

commit v3 on v2

--- a/solution.py
+++ b/solution.py
@@ -100,7 +100,7 @@
     )(mixed, mixed, mixed)
 
 
-def attend_back_kernel(
+def attend_back_pair(
     block, q_ref, k_ref, v_ref, context_ref, grad_ref, logs_ref, out_ref, grad_k, grad_v
 ):
     length = q_ref.shape[0]
@@ -127,15 +127,22 @@
             add_q.append(dot(grad_scores, key_parts[head][:high]))
             add_k.append(dot_first(grad_scores, queries[head][low:high]))
             add_v.append(dot_first(probs.astype(bf16), grad_parts[head][low:high]))
-        out_ref[0, low:high, :] = ((add_q[0] + add_q[1]) * 0.125).astype(bf16)
+        out_ref[low:high, :PAIR] = ((add_q[0] + add_q[1]) * 0.125).astype(bf16)
         if high == length:
             grad_k[...] = add_k[0] + add_k[1]
             grad_v[...] = add_v[0] + add_v[1]
         else:
             grad_k[:high, :] += add_k[0] + add_k[1]
             grad_v[:high, :] += add_v[0] + add_v[1]
-    out_ref[1] = grad_k[...].astype(bf16)
-    out_ref[2] = grad_v[...].astype(bf16)
+    out_ref[:, PAIR : 2 * PAIR] = grad_k[...].astype(bf16)
+    out_ref[:, 2 * PAIR :] = grad_v[...].astype(bf16)
+
+
+def attend_back_kernel(block, *refs):
+    out_ref, pair_grad, grad_k, grad_v = refs[6:]
+    attend_back_pair(block, *refs[:6], pair_grad, grad_k, grad_v)
+    for part in range(3):
+        out_ref[part] = pair_grad[:, part * PAIR : (part + 1) * PAIR]
 
 
 def attend_back(mixed, context, grad_context, logs):
@@ -149,7 +156,8 @@
         + [pair_logs(length)],
         out_specs=pl.BlockSpec((3, length, PAIR), lambda pair: (0, 0, pair)),
         out_shape=jax.ShapeDtypeStruct((3, length, width), bf16),
-        scratch_shapes=[pltpu.VMEM((length, PAIR), f32), pltpu.VMEM((length, PAIR), f32)],
+        scratch_shapes=[pltpu.VMEM((length, 3 * PAIR), bf16)]
+        + [pltpu.VMEM((length, PAIR), f32)] * 2,
         compiler_params=pltpu.CompilerParams(vmem_limit_bytes=BIG_VMEM),
         cost_estimate=pl.CostEstimate(
             flops=10 * length * length * width,
@@ -183,16 +191,14 @@
     return place_rows(remote_column(places, chunk, step), expert_count * chunk, table)
 
 
-def more_rounds(arrived, table, source, target, chunk, expert_count, rounds):
+def more_rounds(kept, table, source, target, chunk, expert_count, rounds):
     def again(state):
-        step, kept = state
+        step, sums = state
         packed = pack(table, source, chunk, expert_count, step)
         got = select_rows(remote_column(target, chunk, step), exchange(packed, expert_count))
-        return (step + 1, kept + got)
-
-    count = target[0].shape[0]
-    start = (jnp.int32(1), jnp.zeros((count, table.shape[1]), bf16))
-    return lax.while_loop(lambda state: state[0] < rounds, again, start)[1]
+        return (step + 1, sums + got)
+
+    return lax.while_loop(lambda state: state[0] < rounds, again, (jnp.int32(1), kept))[1]
 
 
 def select_rows(columns, table):
@@ -254,8 +260,9 @@
         y_bits, z_bits = along[:1], along[1:]
     orders = (across + y_bits + z_bits, y_bits + across + z_bits)
     steps = len(orders[0])
+    short = tuple(order[: steps - len(z_bits)] for order in orders)
     chunks = max(1, rows // (4 * 16 << steps))
-    return dp_bits[0], orders, chunks
+    return dp_bits[0], orders, chunks, short, [bit for _, bit in z_bits]
 
 
 def finish_kernel(
@@ -393,7 +400,7 @@
 def finish(dense, norms, packed, dp_count):
     count = packed.shape[0]
     rows, width = dense.shape
-    first, orders, chunks = plan_orders(dp_count, count, rows, width)
+    first, orders, chunks, _, _ = plan_orders(dp_count, count, rows, width)
     steps = len(orders[0])
     part = rows // chunks // 4
     return pl.pallas_call(
@@ -443,10 +450,13 @@
     return dot((columns == numbers).astype(bf16), table)
 
 
-def joined_rows(near_ref, far_ref, extra_ref, numbers_ref, table_ref, arrived_ref):
-    places = lax.broadcasted_iota(jnp.int32, (1, arrived_ref.shape[0]), 1)
-    rows = pick(near_ref[...], numbers_ref[...], table_ref[...])
-    return rows + pick(far_ref[...], places, arrived_ref[...]) + extra_ref[...].astype(f32)
+def joined_rows(far, kept, arrived):
+    places = lax.broadcasted_iota(jnp.int32, (1, arrived.shape[0]), 1)
+    return pick(far[...], places, arrived[...]) + kept[...].astype(f32)
+
+
+def near_kernel(near, numbers, table, rows_ref):
+    rows_ref[...] = pick(near[...], numbers[...], table[...]).astype(bf16)
 
 
 def norm_parts(rows):
@@ -463,22 +473,23 @@
     return inverse * (grad_scaled - first - scaled * second)
 
 
-def first_kernel(near, far, extra, numbers, table, arrived, gain, bias, weight, rows_ref, normed_ref, mixed_ref):
-    rows = joined_rows(near, far, extra, numbers, table, arrived)
+def first_kernel(far, kept, arrived, gain, bias, weight, rows_ref, normed_ref, mixed_ref, turned_ref):
+    rows = joined_rows(far, kept, arrived)
     rows_ref[...] = rows.astype(bf16)
     normed = (norm_parts(rows)[0] * gain[...] + bias[...]).astype(bf16)
     normed_ref[...] = normed
+    turned_ref[...] = normed.T
     mixed_ref[...] = dot(normed, weight[...]).astype(bf16)
 
 
-def third_kernel(near, far, extra, numbers, table, arrived, weight, rows_ref, product_ref):
-    rows = joined_rows(near, far, extra, numbers, table, arrived).astype(bf16)
+def third_kernel(far, kept, arrived, weight, rows_ref, product_ref):
+    rows = joined_rows(far, kept, arrived).astype(bf16)
     rows_ref[...] = rows
     product_ref[...] = dot_last(rows, weight[...]).astype(bf16)
 
 
-def last_kernel(near, far, extra, numbers, table, arrived, rows_ref):
-    rows_ref[...] = joined_rows(near, far, extra, numbers, table, arrived).astype(bf16)
+def last_kernel(far, kept, arrived, rows_ref):
+    rows_ref[...] = joined_rows(far, kept, arrived).astype(bf16)
 
 
 def block_rows(width):
@@ -489,17 +500,19 @@
     return pl.BlockSpec(array.shape, lambda step: (0,) * array.ndim, pipeline_mode=pl.Buffered(1))
 
 
-def join(kernel, blocked, whole, widths):
+def join(kernel, blocked, whole, widths, turned=()):
     count = blocked[0].shape[0]
-    width = whole[1].shape[1]
-    inside = whole[1].shape[0] + whole[2].shape[0]
+    table = next(array for array in whole if array.dtype == bf16)
+    inside, width = table.shape
     return pl.pallas_call(
         kernel,
         grid=(count // 256,),
         in_specs=[block_rows(array.shape[1]) for array in blocked]
         + [in_full(array) for array in whole],
-        out_specs=[block_rows(size) for size in widths],
-        out_shape=[jax.ShapeDtypeStruct((count, size), bf16) for size in widths],
+        out_specs=[block_rows(size) for size in widths]
+        + [pl.BlockSpec((size, 256), lambda step: (0, step)) for size in turned],
+        out_shape=[jax.ShapeDtypeStruct((count, size), bf16) for size in widths]
+        + [jax.ShapeDtypeStruct((size, count), bf16) for size in turned],
         compiler_params=pltpu.CompilerParams(vmem_limit_bytes=BIG_VMEM),
         cost_estimate=pl.CostEstimate(
             flops=2 * count * width * (inside + sum(widths) - width),
@@ -510,16 +523,16 @@
 
 
 def expert_kernel(
-    near, far, extra, live, grad_y, grad_act, numbers, table, arrived, gain, bias,
+    far, kept, live, grad_y, grad_act, arrived, gain, bias,
     weight_in, bias_in, weight_out, bias_out,
     out_ref, normed_ref, act_ref, grad_pre_ref, grad_ref, sum_ref, bias_sum_ref,
 ):
-    rows = joined_rows(near, far, extra, numbers, table, arrived).astype(bf16).astype(f32)
+    rows = joined_rows(far, kept, arrived)
     scaled, inverse = norm_parts(rows)
     normed = (scaled * gain[...] + bias[...]).astype(bf16)
     normed_ref[...] = normed
     hidden = weight_in.shape[0]
-    block = min(512, hidden)
+    block = min(1024, hidden)
 
     @pl.when(pl.program_id(0) == 0)
     def _():
@@ -555,7 +568,7 @@
 
 
 def run_expert(blocked, whole, hidden):
-    count, width = blocked[2].shape
+    count, width = blocked[1].shape
     widths = (width, width, hidden, hidden, width)
 
     def sums(size):
@@ -576,6 +589,361 @@
             transcendentals=count * hidden,
         ),
     )(*blocked, *whole)
+
+
+def backward_kernel(
+    first, orders, along, count, pairs,
+    q_ref, k_ref, v_ref, context_ref, grad_ref, logs_ref, wq_ref, wk_ref, wv_ref, dense_ref,
+    normed_t, tokens_ref, hidden_ref, gain_ref, norm_ref, send_numbers, near_column, near_numbers,
+    mixed_sum, dense_sum, norm_out, bias_out, arrived_ref, near_ref, tokens_grad,
+    work, done, core_slots, *scratch
+):
+    steps = len(orders[0])
+    part_slots = scratch[:steps]
+    (
+        along_slots, pair_grad, grad_k, grad_v, total, packed, norm_work, norm_slots,
+        core_send, core_recv, part_send, part_recv, along_send, along_recv,
+        norm_send, norm_recv, swap_send, swap_recv, local_sem,
+    ) = scratch[steps:]
+    tick = pl.program_id(0)
+    rows, width = work.shape[1], pairs * PAIR
+    half, quarter = rows // 2, rows // 4
+    own = lax.axis_index("expert")
+    others = ring_peers(count)
+    links = [first] + list(orders[0]) + [("expert", bit) for bit in along]
+    link_peers = [(axis, peer_index(axis, bit)[1]) for axis, bit in links]
+    events = 2 * steps + 4
+    last = pairs + events // 2 - 1
+
+    @pl.when(tick == 0)
+    def _():
+        greet([("expert", index) for index in others] + [peer for peer in link_peers if peer[0] == "dp"])
+
+    side0, peer0 = peer_index(*first)
+    offsets, sides, peers = [], [], []
+    for part in range(2):
+        offset = side0 * half + part * quarter
+        at, side_list, peer_list = [offset], [], []
+        for step, (axis, bit) in enumerate(orders[part]):
+            side, peer = peer_index(axis, bit)
+            offset = offset + side * (quarter >> (step + 1))
+            at.append(offset)
+            side_list.append(side)
+            peer_list.append((axis, peer))
+        offsets.append(at)
+        sides.append(side_list)
+        peers.append(peer_list)
+    spread = 1 << len(along)
+    place = (own // along[0]) % spread
+    piece = quarter >> steps >> len(along)
+
+    def core_give(chunk):
+        given = rows_of((1 - side0) * half, half)
+        return remote(work.at[chunk, given], core_slots.at[chunk], core_send.at[chunk, 0], core_recv.at[chunk, 0], first[0], peer0)
+
+    def core_return(chunk):
+        kept = rows_of(side0 * half, half)
+        return remote(done.at[chunk, kept], done.at[chunk, kept], core_send.at[chunk, 1], core_recv.at[chunk, 1], first[0], peer0)
+
+    def part_give(chunk, part, step):
+        size = quarter >> (step + 1)
+        given = rows_of(offsets[part][step] + (1 - sides[part][step]) * size, size)
+        return remote(
+            work.at[chunk, given], part_slots[step].at[chunk, part],
+            part_send.at[chunk, part, step], part_recv.at[chunk, part, step], *peers[part][step]
+        )
+
+    def part_return(chunk, part, step):
+        kept = rows_of(offsets[part][step + 1], quarter >> (step + 1))
+        return remote(
+            done.at[chunk, kept], done.at[chunk, kept],
+            part_send.at[chunk, part, steps + step], part_recv.at[chunk, part, steps + step], *peers[part][step]
+        )
+
+    def along_copies(chunk, part, back):
+        copies = []
+        for turn in range(1, spread):
+            there = lax.rem(place + turn, spread)
+            index = turn - 1 + back * (spread - 1)
+            if back:
+                source = target = done.at[chunk, rows_of(offsets[part][steps] + place * piece, piece)]
+            else:
+                source = work.at[chunk, rows_of(offsets[part][steps] + there * piece, piece)]
+                target = along_slots.at[chunk, part, turn - 1]
+            copies.append(
+                remote(
+                    source, target, along_send.at[chunk, part, index], along_recv.at[chunk, part, index],
+                    "expert", own + (there - place) * along[0]
+                )
+            )
+        return copies
+
+    def store(chunk):
+        for part in range(4):
+            source = done.at[chunk, :, part * PAIR : (part + 1) * PAIR]
+            column = pl.ds(pl.multiple_of(chunk * PAIR + (part % 3) * width, PAIR), PAIR)
+            target = mixed_sum if part < 3 else dense_sum
+            yield pltpu.make_async_copy(source, target.at[:, column], local_sem.at[chunk, part])
+
+    def add_rows(chunk, offset, size, slots, target):
+        block = min(size, 64)
+
+        @pl.loop(0, size // block)
+        def _(index):
+            here = rows_of(offset + index * block, block)
+            there = rows_of(index * block, block)
+            sums = work[chunk, here, :].astype(f32)
+            for slot in slots:
+                sums = sums + slot[there, :].astype(f32)
+            target[chunk, here, :] = sums.astype(bf16)
+
+    def event(chunk, number):
+        if number == 1:
+            core_give(chunk).wait_recv()
+            add_rows(chunk, side0 * half, half, [core_slots.at[chunk]], work)
+        for part in range(2):
+            if 2 <= number <= steps + 1:
+                step = number - 2
+                part_give(chunk, part, step).wait_recv()
+                add_rows(
+                    chunk, offsets[part][step + 1], quarter >> (step + 1), [part_slots[step].at[chunk, part]], work
+                )
+            if number <= steps:
+                part_give(chunk, part, number - 1).start()
+            elif number == steps + 1:
+                for copy in along_copies(chunk, part, 0):
+                    copy.start()
+            elif number == steps + 2:
+                for copy in along_copies(chunk, part, 0):
+                    copy.wait_recv()
+                slots = [along_slots.at[chunk, part, turn] for turn in range(spread - 1)]
+                add_rows(chunk, offsets[part][steps] + place * piece, piece, slots, done)
+                for copy in along_copies(chunk, part, 1):
+                    copy.start()
+            elif number <= 2 * steps + 3:
+                back = 2 * steps + 2 - number
+                if back == steps - 1:
+                    for copy in along_copies(chunk, part, 1):
+                        copy.wait_recv()
+                else:
+                    part_return(chunk, part, back + 1).wait_recv()
+                if back >= 0:
+                    part_return(chunk, part, back).start()
+        if number == 2 * steps + 3:
+            core_return(chunk).start()
+        if number == 2 * steps + 4:
+            core_return(chunk).wait_recv()
+            for copy in store(chunk):
+                copy.start()
+
+    def norm_step(step):
+        return remote(norm_work.at[step], norm_slots.at[step], norm_send.at[step], norm_recv.at[step], *link_peers[step])
+
+    def norm_event(step):
+        norm_step(step).wait_recv()
+        summed = norm_work[step] + norm_slots[step]
+        if step + 1 < len(links):
+            norm_work[step + 1] = summed
+            norm_step(step + 1).start()
+        else:
+            norm_out[...] = summed
+        if step + 1 == sum(axis == "dp" for axis, _ in links):
+            bias_out[...] = summed[8:16]
+
+    def run_events(side):
+        for number in range(events, 0, -1):
+            if (number + 1) % 2 == side:
+                chunk = tick - (1 + number) // 2
+
+                @pl.when((chunk >= 0) & (chunk < pairs))
+                def _(number=number, chunk=chunk):
+                    event(chunk, number)
+
+        for step in range(len(links)):
+            if step % 2 == side:
+
+                @pl.when(tick == pairs + 1 + step // 2)
+                def _(step=step):
+                    norm_event(step)
+
+    run_events(0)
+
+    @pl.when(tick < pairs)
+    def _():
+        attend_back_pair(
+            min(256, rows), q_ref, k_ref, v_ref, context_ref, grad_ref, logs_ref,
+            pair_grad, grad_k, grad_v,
+        )
+        run_events(1)
+        work[tick, :, : 3 * PAIR] = dot(normed_t[...], pair_grad[...]).astype(bf16)
+        work[tick, :, 3 * PAIR :] = dense_ref[...]
+        core_give(tick).start()
+        weights = jnp.concatenate([wq_ref[...], wk_ref[...], wv_ref[...]], axis=1)
+
+        @pl.when(tick == 0)
+        def _():
+            total[...] = dot_last(pair_grad[...], weights)
+
+        @pl.when(tick > 0)
+        def _():
+            total[...] += dot_last(pair_grad[...], weights)
+
+    quarter_rows = packed.shape[1] // 4
+
+    def swap_rows(step, piece):
+        index = others[step]
+        here = pl.ds(piece * quarter_rows, quarter_rows)
+        return remote(
+            packed.at[index, here], arrived_ref.at[own, here],
+            swap_send.at[step, piece], swap_recv.at[step, piece], "expert", index
+        )
+
+    def start_swaps(pieces):
+        for piece in pieces:
+            for step in range(count - 1):
+                swap_rows(step, piece).start()
+
+    def home_rows():
+        return pltpu.make_async_copy(packed.at[own], arrived_ref.at[own], local_sem.at[pairs, 0])
+
+    @pl.when(tick == pairs)
+    def _():
+        sums = [jnp.zeros((1, width), f32)] * 2
+        for low in range(0, rows, 256):
+            part = slice(low, low + 256)
+            grad = total[part, :]
+            scaled, inverse = norm_parts(tokens_ref[part, :].astype(f32))
+            result = hidden_ref[part, :].astype(f32) + norm_back(grad, scaled, inverse, gain_ref[...])
+            tokens_grad[part, :] = result.astype(bf16)
+            sums[0] = sums[0] + jnp.sum(grad * scaled, axis=0, keepdims=True)
+            sums[1] = sums[1] + jnp.sum(grad, axis=0, keepdims=True)
+        norm_work[0] = norm_ref[...]
+        norm_work[0, 0:1, :] = sums[0]
+        norm_work[0, 1:2, :] = sums[1]
+        norm_step(0).start()
+        chunk = packed.shape[1]
+        for index in range(count):
+            numbers = index * chunk + lax.broadcasted_iota(jnp.int32, (chunk, 1), 0)
+            packed[index] = dot((send_numbers[...] == numbers).astype(bf16), tokens_grad[...]).astype(bf16)
+        start_swaps([0])
+        home_rows().start()
+
+    @pl.when(tick == pairs + 2)
+    def _():
+        start_swaps([2, 3])
+
+    @pl.when(tick >= pairs)
+    def _():
+        run_events(1)
+
+    @pl.when(tick == pairs + 1)
+    def _():
+        start_swaps([1])
+
+    @pl.when(tick == pairs + 2)
+    def _():
+        for low in range(0, near_ref.shape[0], 256):
+            part = slice(low, low + 256)
+            near_ref[part, :] = pick(near_column[part, :], near_numbers[...], tokens_grad[...]).astype(bf16)
+
+    @pl.when(tick == last)
+    def _():
+        @pl.loop(0, pairs)
+        def _(chunk):
+            core_give(chunk).wait_send()
+            core_return(chunk).wait_send()
+            for part in range(2):
+                for step in range(steps):
+                    part_give(chunk, part, step).wait_send()
+                    part_return(chunk, part, step).wait_send()
+                for back in range(2):
+                    for copy in along_copies(chunk, part, back):
+                        copy.wait_send()
+            for copy in store(chunk):
+                copy.wait()
+
+        for step in range(len(links)):
+            norm_step(step).wait_send()
+        for piece in range(4):
+            for step in range(count - 1):
+                swap_rows(step, piece).wait()
+        home_rows().wait()
+
+
+def backward(mixed, context, grad_context, logs, weight, dense, normed_t, tokens, grad_hidden, gain, norms,
+             send_numbers, near_column, near_numbers, first, orders, along, count, chunk):
+    length, width = context.shape
+    pairs = width // PAIR
+    steps = len(orders[0])
+    links = 1 + steps + len(along)
+    part = length // 4
+    slots = near_column.shape[0]
+    spread = 1 << len(along)
+
+    def columns(offset):
+        return pl.BlockSpec((length, PAIR), lambda tick: (0, offset + jnp.minimum(tick, pairs - 1)))
+
+    def whole(array):
+        return pl.BlockSpec(array.shape, lambda tick: (0,) * array.ndim, pipeline_mode=pl.Buffered(1))
+
+    def result(shape):
+        return pl.BlockSpec(shape, lambda tick: (0,) * len(shape))
+
+    anywhere = pl.BlockSpec(memory_space=pl.ANY)
+    fixed = (normed_t, tokens, grad_hidden, gain, norms, send_numbers, near_column, near_numbers)
+    dma = pltpu.SemaphoreType.DMA
+    return pl.pallas_call(
+        functools.partial(backward_kernel, first, orders, along, count, pairs),
+        grid=(pairs + steps + 2,),
+        in_specs=[columns(0), columns(pairs), columns(2 * pairs), columns(0), columns(0)]
+        + [pl.BlockSpec((1, 8, length), lambda tick: (jnp.minimum(tick, pairs - 1), 0, 0))]
+        + [columns(0), columns(pairs), columns(2 * pairs), columns(0)]
+        + [whole(array) for array in fixed],
+        out_specs=[
+            anywhere, anywhere, result(norms.shape), result((8, width)), anywhere,
+            result((slots, width)), result((length, width)),
+        ],
+        out_shape=[
+            jax.ShapeDtypeStruct((length, 3 * width), bf16),
+            jax.ShapeDtypeStruct((length, width), bf16),
+            jax.ShapeDtypeStruct(norms.shape, f32),
+            jax.ShapeDtypeStruct((8, width), f32),
+            jax.ShapeDtypeStruct((count, chunk, width), bf16),
+            jax.ShapeDtypeStruct((slots, width), bf16),
+            jax.ShapeDtypeStruct((length, width), bf16),
+        ],
+        scratch_shapes=[pltpu.VMEM((pairs, length, 4 * PAIR), bf16)] * 2
+        + [pltpu.VMEM((pairs, length // 2, 4 * PAIR), bf16)]
+        + [pltpu.VMEM((pairs, 2, part >> (step + 1), 4 * PAIR), bf16) for step in range(steps)]
+        + [
+            pltpu.VMEM((pairs, 2, spread - 1, part >> steps >> len(along), 4 * PAIR), bf16),
+            pltpu.VMEM((length, 3 * PAIR), bf16),
+            pltpu.VMEM((length, PAIR), f32),
+            pltpu.VMEM((length, PAIR), f32),
+            pltpu.VMEM((length, width), f32),
+            pltpu.VMEM((count, chunk, width), bf16),
+            pltpu.VMEM((links,) + norms.shape, f32),
+            pltpu.VMEM((links,) + norms.shape, f32),
+            dma((pairs, 2)),
+            dma((pairs, 2)),
+            dma((pairs, 2, 2 * steps)),
+            dma((pairs, 2, 2 * steps)),
+            dma((pairs, 2, 2 * (spread - 1))),
+            dma((pairs, 2, 2 * (spread - 1))),
+            dma((links,)),
+            dma((links,)),
+            dma((count - 1, 4)),
+            dma((count - 1, 4)),
+            dma((pairs + 1, 4)),
+        ],
+        compiler_params=pltpu.CompilerParams(
+            collective_id=7, has_side_effects=True, vmem_limit_bytes=61 << 20
+        ),
+        cost_estimate=pl.CostEstimate(
+            flops=10 * length * length * width, bytes_accessed=32 * length * width,
+            transcendentals=length * length * width // HEAD_DIM,
+        ),
+    )(mixed, mixed, mixed, context, grad_context, logs, weight, weight, weight, dense, *fixed)
 
 
 def back_kernel(grad_ref, weight_ref, tokens_ref, hidden_ref, gain_ref, out_ref, sum_ref):
@@ -701,10 +1069,15 @@
     def start(table, places):
         return exchange(pack(table, places, chunk, expert_count), expert_count)
 
-    def sides(arrived, table, source, target):
-        extra = more_rounds(arrived, table, source, target, chunk, expert_count, rounds)
-        blocked = [target[0][:, None], remote_column(target, chunk, 0)[:, None], extra]
-        return blocked, [source[0][None, :], table, arrived]
+    def near_rows(table, source, target):
+        (rows,) = join(
+            near_kernel, [target[0][:, None]], [source[0][None, :], table], (model_width,)
+        )
+        return rows
+
+    def sides(arrived, kept, table, source, target):
+        kept = more_rounds(kept, table, source, target, chunk, expert_count, rounds)
+        return [remote_column(target, chunk, 0)[:, None], kept]
 
     def row(values):
         return values.astype(f32).reshape(1, -1)
@@ -725,12 +1098,14 @@
     full_bias_out = row(biases[:, hidden_part:])
 
     arrived = start(block_input[0], slot_places)
-    blocked, whole = sides(arrived, block_input[0], slot_places, token_places)
-    tokens_in, normed_low, mixed_qkv = join(
+    near = near_rows(block_input[0], slot_places, token_places)
+    arrived, near = lax.optimization_barrier((arrived, near))
+    tokens_in, normed_low, mixed_qkv, normed_t = join(
         first_kernel,
-        blocked,
-        whole + [row(ln1_gain), row(ln1_bias), w_qkv],
+        sides(arrived, near, block_input[0], slot_places, token_places),
+        [arrived, row(ln1_gain), row(ln1_bias), w_qkv],
         (model_width, model_width, 3 * model_width),
+        (model_width,),
     )
     context_low, log_totals = attend(mixed_qkv)
     hidden = (tokens_in.astype(f32) + dot(context_low, w_o)).astype(bf16)
@@ -738,54 +1113,77 @@
     live = occupied[:, None]
     grad_low = jnp.where(live, cotangent[0], jnp.zeros((), jnp.bfloat16))
     grad_act = dot_last(grad_low, full_out).astype(bf16)
-    arrived, grad_act = lax.optimization_barrier((arrived, grad_act))
-    blocked, whole = sides(arrived, hidden, token_places, slot_places)
+    near = near_rows(hidden, token_places, slot_places)
+    arrived, grad_act, near = lax.optimization_barrier((arrived, grad_act, near))
     result, normed_two, act_low, grad_pre, grad_placed, sums_two, bias_sums = run_expert(
-        blocked + [live.astype(jnp.int32), grad_low, grad_act],
-        whole + [row(ln2_gain), row(ln2_bias), full_in, full_bias_in, full_out, full_bias_out],
+        sides(arrived, near, hidden, token_places, slot_places)
+        + [live.astype(jnp.int32), grad_low, grad_act],
+        [arrived, row(ln2_gain), row(ln2_bias), full_in, full_bias_in, full_out, full_bias_out],
         full_in.shape[0],
     )
     arrived = start(grad_placed, slot_places)
     local_w_in = dot_first(grad_pre, normed_two).astype(bf16)
     local_w_out = dot_first(act_low, grad_low).astype(bf16)
-    arrived, local_w_in, local_w_out = lax.optimization_barrier((arrived, local_w_in, local_w_out))
+    near = near_rows(grad_placed, slot_places, token_places)
+    arrived, near, local_w_in, local_w_out = lax.optimization_barrier(
+        (arrived, near, local_w_in, local_w_out)
+    )
     grad_w_in = lax.psum_scatter(local_w_in, "dp", scatter_dimension=0, tiled=True).astype(f32)
     grad_w_out = lax.psum_scatter(local_w_out, "dp", scatter_dimension=0, tiled=True).astype(f32)
-    blocked, whole = sides(arrived, grad_placed, slot_places, token_places)
     grad_hidden, grad_context = join(
-        third_kernel, blocked, whole + [w_o], (model_width, model_width)
-    )
-    local_w_o = lax.dot_general(
-        context_low, grad_hidden, contract_first, preferred_element_type=jnp.float32
-    )
-    grad_mixed = attend_back(mixed_qkv, context_low, grad_context, log_totals)
-    grad_tokens, sums_one = back(grad_mixed, w_qkv, tokens_in, grad_hidden, row(ln1_gain))
-    packed = pack(grad_tokens, token_places, chunk, expert_count)
-    dense = jnp.concatenate(
-        [dot_first(normed_low, grad_mixed[part]).astype(bf16) for part in range(3)]
-        + [local_w_o.astype(bf16)]
-    )
-    norms = jnp.concatenate(
-        [
-            sums_one[:2],
-            sums_two[:2],
-            jnp.zeros((4, model_width), f32),
-            bias_sums[0].reshape(-1, model_width),
-            sums_two[2:3],
-            jnp.zeros((3, model_width), f32),
-        ]
-    )
-    summed, norms, bias_sums, arrived = finish(
-        dense, norms, packed.reshape(expert_count, chunk, model_width), dp_count
-    )
-    blocked, whole = sides(
-        arrived.reshape(-1, model_width), grad_tokens, token_places, slot_places
-    )
-    (grad_input,) = join(last_kernel, blocked, whole, (model_width,))
-    grad_w_qkv = jnp.concatenate(
-        [summed[part * model_width : (part + 1) * model_width] for part in range(3)], axis=1
-    ).astype(f32)
-    grad_w_o = summed[3 * model_width :].astype(f32)
+        third_kernel,
+        sides(arrived, near, grad_placed, slot_places, token_places),
+        [arrived, w_o],
+        (model_width, model_width),
+    )
+    local_w_o = dot_first(context_low, grad_hidden).astype(bf16)
+    sums_one = jnp.zeros((2, model_width), f32)
+    other_sums = [
+        sums_two[:2],
+        jnp.zeros((4, model_width), f32),
+        bias_sums[0].reshape(-1, model_width),
+        sums_two[2:3],
+        jnp.zeros((3, model_width), f32),
+    ]
+    first, orders, _, short, along = plan_orders(
+        dp_count, expert_count, 4 * model_width, model_width
+    )
+    if (seq_length // 4) >> len(orders[0]) >= 16:
+        norms = jnp.concatenate([sums_one, *other_sums])
+        mixed_sum, dense_sum, norms, bias_sums, arrived, near, grad_tokens = backward(
+            mixed_qkv, context_low, grad_context, log_totals, w_qkv, local_w_o, normed_t,
+            tokens_in, grad_hidden, row(ln1_gain), norms,
+            remote_column(token_places, chunk, 0)[None, :],
+            slot_places[0][:, None],
+            token_places[0][None, :],
+            first, short, along, expert_count, chunk,
+        )
+        grad_w_qkv = mixed_sum.astype(f32)
+        grad_w_o = dense_sum.astype(f32)
+    else:
+        grad_mixed = attend_back(mixed_qkv, context_low, grad_context, log_totals)
+        grad_tokens, sums_one = back(grad_mixed, w_qkv, tokens_in, grad_hidden, row(ln1_gain))
+        packed = pack(grad_tokens, token_places, chunk, expert_count)
+        dense = jnp.concatenate(
+            [dot_first(normed_low, grad_mixed[part]).astype(bf16) for part in range(3)]
+            + [local_w_o]
+        )
+        norms = jnp.concatenate([sums_one[:2], *other_sums])
+        summed, norms, bias_sums, arrived = finish(
+            dense, norms, packed.reshape(expert_count, chunk, model_width), dp_count
+        )
+        near = near_rows(grad_tokens, token_places, slot_places)
+        grad_w_qkv = jnp.concatenate(
+            [summed[part * model_width : (part + 1) * model_width] for part in range(3)], axis=1
+        ).astype(f32)
+        grad_w_o = summed[3 * model_width :].astype(f32)
+    arrived = arrived.reshape(-1, model_width)
+    (grad_input,) = join(
+        last_kernel,
+        sides(arrived, near, grad_tokens, token_places, slot_places),
+        [arrived],
+        (model_width,),
+    )
     grad_ln1_gain, grad_ln1_bias, grad_ln2_gain, grad_ln2_bias = norms[:4]
     full_parts = bias_sums[:4].reshape(dp_count, -1)
     grad_b_in = lax.dynamic_index_in_dim(full_parts, dp_index, 0, keepdims=False)

time: 624 us -> 555 us (0.89)
  waiting for transfers between devices: 72.5 us -> 33.8 us
  Pallas kernels: 335 us -> 320 us
  matrix products: 91.3 us -> 80.7 us
    all_to_all x3, waiting for transfers between devices: 65.1 us -> 27.5 us  [exchange(): lax.all_to_all(packed.reshape(expert_count, -1, packed.shape[-1]), 'exper...]
    pallas_call x1, Pallas kernels: 78.6 us -> 65.5 us  [run_expert(): pl.pallas_call(expert_kernel, grid=(count // 256,), in_specs=[block_rows(...]
    pallas_call x3 -> x1, Pallas kernels: 189 us -> 180 us  [backward(): pl.pallas_call(functools.partial(backward_kernel, first, orders, along, c...]
    another operation x4 -> x0, local copies, waits for them, and re-layouts: 7.58 us -> none
    pallas_call x3 -> x6, Pallas kernels: 44.5 us -> 52 us  [join(): pl.pallas_call(kernel, grid=(count // 256,), in_specs=[block_rows(array.s...]
    dot_general x5 -> x3, matrix products: 45.8 us -> 41.6 us  [dot_first(): lax.dot_general(left, right, contract_first, preferred_element_type=f32)]
    dot_general x5 -> x4, matrix products: 23.1 us -> 18.9 us  [dot(): return jnp.dot(left, right, preferred_element_type=f32)]
  transfers between devices with their start and end apart: 12 -> 12, of which waited for: 7 -> 6; matrix products, arithmetic and copies ran while one was open for 23% -> 23% of each run, Pallas kernels for 42% -> 47%
where the time goes in v3:
time: 555 us; the launch traced here: 545 us
  Pallas kernels  320 us (58%)
  matrix products  80.7 us (15%)
  other arithmetic  39.1 us (7%)
  waiting for transfers between devices  33.8 us (6%)
  starting transfers between devices  30.5 us (5%)
  local copies, waits for them, and re-layouts  21.8 us (4%)
  between operations  18.4 us (3%)
    pallas_call x1, Pallas kernels, backward(): pl.pallas_call(functools.partial(backward_kernel, first, orders, along, c...  180 us
    pallas_call x1, Pallas kernels, run_expert(): pl.pallas_call(expert_kernel, grid=(count // 256,), in_specs=[block_rows(...  65.5 us
    pallas_call x6, Pallas kernels, join(): pl.pallas_call(kernel, grid=(count // 256,), in_specs=[block_rows(array.s...  52 us
    dot_general x3, matrix products, dot_first(): lax.dot_general(left, right, contract_first, preferred_element_type=f32)  41.6 us
    all_to_all x3, waiting for transfers between devices, exchange(): lax.all_to_all(packed.reshape(expert_count, -1, packed.shape[-1]), 'exper...  27.5 us
    pallas_call x1, Pallas kernels, attend(): pl.pallas_call(functools.partial(attend_kernel, min(512, length)), grid=(...  22.9 us
    dot_general x1, matrix products, dot_last(): lax.dot_general(left, right, contract_last, preferred_element_type=f32)  20.1 us
    all_to_all x3, starting transfers between devices, exchange(): lax.all_to_all(packed.reshape(expert_count, -1, packed.shape[-1]), 'exper...  19.6 us
  transfers between devices with their start and end apart: 12, of which 6 were waited for; matrix products, arithmetic and copies ran while one was open for 23% of the time, Pallas kernels for 47%

profile of v3, /device:TPU:24, one launch (start us, length us, event | category | flops | bytes accessed | tf_op | source)
XLA Modules:
  0.0 545.0 jit_solution(14940675944920317465)
XLA Ops:
  9.9 6.1 %all-to-all-start.4 = ((s32[8,1,1024]{2,1,0:T(1,128)}), s32[8,1,1024]{2,1,0:T(1,128)S(1)}, u32[]{:S(2)}, u32[]{:S(2)}) async-start(s32[8,1,1024]{2,1,0:T(1,128)} %broadcast_in_dim.93), calls=%async_computation.4 | async-start | bytes 65536 | tf_op jit(solution)/shard_map/all_to_all | solution.py:1019
  24.0 6.5 %fusion.71 = bf16[1024,1024]{1,0:T(8,128)(2,1)} fusion(s32[1536]{0:T(1024)S(1)} %get-tuple-element.1359, bf16[1,1536,1024]{2,1,0:T(8,128)(2,1)} %param.21), kind=kOutput, calls=%fused_computation.147 | convolution fusion | flops 3223846912 | bytes 5249024 | tf_op jit(solution)/shard_map/dot_general | solution.py:27
  30.5 7.5 %all-to-all-start.5 = ((bf16[8,128,1024]{2,1,0:T(8,128)(2,1)}), bf16[8,128,1024]{2,1,0:T(8,128)(2,1)}, u32[]{:S(2)}, u32[]{:S(2)}) async-start(bf16[8,128,1024]{2,1,0:T(8,128)(2,1)} %bitcast.22), calls=%async_computation.5 | async-start | bytes 4194304 | tf_op jit(solution)/shard_map/all_to_all | solution.py:176
  60.2 6.8 %shard_map.223 = bf16[1024,1024]{1,0:T(8,128)(2,1)} custom-call(s32[1024,1]{1,0:T(8,128)S(1)} %get-tuple-element.1348.near, s32[1,1536]{1,0:T(1,128)S(1)} %get-tuple-element.1360.numbers, bf16[1536,1024]{1,0:T(8,128)(2,1)} %bitcast.183), custom_call_target="tpu_custom_call" | custom-call | flops 3221225472 | bytes 5242880 | tf_op jit(solution)/shard_map/pallas_call | solution.py:507
  72.5 10.4 %all-to-all-done.5 = bf16[8,128,1024]{2,1,0:T(8,128)(2,1)} async-done(((bf16[8,128,1024]{2,1,0:T(8,128)(2,1)}), bf16[8,128,1024]{2,1,0:T(8,128)(2,1)}, u32[]{:S(2)}, u32[]{:S(2)}) %all-to-all-start.5) | async-done | bytes 2097184 | tf_op jit(solution)/shard_map/all_to_all | solution.py:176
  83.5 16.2 %shard_map.224 = (bf16[1024,1024]{1,0:T(8,128)(2,1)S(1)}, bf16[1024,1024]{1,0:T(8,128)(2,1)}, bf16[1024,3072]{1,0:T(8,128)(2,1)}, bf16[1024,1024]{1,0:T(8,128)(2,1)}) custom-call(s32[1024,1]{1,0:T(8,128)S(1)} %get-tuple-element.1347.far, bf16[1024,1024]{1,0:T(8,128)(2,1)} %get-tuple-element.965.kept, bf16[1024,1024]{1,0:T(8,128)(2,1)} %bitcast.23.arrived, ...), custom_call_target="tpu_custom_call" | custom-call | flops 10737418240 | bytes 12582912 | tf_op jit(solution)/shard_map/pallas_call | solution.py:507
  99.8 22.9 %shard_map.225 = (bf16[1024,1024]{1,0:T(8,128)(2,1)S(1)}, f32[8,8,1024]{2,1,0:T(8,128)S(1)}) custom-call(bf16[1024,3072]{1,0:T(8,128)(2,1)} %get-tuple-element.968.q_ref.k_ref.v_ref, bf16[1024,3072]{1,0:T(8,128)(2,1)} %get-tuple-element.968.q_ref.k_ref.v_ref, bf16[1024,3072]{1,0:T(8,128)(2,1)} %get-tuple-element.968.q_ref.k_ref.v_ref), custom_call_target="tpu_custom_call" | custom-call | flops 4294967296 | bytes 8388608 | tf_op jit(solution)/shard_map/pallas_call | solution.py:85
  128.7 6.9 %all-to-all-start.6 = ((bf16[8,128,1024]{2,1,0:T(8,128)(2,1)}), bf16[8,128,1024]{2,1,0:T(8,128)(2,1)}, u32[]{:S(2)}, u32[]{:S(2)}) async-start(bf16[8,128,1024]{2,1,0:T(8,128)(2,1)} %bitcast.165), calls=%async_computation.6 | async-start | bytes 4194304 | tf_op jit(solution)/shard_map/all_to_all | solution.py:176
  140.9 5.5 %shard_map.226 = bf16[1536,1024]{1,0:T(8,128)(2,1)} custom-call(s32[1536,1]{1,0:T(8,128)S(1)} %get-tuple-element.1356.near.near_column, s32[1,1024]{1,0:T(1,128)S(1)} %get-tuple-element.1363.numbers.near_numbers, bf16[1024,1024]{1,0:T(8,128)(2,1)S(1)} %copy-done.37), custom_call_target="tpu_custom_call" | custom-call | flops 3221225472 | bytes 5242880 | tf_op jit(solution)/shard_map/pallas_call | solution.py:507
  146.4 20.1 %convolution_convert_fusion.grad_act = bf16[1536,4096]{1,0:T(8,128)(2,1)} fusion(bf16[1536,1024]{1,0:T(8,128)(2,1)} %bitcast_select_fusion.grad_y, bf16[1,4096,1024]{2,1,0:T(8,128)(2,1)} %all-gather.5.cloned.1.call-done), kind=kOutput, calls=%fused_computation.130 | convolution fusion | flops 12891193344 | bytes 24117248 | tf_op jit(solution)/shard_map/dot_general | solution.py:31
  166.5 15.4 %all-to-all-done.6 = bf16[8,128,1024]{2,1,0:T(8,128)(2,1)} async-done(((bf16[8,128,1024]{2,1,0:T(8,128)(2,1)}), bf16[8,128,1024]{2,1,0:T(8,128)(2,1)}, u32[]{:S(2)}, u32[]{:S(2)}) %all-to-all-start.6) | async-done | bytes 2097184 | tf_op jit(solution)/shard_map/all_to_all | solution.py:176
  182.4 65.5 %shard_map.227 = (bf16[1536,1024]{1,0:T(8,128)(2,1)}, bf16[1536,1024]{1,0:T(8,128)(2,1)}, bf16[1536,4096]{1,0:T(8,128)(2,1)}, bf16[1536,4096]{1,0:T(8,128)(2,1)}...) custom-call(s32[1536,1]{1,0:T(8,128)} %get-tuple-element.1355.far, ...), custom_call_target="tpu_custom_call" | custom-call | flops 38654705664 | bytes 70254592 | tf_op jit(solution)/shard_map/pallas_call | solution.py:577
  248.0 6.5 %fusion.72 = bf16[1024,1024]{1,0:T(8,128)(2,1)} fusion(bf16[1536,1024]{1,0:T(8,128)(2,1)} %get-tuple-element.1820.table, s32[1536]{0:T(1024)S(1)} %copy-done.34), kind=kOutput, calls=%fused_computation.148 | convolution fusion | flops 3223846912 | bytes 5249024 | tf_op jit(solution)/shard_map/dot_general | solution.py:27
  254.5 5.2 all-to-all-start.7
  259.9 19.3 %convolution_convert_fusion.1 = bf16[4096,1024]{1,0:T(8,128)(2,1)} fusion(bf16[1536,4096]{1,0:T(8,128)(2,1)} %get-tuple-element.978, bf16[1536,1024]{1,0:T(8,128)(2,1)} %bitcast_select_fusion.grad_y), kind=kOutput, calls=%fused_computation.131 | convolution fusion | flops 12889096192 | bytes 24117248 | tf_op jit(solution)/shard_map/dot_general | solution.py:35
  279.1 7.0 %shard_map.228 = bf16[1024,1024]{1,0:T(8,128)(2,1)} custom-call(s32[1024,1]{1,0:T(8,128)S(1)} %get-tuple-element.1348.near, s32[1,1536]{1,0:T(1,128)S(1)} %get-tuple-element.1360.numbers, bf16[1536,1024]{1,0:T(8,128)(2,1)} %get-tuple-element.1820.table), custom_call_target="tpu_custom_call" | custom-call | flops 3221225472 | bytes 5242880 | tf_op jit(solution)/shard_map/pallas_call | solution.py:507
  286.1 18.7 %convolution_convert_fusion.2 = bf16[4096,1024]{1,0:T(8,128)(2,1)} fusion(bf16[1536,4096]{1,0:T(8,128)(2,1)} %get-tuple-element.976, bf16[1536,1024]{1,0:T(8,128)(2,1)S(1)} %copy-done.40), kind=kOutput, calls=%fused_computation.132 | convolution fusion | flops 12889096192 | bytes 24117248 | tf_op jit(solution)/shard_map/dot_general | solution.py:35
  313.5 9.0 %shard_map.229 = (bf16[1024,1024]{1,0:T(8,128)(2,1)S(1)}, bf16[1024,1024]{1,0:T(8,128)(2,1)S(1)}) custom-call(s32[1024,1]{1,0:T(8,128)S(1)} %copy-done.8, bf16[1024,1024]{1,0:T(8,128)(2,1)} %get-tuple-element.980.kept, bf16[1024,1024]{1,0:T(8,128)(2,1)} %bitcast.163, bf16[1024,1024]{1,0:T(8,128)(2,1)} %weight.3), custom_call_target="tpu_custom_call" | custom-call | flops 4294967296 | bytes 6291456 | tf_op jit(solution)/shard_map/pallas_call | solution.py:507
  322.6 3.7 convolution_convert_fusion.3.dense_ref
  326.3 179.7 %shard_map.230 = (bf16[1024,3072]{1,0:T(8,128)(2,1)}, bf16[1024,1024]{1,0:T(8,128)(2,1)}, f32[16,1024]{1,0:T(8,128)}, f32[8,1024]{1,0:T(8,128)}, bf16[8,128,1024...) custom-call(bf16[1024,3072]{1,0:T(8,128)(2,1)} %get-tuple-element.968.q_ref.k_ref.v_ref, ...), custom_call_target="tpu_custom_call" | custom-call | flops 10737418240 | bytes 33554432 | tf_op jit(solution)/shard_map/pallas_call | solution.py:895
  506.0 9.4 %convert_element_type.145 = f32[1024,3072]{1,0:T(8,128)} convert(bf16[1024,3072]{1,0:T(8,128)(2,1)} %get-tuple-element.993) | non-fusion elementwise | flops 3145728 | bytes 18874368 | tf_op jit(solution)/shard_map/convert_element_type | solution.py:1161
  522.5 7.6 %shard_map.231 = bf16[1536,1024]{1,0:T(8,128)(2,1)} custom-call(s32[1536,1]{1,0:T(8,128)S(1)} %copy-done.6, bf16[1536,1024]{1,0:T(8,128)(2,1)} %get-tuple-element.990.kept, bf16[1024,1024]{1,0:T(8,128)(2,1)S(1)} %bitcast.153), custom_call_target="tpu_custom_call" | custom-call | flops 3221225472 | bytes 5242880 | tf_op jit(solution)/shard_map/pallas_call | solution.py:507
  530.1 4.1 bitcast_convert_fusion
  534.1 4.1 bitcast_convert_fusion.1
  (173 shorter events, 62.9 us)
Async XLA Ops:
  7.2 139.3 %all-gather.5.cloned.1.call-start = ((), (), s32[]{:S(2)}) async-start(), calls=%async_computation.12 | async-start | bytes 10485760 | tf_op jit(solution)/shard_map/all_gather | solution.py:1095
  9.9 9.5 %all-to-all-start.4 = ((s32[8,1,1024]{2,1,0:T(1,128)}), s32[8,1,1024]{2,1,0:T(1,128)S(1)}, u32[]{:S(2)}, u32[]{:S(2)}) async-start(s32[8,1,1024]{2,1,0:T(1,128)} %broadcast_in_dim.93), calls=%async_computation.4 | async-start | bytes 65536 | tf_op jit(solution)/shard_map/all_to_all | solution.py:1019
  16.7 21.4 %collective-permute-start.2 = (bf16[1,1280]{1,0:T(2,128)(2,1)S(1)}, bf16[1,1280]{1,0:T(2,128)(2,1)S(1)}, u32[]{:S(2)}, u32[]{:S(2)}) collective-permute-start(bf16[1,1280]{1,0:T(2,128)(2,1)S(1)} %constant_dynamic-update-slice_fusion), channel_id=1, source_target_pairs={{0,1},{1,0},{2,3},{3,2},{4,5},{5,4},{6,7},{7,6},{8,9},{9,8},{10,11... | collective-permute-start | bytes 7688 | tf_op jit(solution)/shard_map/ppermute | solution.py:211
  30.5 52.3 %all-to-all-start.5 = ((bf16[8,128,1024]{2,1,0:T(8,128)(2,1)}), bf16[8,128,1024]{2,1,0:T(8,128)(2,1)}, u32[]{:S(2)}, u32[]{:S(2)}) async-start(bf16[8,128,1024]{2,1,0:T(8,128)(2,1)} %bitcast.22), calls=%async_computation.5 | async-start | bytes 4194304 | tf_op jit(solution)/shard_map/all_to_all | solution.py:176
  38.0 144.4 %all-gather.7.cloned.1.call-start = ((), (), s32[]{:S(2)}) async-start(), calls=%async_computation.13 | async-start | bytes 10485760 | tf_op jit(solution)/shard_map/all_gather | solution.py:1094
  38.1 3.8 collective-permute-start.3
  45.7 21.3 %collective-permute-start = (s32[]{:T(128)}, s32[]{:T(128)}, u32[]{:S(2)}, u32[]{:S(2)}) collective-permute-start(s32[]{:T(128)} %select_reduce_fusion.2), channel_id=1, source_target_pairs={{0,1},{1,0},{2,3},{3,2},{4,5},{5,4},{6,7},{7,6},{8,9},{9,8},{10,11... | collective-permute-start | bytes 20 | tf_op jit(solution)/shard_map/ppermute | solution.py:211
  51.3 31.7 %copy-start.7 = (s32[1024,1]{1,0:T(8,128)}, s32[1024,1]{1,0:T(8,128)S(1)}, u32[]{:S(2)}) copy-start(s32[1024,1]{1,0:T(8,128)S(1)} %get-tuple-element.1347.far) | copy-start | bytes 12292
  56.9 84.0 %copy-start = (s32[1536,1]{1,0:T(8,128)}, s32[1536,1]{1,0:T(8,128)S(1)}, u32[]{:S(2)}) copy-start(s32[1536,1]{1,0:T(8,128)S(1)} %get-tuple-element.1356.near.near_column) | copy-start | bytes 18436
  60.2 80.7 %copy-start.10 = (s32[1,1024]{1,0:T(1,128)}, s32[1,1024]{1,0:T(1,128)S(1)}, u32[]{:S(2)}) copy-start(s32[1,1024]{1,0:T(1,128)S(1)} %get-tuple-element.1363.numbers.near_numbers) | copy-start | bytes 12292
  68.2 3.7 collective-permute-start.1
  83.0 16.7 %copy-start.20 = (s32[1,1536]{1,0:T(1,128)}, s32[1,1536]{1,0:T(1,128)S(1)}, u32[]{:S(2)}) copy-start(s32[1,1536]{1,0:T(1,128)S(1)} %get-tuple-element.1949) | copy-start | bytes 18436
  99.7 22.9 %copy-start.1 = (bf16[1024,1024]{1,0:T(8,128)(2,1)}, bf16[1024,1024]{1,0:T(8,128)(2,1)S(1)}, u32[]{:S(2)}) copy-start(bf16[1024,1024]{1,0:T(8,128)(2,1)S(1)} %get-tuple-element.967.tokens_ref) | copy-start | bytes 6291460
  99.8 22.9 %copy-start.35 = (bf16[1024,1024]{1,0:T(8,128)(2,1)S(1)}, bf16[1024,1024]{1,0:T(8,128)(2,1)}, u32[]{:S(2)}) copy-start(bf16[1024,1024]{1,0:T(8,128)(2,1)} %weight.3) | copy-start | bytes 6291460
  128.7 53.2 %all-to-all-start.6 = ((bf16[8,128,1024]{2,1,0:T(8,128)(2,1)}), bf16[8,128,1024]{2,1,0:T(8,128)(2,1)}, u32[]{:S(2)}, u32[]{:S(2)}) async-start(bf16[8,128,1024]{2,1,0:T(8,128)(2,1)} %bitcast.165), calls=%async_computation.6 | async-start | bytes 4194304 | tf_op jit(solution)/shard_map/all_to_all | solution.py:176
  146.4 35.5 %copy-start.38 = (bf16[1024,1024]{1,0:T(8,128)(2,1)S(1)}, bf16[1024,1024]{1,0:T(8,128)(2,1)}, u32[]{:S(2)}) copy-start(bf16[1024,1024]{1,0:T(8,128)(2,1)} %copy-done.36) | copy-start | bytes 6291460
  182.3 65.6 %copy-start.16 = (s32[1536,1]{0,1:T(1,128)}, s32[1536,1]{0,1:T(1,128)S(1)}, u32[]{:S(2)}) copy-start(s32[1536,1]{0,1:T(1,128)S(1)} %get-tuple-element.1965) | copy-start | bytes 18436
  182.3 65.6 %copy-start.18 = (s32[1536,1]{0,1:T(1,128)}, s32[1536,1]{0,1:T(1,128)S(1)}, u32[]{:S(2)}) copy-start(s32[1536,1]{0,1:T(1,128)S(1)} %get-tuple-element.1967) | copy-start | bytes 18436
  182.3 65.6 %copy-start.26 = (s32[1,1024]{1,0:T(1,128)}, s32[1,1024]{1,0:T(1,128)S(1)}, u32[]{:S(2)}) copy-start(s32[1,1024]{1,0:T(1,128)S(1)} %get-tuple-element.1970) | copy-start | bytes 12292
  182.3 65.6 %copy-start.30 = (s32[1,1024]{1,0:T(1,128)}, s32[1,1024]{1,0:T(1,128)S(1)}, u32[]{:S(2)}) copy-start(s32[1,1024]{1,0:T(1,128)S(1)} %get-tuple-element.1972) | copy-start | bytes 12292
  182.4 65.6 %copy-start.34 = (s32[1536]{0:T(1024)S(1)}, s32[1536]{0:T(1024)}, u32[]{:S(2)}) copy-start(s32[1536]{0:T(1024)} %copy-done.33) | copy-start | bytes 18436
  254.5 52.1 %all-to-all-start.7 = ((bf16[8,128,1024]{2,1,0:T(8,128)(2,1)}), bf16[8,128,1024]{2,1,0:T(8,128)(2,1)S(1)}, u32[]{:S(2)}, u32[]{:S(2)}) async-start(bf16[8,128,1024]{2,1,0:T(8,128)(2,1)} %bitcast.164), calls=%async_computation.7 | async-start | bytes 4194304 | tf_op jit(solution)/shard_map/all_to_all | solution.py:176
  259.7 270.4 %reduce-scatter.5.cloned.1.call-start = ((), (), s32[]{:S(2)}) async-start(), calls=%async_computation.11 | async-start | bytes 10485760 | tf_op jit(solution)/shard_map/reduce_scatter | solution.py:1132
  307.9 226.3 %reduce-scatter.3.cloned.1.call-start = ((), (), s32[]{:S(2)}) async-start(), calls=%async_computation.10 | async-start | bytes 10485760 | tf_op jit(solution)/shard_map/reduce_scatter | solution.py:1131
  (28 other events, 136.9 us)
Sparse Core Ops, SparseCore 0:
  9.6 59.3 all-gather.4
  70.5 58.2 all-gather.6
  306.7 99.0 reduce-scatter.4
  408.4 88.8 reduce-scatter.2

commit v4 on v3

--- a/solution.py
+++ b/solution.py
@@ -191,19 +191,38 @@
     return place_rows(remote_column(places, chunk, step), expert_count * chunk, table)
 
 
-def more_rounds(kept, table, source, target, chunk, expert_count, rounds):
-    def again(state):
-        step, sums = state
-        packed = pack(table, source, chunk, expert_count, step)
-        got = select_rows(remote_column(target, chunk, step), exchange(packed, expert_count))
-        return (step + 1, sums + got)
-
-    return lax.while_loop(lambda state: state[0] < rounds, again, (jnp.int32(1), kept))[1]
-
-
-def select_rows(columns, table):
-    chosen = (columns[:, None] == jnp.arange(table.shape[0], dtype=jnp.int32)[None, :]).astype(bf16)
-    return dot(chosen, table).astype(bf16)
+def pack_slots_kernel(starts, limits, table_ref, out_ref):
+    index = pl.program_id(0)
+    rows, window = out_ref.shape[0], min(256, table_ref.shape[0])
+    start = starts[index]
+    base = jnp.minimum(start // 16 * 16, table_ref.shape[0] - window)
+    rank = lax.broadcasted_iota(jnp.int32, (rows, window), 0)
+    place = lax.broadcasted_iota(jnp.int32, (rows, window), 1)
+    chosen = (place == rank + (start - base)) & (rank < limits[index])
+    near = table_ref[pl.ds(pl.multiple_of(base, 16), window), :]
+    out_ref[...] = dot(chosen.astype(bf16), near).astype(bf16)
+
+
+def pack_slots(table, starts, limits, chunk):
+    count, width = starts.shape[0], table.shape[1]
+    return pl.pallas_call(
+        pack_slots_kernel,
+        grid_spec=pltpu.PrefetchScalarGridSpec(
+            num_scalar_prefetch=2,
+            grid=(count,),
+            in_specs=[
+                pl.BlockSpec(
+                    table.shape, lambda index, *_: (0, 0), pipeline_mode=pl.Buffered(1)
+                )
+            ],
+            out_specs=pl.BlockSpec((chunk, width), lambda index, *_: (index, 0)),
+        ),
+        out_shape=jax.ShapeDtypeStruct((count * chunk, width), bf16),
+        compiler_params=pltpu.CompilerParams(vmem_limit_bytes=BIG_VMEM),
+        cost_estimate=pl.CostEstimate(
+            flops=512 * count * chunk * width, bytes_accessed=2 * table.size, transcendentals=0
+        ),
+    )(starts, limits, table)
 
 
 def swap(values, axis, bit):
@@ -450,13 +469,18 @@
     return dot((columns == numbers).astype(bf16), table)
 
 
-def joined_rows(far, kept, arrived):
+def joined_rows(columns, kept, arrived):
     places = lax.broadcasted_iota(jnp.int32, (1, arrived.shape[0]), 1)
-    return pick(far[...], places, arrived[...]) + kept[...].astype(f32)
-
-
-def near_kernel(near, numbers, table, rows_ref):
-    rows_ref[...] = pick(near[...], numbers[...], table[...]).astype(bf16)
+    return pick(columns[:, 1:2], places, arrived[...]) + kept[...].astype(f32)
+
+
+def near_numbers_of(rows):
+    return jnp.where(rows < 0, -2, rows)
+
+
+def near_kernel(columns, numbers, table, rows_ref):
+    chosen = near_numbers_of(numbers[0:1, :])
+    rows_ref[...] = pick(columns[:, 0:1], chosen, table[...]).astype(bf16)
 
 
 def norm_parts(rows):
@@ -473,23 +497,84 @@
     return inverse * (grad_scaled - first - scaled * second)
 
 
-def first_kernel(far, kept, arrived, gain, bias, weight, rows_ref, normed_ref, mixed_ref, turned_ref):
-    rows = joined_rows(far, kept, arrived)
-    rows_ref[...] = rows.astype(bf16)
-    normed = (norm_parts(rows)[0] * gain[...] + bias[...]).astype(bf16)
-    normed_ref[...] = normed
-    turned_ref[...] = normed.T
-    mixed_ref[...] = dot(normed, weight[...]).astype(bf16)
-
-
 def third_kernel(far, kept, arrived, weight, rows_ref, product_ref):
     rows = joined_rows(far, kept, arrived).astype(bf16)
     rows_ref[...] = rows
     product_ref[...] = dot_last(rows, weight[...]).astype(bf16)
 
 
-def last_kernel(far, kept, arrived, rows_ref):
+def last_kernel(far, kept, arrived, *rest):
+    rows_ref = rest[len(rest) // 2]
     rows_ref[...] = joined_rows(far, kept, arrived).astype(bf16)
+    for source, target in zip(rest[: len(rest) // 2], rest[len(rest) // 2 + 1 :]):
+        target[...] = source[...].astype(f32)
+
+
+def again_kernel(columns, kept, arrived, rows_ref):
+    places = lax.broadcasted_iota(jnp.int32, (1, arrived.shape[0]), 1)
+    rows = pick(columns[...], places, arrived[...]) + kept[...].astype(f32)
+    rows_ref[...] = rows.astype(bf16)
+
+
+def first_again_kernel(columns, kept, arrived, gain, bias, weight, rows_ref, normed_ref, mixed_ref, turned_ref):
+    again_kernel(columns, kept, arrived, rows_ref)
+    normed = (norm_parts(rows_ref[...].astype(f32))[0] * gain[...] + bias[...]).astype(bf16)
+    normed_ref[...] = normed
+    mixed_ref[...] = dot(normed, weight[...]).astype(bf16)
+    turned_ref[...] = normed.T
+
+
+def later_rows(step, table, source, target, chunk, expert_count):
+    packed = pack(table, source, chunk, expert_count, step)
+    return remote_column(target, chunk, step)[:, None], exchange(packed, expert_count)
+
+
+def more_rounds(kept, table, source, target, chunk, expert_count, rounds):
+    def again(state):
+        step, sums = state
+        columns, arrived = later_rows(step, table, source, target, chunk, expert_count)
+        (sums,) = join(again_kernel, [columns, sums], [arrived], (table.shape[1],))
+        return (step + 1, sums)
+
+    return lax.while_loop(lambda state: state[0] < rounds, again, (jnp.int32(1), kept))[1]
+
+
+def more_first_rounds(kept, table, source, target, chunk, expert_count, rounds, gain, bias, weight):
+    width = table.shape[1]
+
+    def again(state):
+        step, rows, *_ = state
+        columns, arrived = later_rows(step, table, source, target, chunk, expert_count)
+        rows, normed, mixed, turned = join(
+            first_again_kernel, [columns, rows], [arrived, gain, bias, weight],
+            (width, width, 3 * width), (width,),
+        )
+        return (step + 1, rows, normed, turned, mixed)
+
+    return lax.while_loop(lambda state: state[0] < rounds, again, (jnp.int32(1), *kept))[1:]
+
+
+def finish_rows(far, kept, arrived, sums):
+    steps = 8
+
+    def blocks(array):
+        return pl.BlockSpec((array.shape[0] // steps, array.shape[1]), lambda step: (step, 0))
+
+    count, width = kept.shape
+    return pl.pallas_call(
+        last_kernel,
+        grid=(steps,),
+        in_specs=[blocks(far), blocks(kept), in_full(arrived)] + [blocks(array) for array in sums],
+        out_specs=[blocks(kept)] + [blocks(array) for array in sums],
+        out_shape=[jax.ShapeDtypeStruct(kept.shape, bf16)]
+        + [jax.ShapeDtypeStruct(array.shape, f32) for array in sums],
+        compiler_params=pltpu.CompilerParams(vmem_limit_bytes=BIG_VMEM),
+        cost_estimate=pl.CostEstimate(
+            flops=2 * count * width * arrived.shape[0],
+            bytes_accessed=4 * count * width + 6 * sum(array.size for array in sums),
+            transcendentals=0,
+        ),
+    )(far, kept, arrived, *sums)
 
 
 def block_rows(width):
@@ -523,78 +608,101 @@
 
 
 def expert_kernel(
-    far, kept, live, grad_y, grad_act, arrived, gain, bias,
-    weight_in, bias_in, weight_out, bias_out,
-    out_ref, normed_ref, act_ref, grad_pre_ref, grad_ref, sum_ref, bias_sum_ref,
+    columns, kept, grad_y, grad_act, arrived, gain, bias, bias_in, bias_out, weight_in_hbm, weight_out_hbm,
+    out_ref, normed_ref, act_ref, grad_pre_ref, grad_ref, sum_ref, weight_in, weight_out, load_sem,
 ):
-    rows = joined_rows(far, kept, arrived)
-    scaled, inverse = norm_parts(rows)
-    normed = (scaled * gain[...] + bias[...]).astype(bf16)
-    normed_ref[...] = normed
-    hidden = weight_in.shape[0]
-    block = min(1024, hidden)
+    hidden, width = weight_in.shape
+    block = width
+    loads = []
+    for index, low in enumerate(range(0, hidden, block)):
+        part = pl.ds(low, block)
+        loads.append(
+            [
+                pltpu.make_async_copy(source.at[part], target.at[part], load_sem.at[index, side])
+                for side, (source, target) in enumerate(
+                    ((weight_in_hbm, weight_in), (weight_out_hbm, weight_out))
+                )
+            ]
+        )
+
+    def work(first):
+        if first:
+            for pair in loads:
+                for copy in pair:
+                    copy.start()
+            sum_ref[...] = jnp.zeros_like(sum_ref)
+        rows = joined_rows(columns, kept, arrived)
+        scaled, inverse = norm_parts(rows)
+        normed = (scaled * gain[...] + bias[...]).astype(bf16)
+        normed_ref[...] = normed
+        result = jnp.zeros(rows.shape, f32)
+        grad = jnp.zeros(rows.shape, f32)
+        for number, low in enumerate(range(0, hidden, block)):
+            if first:
+                for copy in loads[number]:
+                    copy.wait()
+            part = slice(low, low + block)
+            pre = dot_last(normed, weight_in[part, :]) + bias_in[:, part]
+            square = pre * pre
+            tangent = jnp.tanh(gelu_c * (pre + 0.044715 * pre * square))
+            half = 0.5 * pre
+            act = (half + half * tangent).astype(bf16)
+            slope = (0.5 + 0.5 * tangent) + half * (1.0 - tangent * tangent) * (
+                gelu_c + (3.0 * 0.044715 * gelu_c) * square
+            )
+            grad_pre = (grad_act[:, part].astype(f32) * slope).astype(bf16)
+            act_ref[:, part] = act
+            grad_pre_ref[:, part] = grad_pre
+            index = 8 + number
+            sum_ref[index : index + 1, :] += jnp.sum(grad_pre.astype(f32), axis=0, keepdims=True)
+            result += dot(act, weight_out[part, :])
+            grad += dot(grad_pre, weight_in[part, :])
+        out = rows + result + bias_out[...]
+        out_ref[...] = jnp.where(columns[:, 4:5] > 0, out, 0.0).astype(bf16)
+        grad_in = grad_y[...].astype(f32)
+        grad_ref[...] = (grad_in + norm_back(grad, scaled, inverse, gain[...])).astype(bf16)
+        sum_ref[2:3, :] += jnp.sum(grad * scaled, axis=0, keepdims=True)
+        sum_ref[3:4, :] += jnp.sum(grad, axis=0, keepdims=True)
+        sum_ref[12:13, :] += jnp.sum(grad_in, axis=0, keepdims=True)
 
     @pl.when(pl.program_id(0) == 0)
     def _():
-        sum_ref[...] = jnp.zeros_like(sum_ref)
-        bias_sum_ref[...] = jnp.zeros_like(bias_sum_ref)
-
-    result = jnp.zeros(rows.shape, f32)
-    grad = jnp.zeros(rows.shape, f32)
-    for low in range(0, hidden, block):
-        part = slice(low, low + block)
-        pre = dot_last(normed, weight_in[part, :]) + bias_in[:, part]
-        square = pre * pre
-        tangent = jnp.tanh(gelu_c * (pre + 0.044715 * pre * square))
-        half = 0.5 * pre
-        act = (half + half * tangent).astype(bf16)
-        slope = (0.5 + 0.5 * tangent) + half * (1.0 - tangent * tangent) * (
-            gelu_c + (3.0 * 0.044715 * gelu_c) * square
-        )
-        grad_pre_f = grad_act[:, part].astype(f32) * slope
-        grad_pre = grad_pre_f.astype(bf16)
-        act_ref[:, part] = act
-        grad_pre_ref[:, part] = grad_pre
-        bias_sum_ref[0:1, part] += jnp.sum(grad_pre.astype(f32), axis=0, keepdims=True)
-        result += dot(act, weight_out[part, :])
-        grad += dot(grad_pre, weight_in[part, :])
-    out = rows + result + bias_out[...]
-    out_ref[...] = jnp.where(live[...] > 0, out, 0.0).astype(bf16)
-    grad_in = grad_y[...].astype(f32)
-    grad_ref[...] = (grad_in + norm_back(grad, scaled, inverse, gain[...])).astype(bf16)
-    sum_ref[0:1, :] += jnp.sum(grad * scaled, axis=0, keepdims=True)
-    sum_ref[1:2, :] += jnp.sum(grad, axis=0, keepdims=True)
-    sum_ref[2:3, :] += jnp.sum(grad_in, axis=0, keepdims=True)
-
-
-def run_expert(blocked, whole, hidden):
+        work(True)
+
+    @pl.when(pl.program_id(0) > 0)
+    def _():
+        work(False)
+
+
+def run_expert(blocked, whole, weights):
     count, width = blocked[1].shape
+    hidden = weights[0].shape[0]
     widths = (width, width, hidden, hidden, width)
-
-    def sums(size):
-        return pl.BlockSpec((8, size), lambda step: (0, 0))
-
     return pl.pallas_call(
         expert_kernel,
         grid=(count // 256,),
         in_specs=[block_rows(array.shape[1]) for array in blocked]
-        + [in_full(array) for array in whole],
-        out_specs=[block_rows(size) for size in widths] + [sums(width), sums(hidden)],
+        + [in_full(array) for array in whole]
+        + [pl.BlockSpec(memory_space=pl.ANY)] * 2,
+        out_specs=[block_rows(size) for size in widths]
+        + [pl.BlockSpec((16, width), lambda step: (0, 0))],
         out_shape=[jax.ShapeDtypeStruct((count, size), bf16) for size in widths]
-        + [jax.ShapeDtypeStruct((8, width), f32), jax.ShapeDtypeStruct((8, hidden), f32)],
+        + [jax.ShapeDtypeStruct((16, width), f32)],
+        scratch_shapes=[pltpu.VMEM((hidden, width), bf16)] * 2
+        + [pltpu.SemaphoreType.DMA((hidden // width, 2))],
         compiler_params=pltpu.CompilerParams(vmem_limit_bytes=58 << 20),
         cost_estimate=pl.CostEstimate(
             flops=6 * count * width * hidden,
             bytes_accessed=2 * count * (5 * width + 3 * hidden) + 4 * width * hidden,
             transcendentals=count * hidden,
         ),
-    )(*blocked, *whole)
+    )(*blocked, *whole, *weights)
 
 
 def backward_kernel(
     first, orders, along, count, pairs,
     q_ref, k_ref, v_ref, context_ref, grad_ref, logs_ref, wq_ref, wk_ref, wv_ref, dense_ref,
-    normed_t, tokens_ref, hidden_ref, gain_ref, norm_ref, send_numbers, near_column, near_numbers,
+    normed_t, tokens_ref, hidden_ref, gain_ref, norm_ref, token_rows, slot_columns,
     mixed_sum, dense_sum, norm_out, bias_out, arrived_ref, near_ref, tokens_grad,
     work, done, core_slots, *scratch
 ):
@@ -788,11 +896,12 @@
         def _():
             total[...] += dot_last(pair_grad[...], weights)
 
-    quarter_rows = packed.shape[1] // 4
+    pieces = swap_send.shape[1]
+    piece_rows = packed.shape[1] // pieces
 
     def swap_rows(step, piece):
         index = others[step]
-        here = pl.ds(piece * quarter_rows, quarter_rows)
+        here = pl.ds(piece * piece_rows, piece_rows)
         return remote(
             packed.at[index, here], arrived_ref.at[own, here],
             swap_send.at[step, piece], swap_recv.at[step, piece], "expert", index
@@ -824,13 +933,13 @@
         chunk = packed.shape[1]
         for index in range(count):
             numbers = index * chunk + lax.broadcasted_iota(jnp.int32, (chunk, 1), 0)
-            packed[index] = dot((send_numbers[...] == numbers).astype(bf16), tokens_grad[...]).astype(bf16)
+            packed[index] = dot((token_rows[1:2, :] == numbers).astype(bf16), tokens_grad[...]).astype(bf16)
         start_swaps([0])
         home_rows().start()
 
     @pl.when(tick == pairs + 2)
     def _():
-        start_swaps([2, 3])
+        start_swaps([2])
 
     @pl.when(tick >= pairs)
     def _():
@@ -839,12 +948,16 @@
     @pl.when(tick == pairs + 1)
     def _():
         start_swaps([1])
+
+    @pl.when(tick == pairs + 2)
+    def _():
+        start_swaps([3])
 
     @pl.when(tick == pairs + 2)
     def _():
         for low in range(0, near_ref.shape[0], 256):
             part = slice(low, low + 256)
-            near_ref[part, :] = pick(near_column[part, :], near_numbers[...], tokens_grad[...]).astype(bf16)
+            near_ref[part, :] = pick(slot_columns[part, 0:1], near_numbers_of(token_rows[0:1, :]), tokens_grad[...]).astype(bf16)
 
     @pl.when(tick == last)
     def _():
@@ -864,20 +977,20 @@
 
         for step in range(len(links)):
             norm_step(step).wait_send()
-        for piece in range(4):
+        for piece in range(pieces):
             for step in range(count - 1):
                 swap_rows(step, piece).wait()
         home_rows().wait()
 
 
 def backward(mixed, context, grad_context, logs, weight, dense, normed_t, tokens, grad_hidden, gain, norms,
-             send_numbers, near_column, near_numbers, first, orders, along, count, chunk):
+             token_rows, slot_columns, first, orders, along, count, chunk):
     length, width = context.shape
     pairs = width // PAIR
     steps = len(orders[0])
     links = 1 + steps + len(along)
     part = length // 4
-    slots = near_column.shape[0]
+    slots = slot_columns.shape[0]
     spread = 1 << len(along)
 
     def columns(offset):
@@ -890,7 +1003,7 @@
         return pl.BlockSpec(shape, lambda tick: (0,) * len(shape))
 
     anywhere = pl.BlockSpec(memory_space=pl.ANY)
-    fixed = (normed_t, tokens, grad_hidden, gain, norms, send_numbers, near_column, near_numbers)
+    fixed = (normed_t, tokens, grad_hidden, gain, norms, token_rows, slot_columns)
     dma = pltpu.SemaphoreType.DMA
     return pl.pallas_call(
         functools.partial(backward_kernel, first, orders, along, count, pairs),
@@ -946,6 +1059,206 @@
     )(mixed, mixed, mixed, context, grad_context, logs, weight, weight, weight, dense, *fixed)
 
 
+def begin_kernel(
+    count, chunk, dp_count, ids_ref, table_hbm, gain_ref, bias_ref, weight_hbm,
+    token_columns, slot_columns, token_rows, slot_rows, info_ref, rows_out, normed_out, turned_out, mixed_out,
+    ids_all, table, weight, packed, arrived, near, rows_work, normed_work, turned_work, mixed_work, most_work, most_slots,
+    ids_send, ids_recv, swap_send, swap_recv, most_send, most_recv, local_sem, out_sem,
+):
+    own = lax.axis_index("expert")
+    others = ring_peers(count)
+    load = pltpu.make_async_copy(table_hbm, table, local_sem.at[0])
+    load.start()
+    load_weight = pltpu.make_async_copy(weight_hbm, weight, local_sem.at[1])
+    load_weight.start()
+    dp_own = lax.axis_index("dp")
+    dp_others = [lax.rem(dp_own + step, dp_count) for step in range(1, dp_count)]
+    greet([("expert", index) for index in others] + [("dp", index) for index in dp_others])
+    sends = [
+        remote(ids_ref, ids_all.at[own], ids_send.at[step], ids_recv.at[step], "expert", index)
+        for step, index in enumerate(others)
+    ]
+    for copy in sends:
+        copy.start()
+    ids_all[own] = ids_ref[...]
+    length, slots = ids_ref.shape[1], table.shape[0]
+    earlier = lax.broadcasted_iota(jnp.int32, (length, length), 0) < lax.broadcasted_iota(
+        jnp.int32, (length, length), 1
+    )
+    earlier = earlier.astype(bf16)
+    for copy in sends:
+        copy.wait()
+
+    own_f = own.astype(f32)
+    rows = [ids_all[index] for index in range(count)]
+    ids = jnp.concatenate(rows, axis=0).astype(f32)
+    lane = lax.broadcasted_iota(jnp.int32, (count, 128), 1).astype(f32)
+    sequence = lax.broadcasted_iota(jnp.int32, (count, 1), 0).astype(f32)
+    counts = jnp.zeros((count, 128), f32)
+    for expert in range(count):
+        taken = jnp.sum((ids == float(expert)).astype(f32), axis=1, keepdims=True)
+        counts = jnp.where(lane == float(expert), taken, counts)
+    fullest = (counts == jnp.max(counts, axis=0, keepdims=True)) & (lane < float(count))
+    fullest = fullest.astype(f32)
+    peaks = jnp.sum(fullest, axis=1, keepdims=True)
+    single = (jnp.max(peaks, axis=0, keepdims=True) == 1.0) & (jnp.min(peaks, axis=0, keepdims=True) == 1.0)
+    owner = jnp.where(single, jnp.sum(fullest * lane, axis=1, keepdims=True), sequence)
+    from_each = jnp.sum(jnp.where(lane == own_f, counts, 0.0), axis=1, keepdims=True)
+    as_row = jnp.sum(jnp.where(lane == sequence, from_each, 0.0), axis=0, keepdims=True)
+    starts = jnp.sum(jnp.where(lane < sequence, as_row, 0.0), axis=1, keepdims=True)
+    away = jnp.max(jnp.where(lane == owner, 0.0, counts), axis=1, keepdims=True)
+    most = jnp.max(away, axis=0, keepdims=True)
+    at_device = lane == owner
+    device_starts = jnp.sum(jnp.where(at_device, starts, 0.0), axis=0, keepdims=True)
+    limits = jnp.where(owner == own_f, 0.0, from_each)
+    device_limits = jnp.sum(jnp.where(at_device, limits, 0.0), axis=0, keepdims=True)
+    most_work[...] = jnp.broadcast_to(most, (8, 128))
+    mosts = [
+        remote(most_work, most_slots.at[step], most_send.at[step], most_recv.at[step], "dp", index)
+        for step, index in enumerate(dp_others)
+    ]
+    for copy in mosts:
+        copy.start()
+
+    def places(inside, home, device, rank):
+        near = jnp.where(inside & home, rank, -1.0)
+        there = inside & ~home
+        far = jnp.where(there & (rank < float(chunk)), device * float(chunk) + rank, -1.0)
+        rank = jnp.where(there, rank, -float(chunk))
+        empty = jnp.zeros((3, rank.shape[1]), f32)
+        return jnp.concatenate([near, far, device, rank, inside.astype(f32), empty], axis=0)
+
+    slot = lax.broadcasted_iota(jnp.int32, (1, slots), 1).astype(f32)
+    used = jnp.zeros((1, slots), f32)
+    slot_rank = jnp.zeros((1, slots), f32)
+    slot_device = jnp.zeros((1, slots), f32)
+    for index in range(count):
+        start = starts[index : index + 1]
+        inside = (slot >= start) & (slot < start + from_each[index : index + 1])
+        used = jnp.where(inside, 1.0, used)
+        slot_rank = jnp.where(inside, slot - start, slot_rank)
+        slot_device = jnp.where(inside, owner[index : index + 1], slot_device)
+    slot_places = places(used > 0.0, slot_device == own_f, slot_device, slot_rank)
+    far_slots = slot_places[1:2]
+
+    load.wait()
+    swaps = []
+    for step, index in enumerate(others):
+        numbers = index * chunk + lax.broadcasted_iota(jnp.int32, (chunk, 1), 0)
+        chosen = (far_slots == numbers.astype(f32)).astype(bf16)
+        packed[step] = dot(chosen, table[...]).astype(bf16)
+        copy = remote(packed.at[step], arrived.at[own], swap_send.at[step], swap_recv.at[step], "expert", index)
+        copy.start()
+        swaps.append(copy)
+    arrived[own] = jnp.zeros(packed.shape[1:], bf16)
+
+    held = jnp.zeros((1, length), f32)
+    for index in range(count):
+        held = jnp.where(owner[index : index + 1] == own_f, rows[index].astype(f32), held)
+    expert = lax.broadcasted_iota(jnp.int32, (16, 1), 0).astype(f32)
+    choose = (held == expert).astype(f32)
+    before = dot(choose.astype(bf16), earlier)
+    token_rank = jnp.sum(choose * before, axis=0, keepdims=True)
+    token_places = places(held >= 0.0, held == own_f, held, token_rank)
+    slot_rows[...] = slot_places.astype(jnp.int32)
+    token_rows[...] = token_places.astype(jnp.int32)
+    slot_turned = slot_places.T
+    token_turned = token_places.T
+    slot_columns[...] = slot_turned.astype(jnp.int32)
+    token_columns[...] = token_turned.astype(jnp.int32)
+    near_slots = jnp.where(slot_places[0:1] < 0.0, -2.0, slot_places[0:1])
+    for low in range(0, length, 256):
+        part = slice(low, low + 256)
+        near[part, :] = pick(token_turned[part, 0:1], near_slots, table[...]).astype(bf16)
+    for copy in mosts:
+        copy.wait()
+    overall = most_work[0:1, :]
+    for step in range(dp_count - 1):
+        overall = jnp.maximum(overall, most_slots[step, 0:1, :])
+    blank = jnp.zeros((5, 128), f32)
+    info = jnp.concatenate([overall, device_starts, device_limits, blank], axis=0)
+    info_ref[...] = info.astype(jnp.int32)
+    load_weight.wait()
+    for copy in swaps:
+        copy.wait()
+    far_places = lax.broadcasted_iota(jnp.int32, (1, count * chunk), 1).astype(f32)
+    stores = []
+    for index, low in enumerate(range(0, length, 256)):
+        part = slice(low, low + 256)
+        there = (token_turned[part, 1:2] == far_places).astype(bf16)
+        got = near[part, :].astype(f32)
+        for source in range(count):
+            got = got + dot(there[:, source * chunk : (source + 1) * chunk], arrived[source])
+        normed = (norm_parts(got)[0] * gain_ref[...] + bias_ref[...]).astype(bf16)
+        rows_work[part, :] = got.astype(bf16)
+        normed_work[part, :] = normed
+        turned_work[:, part] = normed.T
+        mixed_work[part, :] = dot(normed, weight[...]).astype(bf16)
+        here = pl.ds(low, 256)
+        for number, (source, target) in enumerate(
+            ((rows_work, rows_out), (normed_work, normed_out), (mixed_work, mixed_out))
+        ):
+            stores.append(pltpu.make_async_copy(source.at[here], target.at[here], out_sem.at[index, number]))
+            stores[-1].start()
+        stores.append(pltpu.make_async_copy(turned_work.at[:, here], turned_out.at[:, here], out_sem.at[index, 3]))
+        stores[-1].start()
+    for copy in stores:
+        copy.wait()
+
+
+def begin(ids, table, gain, bias, weight, count, chunk, dp_count):
+    length = ids.shape[0]
+    slots, width = table.shape
+    vmem = pl.BlockSpec(memory_space=pltpu.VMEM)
+    anywhere = pl.BlockSpec(memory_space=pl.ANY)
+    whole = jax.ShapeDtypeStruct
+    dma = pltpu.SemaphoreType.DMA
+    return pl.pallas_call(
+        functools.partial(begin_kernel, count, chunk, dp_count),
+        in_specs=[vmem, anywhere, vmem, vmem, anywhere],
+        out_specs=[vmem] * 5 + [anywhere] * 4,
+        out_shape=[
+            whole((length, 8), jnp.int32),
+            whole((slots, 8), jnp.int32),
+            whole((8, length), jnp.int32),
+            whole((8, slots), jnp.int32),
+            whole((8, 128), jnp.int32),
+            whole((length, width), bf16),
+            whole((length, width), bf16),
+            whole((width, length), bf16),
+            whole((length, 3 * width), bf16),
+        ],
+        scratch_shapes=[
+            pltpu.VMEM((count, 1, length), jnp.int32),
+            pltpu.VMEM((slots, width), bf16),
+            pltpu.VMEM(weight.shape, bf16),
+            pltpu.VMEM((count - 1, chunk, width), bf16),
+            pltpu.VMEM((count, chunk, width), bf16),
+            pltpu.VMEM((length, width), bf16),
+            pltpu.VMEM((length, width), bf16),
+            pltpu.VMEM((length, width), bf16),
+            pltpu.VMEM((width, length), bf16),
+            pltpu.VMEM((length, 3 * width), bf16),
+            pltpu.VMEM((8, 128), f32),
+            pltpu.VMEM((dp_count - 1, 8, 128), f32),
+            dma((count - 1,)),
+            dma((count - 1,)),
+            dma((count - 1,)),
+            dma((count - 1,)),
+            dma((dp_count - 1,)),
+            dma((dp_count - 1,)),
+            dma((2,)),
+            dma((length // 256, 4)),
+        ],
+        compiler_params=pltpu.CompilerParams(
+            collective_id=5, has_side_effects=True, vmem_limit_bytes=BIG_VMEM
+        ),
+        cost_estimate=pl.CostEstimate(
+            flops=12 * length * slots * width, bytes_accessed=8 * slots * width, transcendentals=0
+        ),
+    )(ids[None, :], table, gain, bias, weight)
+
+
 def back_kernel(grad_ref, weight_ref, tokens_ref, hidden_ref, gain_ref, out_ref, sum_ref):
     width = gain_ref.shape[1]
     grad = sum(
@@ -1009,81 +1322,54 @@
     cotangent,
 ):
     expert_count = lax.axis_size("expert")
-    own_expert = lax.axis_index("expert")
-    slot_rows = block_input.shape[1]
     model_width = block_input.shape[2]
     seq_ids = expert_ids[0]
     seq_length = seq_ids.shape[0]
-    capacity = 5 * seq_length // expert_count
     chunk = seq_length // expert_count
-    group_ids = lax.all_to_all(
-        jnp.broadcast_to(seq_ids[None], (expert_count, seq_length)),
-        "expert",
-        split_axis=0,
-        concat_axis=0,
-        tiled=True,
-    )
-    devices = jnp.arange(expert_count, dtype=jnp.int32)
-    counts = jnp.sum(
-        (group_ids[:, :, None] == devices[None, None, :]).astype(jnp.int32), axis=1
-    )
-    fullest = jnp.argmax(counts, axis=0).astype(jnp.int32)
-    taken = jnp.sum((fullest[:, None] == devices[None, :]).astype(jnp.int32), axis=0)
-    distinct = jnp.all(taken == 1)
-    held_by = jnp.where(distinct, fullest, devices)
-    owner = jnp.sum(
-        (held_by[:, None] == devices[None, :]).astype(jnp.int32) * devices[:, None], axis=0
-    )
-    held = held_by[own_expert]
-    most = jnp.max(jnp.where(owner[:, None] == devices[None, :], 0, counts))
-    for axis, bit in bits_of("dp"):
-        most = jnp.maximum(most, swap(most, axis, bit))
-    rounds = (most + chunk - 1) // chunk
-    from_each = counts[:, own_expert]
-    ends_at = jnp.cumsum(from_each)
-    starts_at = ends_at - from_each
-    slot_index = jnp.arange(slot_rows, dtype=jnp.int32)
-    passed = (ends_at[None, :] <= slot_index[:, None]).astype(jnp.int32)
-    source = jnp.sum(passed, axis=1)
-    occupied = slot_index < ends_at[-1]
-    within = slot_index - jnp.sum(passed * from_each[None, :], axis=1)
-    at_device = jnp.sum(
-        (source[:, None] == devices[None, :]).astype(jnp.int32) * owner[None, :], axis=1
-    )
-    at_home = at_device == own_expert
-    slot_places = (
-        jnp.where(occupied & at_home, within, -2),
-        at_device,
-        jnp.where(occupied & ~at_home, within, -chunk),
-    )
-    held_ids = lax.dynamic_index_in_dim(group_ids, held, 0, keepdims=False)
-    choose = (held_ids[:, None] == devices[None, :]).astype(jnp.int32)
-    rank_in = jnp.sum((jnp.cumsum(choose, axis=0) - 1) * choose, axis=1)
-    is_own = held_ids == own_expert
-    token_places = (
-        jnp.where(is_own, rank_in, -1),
-        held_ids,
-        jnp.where(is_own, -chunk, rank_in),
-    )
-
-    def start(table, places):
-        return exchange(pack(table, places, chunk, expert_count), expert_count)
-
-    def near_rows(table, source, target):
-        (rows,) = join(
-            near_kernel, [target[0][:, None]], [source[0][None, :], table], (model_width,)
-        )
-        return rows
-
-    def sides(arrived, kept, table, source, target):
-        kept = more_rounds(kept, table, source, target, chunk, expert_count, rounds)
-        return [remote_column(target, chunk, 0)[:, None], kept]
+    dp_index = lax.axis_index("dp")
+    dp_count = lax.axis_size("dp")
 
     def row(values):
         return values.astype(f32).reshape(1, -1)
 
-    dp_index = lax.axis_index("dp")
-    dp_count = lax.axis_size("dp")
+    token_columns, slot_columns, token_rows, slot_rows, info, *first_rows = begin(
+        seq_ids, block_input[0], row(ln1_gain), row(ln1_bias), w_qkv, expert_count, chunk, dp_count
+    )
+    rounds = (info[0, 0] + chunk - 1) // chunk
+    token_places = tuple(token_rows[part] for part in (0, 2, 3))
+    slot_places = tuple(slot_rows[part] for part in (0, 2, 3))
+    token_side = (token_places, token_rows, token_columns)
+    slot_side = (slot_places, slot_rows, slot_columns)
+    device_starts, device_limits = info[1, :expert_count], info[2, :expert_count]
+
+    def start(table):
+        return exchange(pack(table, token_places, chunk, expert_count), expert_count)
+
+    def start_slots(table):
+        packed = pack_slots(table, device_starts, device_limits, chunk)
+        return exchange(packed, expert_count)
+
+    def near_rows(table, source, target):
+        (rows,) = join(near_kernel, [target[2]], [source[1], table], (model_width,))
+        return rows
+
+    def sides(kept, table, source, target):
+        kept = more_rounds(kept, table, source[0], target[0], chunk, expert_count, rounds)
+        return [target[2], kept]
+
+    full_in = lax.all_gather(w_in[0], "dp", axis=0, tiled=True)
+    full_out = lax.all_gather(w_out[0], "dp", axis=0, tiled=True)
+
+    tokens_in, normed_low, normed_t, mixed_qkv = more_first_rounds(
+        first_rows, block_input[0], slot_places, token_places, chunk, expert_count, rounds,
+        row(ln1_gain), row(ln1_bias), w_qkv,
+    )
+    context_low, log_totals = attend(mixed_qkv)
+    hidden = (tokens_in.astype(f32) + dot(context_low, w_o)).astype(bf16)
+    late, b_in, b_out, hidden = lax.optimization_barrier((cotangent[0], b_in, b_out, hidden))
+    arrived = start(hidden)
+    grad_low = jnp.where(slot_columns[:, 4:5] > 0, late, jnp.zeros((), jnp.bfloat16))
+    grad_act = dot_last(grad_low, full_out).astype(bf16)
     biases = jnp.concatenate([b_in, b_out], axis=1)
     for axis, bit in bits_of("dp"):
         got = swap(biases, axis, bit)
@@ -1091,75 +1377,42 @@
         biases = jnp.where(
             upper, jnp.concatenate([got, biases]), jnp.concatenate([biases, got])
         )
-    full_in = lax.all_gather(w_in[0], "dp", axis=0, tiled=True)
-    full_out = lax.all_gather(w_out[0], "dp", axis=0, tiled=True)
     hidden_part = b_in.shape[1]
     full_bias_in = row(biases[:, :hidden_part])
     full_bias_out = row(biases[:, hidden_part:])
-
-    arrived = start(block_input[0], slot_places)
-    near = near_rows(block_input[0], slot_places, token_places)
-    arrived, near = lax.optimization_barrier((arrived, near))
-    tokens_in, normed_low, mixed_qkv, normed_t = join(
-        first_kernel,
-        sides(arrived, near, block_input[0], slot_places, token_places),
-        [arrived, row(ln1_gain), row(ln1_bias), w_qkv],
-        (model_width, model_width, 3 * model_width),
-        (model_width,),
+    near = near_rows(hidden, token_side, slot_side)
+    arrived, grad_act, near = lax.optimization_barrier((arrived, grad_act, near))
+    result, normed_two, act_low, grad_pre, grad_placed, norms = run_expert(
+        sides(near, hidden, token_side, slot_side) + [grad_low, grad_act],
+        [arrived, row(ln2_gain), row(ln2_bias), full_bias_in, full_bias_out],
+        [full_in, full_out],
     )
-    context_low, log_totals = attend(mixed_qkv)
-    hidden = (tokens_in.astype(f32) + dot(context_low, w_o)).astype(bf16)
-    arrived = start(hidden, token_places)
-    live = occupied[:, None]
-    grad_low = jnp.where(live, cotangent[0], jnp.zeros((), jnp.bfloat16))
-    grad_act = dot_last(grad_low, full_out).astype(bf16)
-    near = near_rows(hidden, token_places, slot_places)
-    arrived, grad_act, near = lax.optimization_barrier((arrived, grad_act, near))
-    result, normed_two, act_low, grad_pre, grad_placed, sums_two, bias_sums = run_expert(
-        sides(arrived, near, hidden, token_places, slot_places)
-        + [live.astype(jnp.int32), grad_low, grad_act],
-        [arrived, row(ln2_gain), row(ln2_bias), full_in, full_bias_in, full_out, full_bias_out],
-        full_in.shape[0],
-    )
-    arrived = start(grad_placed, slot_places)
+    arrived = start_slots(grad_placed)
     local_w_in = dot_first(grad_pre, normed_two).astype(bf16)
     local_w_out = dot_first(act_low, grad_low).astype(bf16)
-    near = near_rows(grad_placed, slot_places, token_places)
+    near = near_rows(grad_placed, slot_side, token_side)
     arrived, near, local_w_in, local_w_out = lax.optimization_barrier(
         (arrived, near, local_w_in, local_w_out)
     )
-    grad_w_in = lax.psum_scatter(local_w_in, "dp", scatter_dimension=0, tiled=True).astype(f32)
-    grad_w_out = lax.psum_scatter(local_w_out, "dp", scatter_dimension=0, tiled=True).astype(f32)
+    sum_in = lax.psum_scatter(local_w_in, "dp", scatter_dimension=0, tiled=True)
+    sum_out = lax.psum_scatter(local_w_out, "dp", scatter_dimension=0, tiled=True)
     grad_hidden, grad_context = join(
         third_kernel,
-        sides(arrived, near, grad_placed, slot_places, token_places),
+        sides(near, grad_placed, slot_side, token_side),
         [arrived, w_o],
         (model_width, model_width),
     )
     local_w_o = dot_first(context_low, grad_hidden).astype(bf16)
-    sums_one = jnp.zeros((2, model_width), f32)
-    other_sums = [
-        sums_two[:2],
-        jnp.zeros((4, model_width), f32),
-        bias_sums[0].reshape(-1, model_width),
-        sums_two[2:3],
-        jnp.zeros((3, model_width), f32),
-    ]
     first, orders, _, short, along = plan_orders(
         dp_count, expert_count, 4 * model_width, model_width
     )
     if (seq_length // 4) >> len(orders[0]) >= 16:
-        norms = jnp.concatenate([sums_one, *other_sums])
         mixed_sum, dense_sum, norms, bias_sums, arrived, near, grad_tokens = backward(
             mixed_qkv, context_low, grad_context, log_totals, w_qkv, local_w_o, normed_t,
             tokens_in, grad_hidden, row(ln1_gain), norms,
-            remote_column(token_places, chunk, 0)[None, :],
-            slot_places[0][:, None],
-            token_places[0][None, :],
+            token_rows, slot_columns,
             first, short, along, expert_count, chunk,
         )
-        grad_w_qkv = mixed_sum.astype(f32)
-        grad_w_o = dense_sum.astype(f32)
     else:
         grad_mixed = attend_back(mixed_qkv, context_low, grad_context, log_totals)
         grad_tokens, sums_one = back(grad_mixed, w_qkv, tokens_in, grad_hidden, row(ln1_gain))
@@ -1168,21 +1421,19 @@
             [dot_first(normed_low, grad_mixed[part]).astype(bf16) for part in range(3)]
             + [local_w_o]
         )
-        norms = jnp.concatenate([sums_one[:2], *other_sums])
+        norms = norms.at[:2].set(sums_one[:2])
         summed, norms, bias_sums, arrived = finish(
             dense, norms, packed.reshape(expert_count, chunk, model_width), dp_count
         )
-        near = near_rows(grad_tokens, token_places, slot_places)
-        grad_w_qkv = jnp.concatenate(
+        near = near_rows(grad_tokens, token_side, slot_side)
+        mixed_sum = jnp.concatenate(
             [summed[part * model_width : (part + 1) * model_width] for part in range(3)], axis=1
-        ).astype(f32)
-        grad_w_o = summed[3 * model_width :].astype(f32)
+        )
+        dense_sum = summed[3 * model_width :]
     arrived = arrived.reshape(-1, model_width)
-    (grad_input,) = join(
-        last_kernel,
-        sides(arrived, near, grad_tokens, token_places, slot_places),
-        [arrived],
-        (model_width,),
+    columns, kept = sides(near, grad_tokens, token_side, slot_side)
+    grad_input, grad_w_qkv, grad_w_o, grad_w_in, grad_w_out = finish_rows(
+        columns, kept, arrived, [mixed_sum, dense_sum, sum_in, sum_out]
     )
     grad_ln1_gain, grad_ln1_bias, grad_ln2_gain, grad_ln2_bias = norms[:4]
     full_parts = bias_sums[:4].reshape(dp_count, -1)

time: 555 us -> 529 us (0.953)
  Pallas kernels: 320 us -> 379 us
  other arithmetic: 39.1 us -> 3.34 us
  waiting for transfers between devices: 33.8 us -> 18.6 us
  matrix products: 80.7 us -> 67.6 us
  starting transfers between devices: 30.5 us -> 17.7 us
    pallas_call x0 -> x3, Pallas kernels: none -> 86.4 us  [the longest x1 65.4 us: begin(): pl.pallas_call(functools.partial(begin_kernel, count, chunk, dp_count), i...]
    pallas_call x6 -> x3, Pallas kernels: 52 us -> 22 us  [join(): pl.pallas_call(kernel, grid=(count // 256,), in_specs=[block_rows(array.s...]
    convert_element_type x4 -> x0, other arithmetic: 13.5 us -> none  [the longest x1 9.37 us: body(): grad_w_qkv = mixed_sum.astype(f32)]
    dot_general x4 -> x2, matrix products: 18.9 us -> 6.02 us  [dot(): return jnp.dot(left, right, preferred_element_type=f32)]
    all_to_all x3 -> x2, waiting for transfers between devices: 27.5 us -> 16.7 us  [exchange(): lax.all_to_all(packed.reshape(expert_count, -1, packed.shape[-1]), 'exper...]
    broadcast_in_dim x2 -> x0, other arithmetic: 8.14 us -> none  [the longest x1 4.07 us: body(): grad_w_out[None]]
    all_to_all x1 -> x0, starting transfers between devices: 6.05 us -> none  [body(): lax.all_to_all(jnp.broadcast_to(seq_ids[None], (expert_count, seq_length)...]
    all_to_all x3 -> x2, starting transfers between devices: 19.6 us -> 15.9 us  [exchange(): lax.all_to_all(packed.reshape(expert_count, -1, packed.shape[-1]), 'exper...]
  transfers between devices with their start and end apart: 12 -> 8, of which waited for: 6 -> 2; matrix products, arithmetic and copies ran while one was open for 23% -> 16% of each run, Pallas kernels for 47% -> 57%
where the time goes in v4:
time: 529 us; the launch traced here: 519 us
  Pallas kernels  379 us (72%)
  matrix products  67.6 us (13%)
  waiting for transfers between devices  18.6 us (4%)
  starting transfers between devices  17.7 us (3%)
  local copies, waits for them, and re-layouts  16.5 us (3%)
  between operations  15.4 us (3%)
    pallas_call x1, Pallas kernels, backward(): pl.pallas_call(functools.partial(backward_kernel, first, orders, along, c...  185 us
    pallas_call x1, Pallas kernels, begin(): pl.pallas_call(functools.partial(begin_kernel, count, chunk, dp_count), i...  65.4 us
    pallas_call x1, Pallas kernels, run_expert(): pl.pallas_call(expert_kernel, grid=(count // 256,), in_specs=[block_rows(...  64 us
    dot_general x3, matrix products, dot_first(): lax.dot_general(left, right, contract_first, preferred_element_type=f32)  41.6 us
    pallas_call x1, Pallas kernels, attend(): pl.pallas_call(functools.partial(attend_kernel, min(512, length)), grid=(...  22.4 us
    pallas_call x3, Pallas kernels, join(): pl.pallas_call(kernel, grid=(count // 256,), in_specs=[block_rows(array.s...  22 us
    dot_general x1, matrix products, dot_last(): lax.dot_general(left, right, contract_last, preferred_element_type=f32)  20 us
    all_to_all x2, waiting for transfers between devices, exchange(): lax.all_to_all(packed.reshape(expert_count, -1, packed.shape[-1]), 'exper...  16.7 us
  transfers between devices with their start and end apart: 8, of which 2 were waited for; matrix products, arithmetic and copies ran while one was open for 16% of the time, Pallas kernels for 57%

profile of v4, /device:TPU:24, one launch (start us, length us, event | category | flops | bytes accessed | tf_op | source)
XLA Modules:
  0.0 519.0 jit_solution(6363340077590190743)
XLA Ops:
  8.7 65.4 %shard_map.220 = (s32[1024,8]{1,0:T(8,128)S(1)}, s32[1536,8]{1,0:T(8,128)S(1)}, s32[8,1024]{1,0:T(8,128)S(1)}, s32[8,1536]{1,0:T(8,128)S(1)}, s32[8,128]{1,0:T(8...) custom-call(s32[1,1024]{1,0:T(1,128)S(1)} %copy-done.15, ...), custom_call_target="tpu_custom_call" | custom-call | flops 19327352832 | bytes 12582912 | tf_op jit(solution)/shard_map/pallas_call | solution.py:1216
  79.3 22.4 %shard_map.221 = (bf16[1024,1024]{1,0:T(8,128)(2,1)S(1)}, f32[8,8,1024]{2,1,0:T(8,128)S(1)}) custom-call(bf16[1024,3072]{1,0:T(8,128)(2,1)} %get-tuple-element.1088.q_ref.k_ref.v_ref, bf16[1024,3072]{1,0:T(8,128)(2,1)} %get-tuple-element.1088.q_ref.k_ref.v_ref, bf16[1024,3072]{1,0:T(8,128)(2,1)} %get-tuple-element.1088.q_ref.k_ref.v_ref), custom_call_target="tpu_custom_call" | custom-call | flops 4294967296 | bytes 8388608 | tf_op jit(solution)/shard_map/pallas_call | solution.py:85
  101.8 2.4 add_convert_fusion.table
  104.8 3.7 fusion.50
  108.5 2.1 broadcast_select_fusion.grad_y
  110.6 10.1 %all-to-all-start.4 = ((bf16[8,128,1024]{2,1,0:T(8,128)(2,1)}), bf16[8,128,1024]{2,1,0:T(8,128)(2,1)S(1)}, u32[]{:S(2)}, u32[]{:S(2)}) async-start(bf16[8,128,1024]{2,1,0:T(8,128)(2,1)} %bitcast.116), calls=%async_computation.4 | async-start | bytes 4194304 | tf_op jit(solution)/shard_map/all_to_all | solution.py:176
  120.7 7.1 %shard_map.222 = bf16[1536,1024]{1,0:T(8,128)(2,1)} custom-call(s32[1536,8]{1,0:T(8,128)S(1)} %get-tuple-element.1080.columns.slot_columns.far, s32[8,1024]{1,0:T(8,128)S(1)} %get-tuple-element.1081.numbers.token_rows, bf16[1024,1024]{1,0:T(8,128)(2,1)} %copy-done.49), custom_call_target="tpu_custom_call" | custom-call | flops 3221225472 | bytes 5242880 | tf_op jit(solution)/shard_map/pallas_call | solution.py:592
  127.8 1.6 collective-permute-start.1
  133.1 20.0 %convolution_convert_fusion.grad_act = bf16[1536,4096]{1,0:T(8,128)(2,1)} fusion(bf16[1536,1024]{1,0:T(8,128)(2,1)} %broadcast_select_fusion.grad_y, bf16[1,4096,1024]{2,1,0:T(8,128)(2,1)} %all-gather.5.cloned.1.call-done), kind=kOutput, calls=%fused_computation.106 | convolution fusion | flops 12891193344 | bytes 24117248 | tf_op jit(solution)/shard_map/dot_general | solution.py:31
  153.0 14.9 %all-to-all-done.4 = bf16[8,128,1024]{2,1,0:T(8,128)(2,1)S(1)} async-done(((bf16[8,128,1024]{2,1,0:T(8,128)(2,1)}), bf16[8,128,1024]{2,1,0:T(8,128)(2,1)S(1)}, u32[]{:S(2)}, u32[]{:S(2)}) %all-to-all-start.4) | async-done | bytes 2097184 | tf_op jit(solution)/shard_map/all_to_all | solution.py:176
  169.3 64.0 %shard_map.223 = (bf16[1536,1024]{1,0:T(8,128)(2,1)}, bf16[1536,1024]{1,0:T(8,128)(2,1)}, bf16[1536,4096]{1,0:T(8,128)(2,1)}, bf16[1536,4096]{1,0:T(8,128)(2,1)}...) custom-call(s32[1536,8]{1,0:T(8,128)} %copy-done.3, bf16[1536,1024]{1,0:T(8,128)(2,1)} %get-tuple-element.1093.kept, ...), custom_call_target="tpu_custom_call" | custom-call | flops 38654705664 | bytes 70254592 | tf_op jit(solution)/shard_map/pallas_call | solution.py:681
  233.3 4.8 shard_map.224
  238.1 5.8 %all-to-all-start.5 = ((bf16[8,128,1024]{2,1,0:T(8,128)(2,1)}), bf16[8,128,1024]{2,1,0:T(8,128)(2,1)}, u32[]{:S(2)}, u32[]{:S(2)}) async-start(bf16[8,128,1024]{2,1,0:T(8,128)(2,1)} %bitcast.35), calls=%async_computation.5 | async-start | bytes 4194304 | tf_op jit(solution)/shard_map/all_to_all | solution.py:176
  243.9 19.3 %convolution_convert_fusion.1 = bf16[4096,1024]{1,0:T(8,128)(2,1)} fusion(bf16[1536,4096]{1,0:T(8,128)(2,1)} %get-tuple-element.1103, bf16[1536,1024]{1,0:T(8,128)(2,1)} %broadcast_select_fusion.grad_y), kind=kOutput, calls=%fused_computation.107 | convolution fusion | flops 12889096192 | bytes 24117248 | tf_op jit(solution)/shard_map/dot_general | solution.py:35
  263.3 7.0 %shard_map.225 = bf16[1024,1024]{1,0:T(8,128)(2,1)} custom-call(s32[1024,8]{1,0:T(8,128)S(1)} %copy-done.17, s32[8,1536]{1,0:T(8,128)S(1)} %copy-done.14, bf16[1536,1024]{1,0:T(8,128)(2,1)} %copy-done.29), custom_call_target="tpu_custom_call" | custom-call | flops 3221225472 | bytes 5242880 | tf_op jit(solution)/shard_map/pallas_call | solution.py:592
  270.2 18.5 %convolution_convert_fusion.2 = bf16[4096,1024]{1,0:T(8,128)(2,1)} fusion(bf16[1536,4096]{1,0:T(8,128)(2,1)} %get-tuple-element.1101, bf16[1536,1024]{1,0:T(8,128)(2,1)S(1)} %copy-done.50), kind=kOutput, calls=%fused_computation.108 | convolution fusion | flops 12889096192 | bytes 24117248 | tf_op jit(solution)/shard_map/dot_general | solution.py:35
  288.8 1.8 all-to-all-done.5
  291.4 7.9 %shard_map.226 = (bf16[1024,1024]{1,0:T(8,128)(2,1)S(1)}, bf16[1024,1024]{1,0:T(8,128)(2,1)S(1)}) custom-call(s32[1024,8]{1,0:T(8,128)S(1)} %copy-done.17, bf16[1024,1024]{1,0:T(8,128)(2,1)} %get-tuple-element.1105.kept, bf16[1024,1024]{1,0:T(8,128)(2,1)} %bitcast.36.arrived, bf16[1024,1024]{1,0:T(8,128)(2,1)} %weight.1), custom_call_target="tpu_custom_call" | custom-call | flops 4294967296 | bytes 6291456 | tf_op jit(solution)/shard_map/pallas_call | solution.py:592
  299.4 3.7 convolution_convert_fusion.3.dense_ref
  303.1 184.7 %shard_map.227 = (bf16[1024,3072]{1,0:T(8,128)(2,1)}, bf16[1024,1024]{1,0:T(8,128)(2,1)}, f32[16,1024]{1,0:T(8,128)}, f32[8,1024]{1,0:T(8,128)}, bf16[8,128,1024...) custom-call(bf16[1024,3072]{1,0:T(8,128)(2,1)} %get-tuple-element.1088.q_ref.k_ref.v_ref, ...), custom_call_target="tpu_custom_call" | custom-call | flops 10737418240 | bytes 33554432 | tf_op jit(solution)/shard_map/pallas_call | solution.py:1008
  488.6 1.6 fusion.56
  492.6 1.6 copy-done.7
  494.2 1.6 copy-done.8
  495.8 16.2 %shard_map.228 = (bf16[1536,1024]{1,0:T(8,128)(2,1)}, f32[1024,3072]{1,0:T(8,128)}, f32[1024,1024]{1,0:T(8,128)}, f32[1024,1024]{1,0:T(8,128)}, f32[1024,1024]{1,0:T(8,128)}) custom-call(s32[1536,8]{1,0:T(8,128)S(1)} %copy-done.4, bf16[1536,1024]{1,0:T(8,128)(2,1)} %get-tuple-element.1114.kept, bf16[1024,1024]{1,0:T(8,128)(2,1)S(1)} %bitcast.112, ...), custom_call_target="tpu_custom_call" | custom-call | flops 3221225472 | bytes 44040192 | tf_op jit(solution)/shard_map/pallas_call | solution.py:564
  (120 shorter events, 15.5 us)
Async XLA Ops:
  7.2 125.8 %all-gather.5.cloned.1.call-start = ((), (), s32[]{:S(2)}) async-start(), calls=%async_computation.10 | async-start | bytes 10485760 | tf_op jit(solution)/shard_map/all_gather | solution.py:1361
  7.9 160.0 %all-gather.7.cloned.1.call-start = ((), (), s32[]{:S(2)}) async-start(), calls=%async_computation.11 | async-start | bytes 10485760 | tf_op jit(solution)/shard_map/all_gather | solution.py:1360
  74.9 45.8 %copy-start.3 = (s32[1536,8]{1,0:T(8,128)}, s32[1536,8]{1,0:T(8,128)S(1)}, u32[]{:S(2)}) copy-start(s32[1536,8]{1,0:T(8,128)S(1)} %get-tuple-element.1080.columns.slot_columns.far) | copy-start | bytes 147460
  74.9 45.8 %copy-start.12 = (s32[8,1024]{1,0:T(8,128)}, s32[8,1024]{1,0:T(8,128)S(1)}, u32[]{:S(2)}) copy-start(s32[8,1024]{1,0:T(8,128)S(1)} %get-tuple-element.1081.numbers.token_rows) | copy-start | bytes 98308
  79.3 22.4 %copy-start.31 = (s32[1536]{0:T(1024)}, s32[1536]{0:T(1024)S(1)}, u32[]{:S(2)}) copy-start(s32[1536]{0:T(1024)S(1)} %get-tuple-element.1898) | copy-start | bytes 18436
  79.3 22.4 %copy-start.33 = (s32[1,1536]{1,0:T(1,128)}, s32[1,1536]{1,0:T(1,128)S(1)}, u32[]{:S(2)}) copy-start(s32[1,1536]{1,0:T(1,128)S(1)} %get-tuple-element.1899) | copy-start | bytes 18436
  79.3 22.4 %copy-start.35 = (s32[1,1536]{1,0:T(1,128)}, s32[1,1536]{1,0:T(1,128)S(1)}, u32[]{:S(2)}) copy-start(s32[1,1536]{1,0:T(1,128)S(1)} %get-tuple-element.1900) | copy-start | bytes 18436
  79.3 22.4 %copy-start.22 = (bf16[1024,1024]{1,0:T(8,128)(2,1)S(1)}, bf16[1024,1024]{1,0:T(8,128)(2,1)}, u32[]{:S(2)}) copy-start(bf16[1024,1024]{1,0:T(8,128)(2,1)} %get-tuple-element.1087.tokens_ref) | copy-start | bytes 6291460
  79.3 22.4 %copy-start.47 = (bf16[1024,1024]{1,0:T(8,128)(2,1)S(1)}, bf16[1024,1024]{1,0:T(8,128)(2,1)}, u32[]{:S(2)}) copy-start(bf16[1024,1024]{1,0:T(8,128)(2,1)} %weight.1) | copy-start | bytes 6291460
  104.2 23.5 %collective-permute-start = (bf16[1,1280]{1,0:T(2,128)(2,1)S(1)}, bf16[1,1280]{1,0:T(2,128)(2,1)S(1)}, u32[]{:S(2)}, u32[]{:S(2)}) collective-permute-start(bf16[1,1280]{1,0:T(2,128)(2,1)S(1)} %constant_dynamic-update-slice_fusion), channel_id=1, source_target_pairs={{0,1},{1,0},{2,3},{3,2},{4,5},{5,4},{6,7},{7,6},{8,9},{9,8},{10,11... | collective-permute-start | bytes 7688 | tf_op jit(solution)/shard_map/ppermute | solution.py:230
  110.6 57.4 %all-to-all-start.4 = ((bf16[8,128,1024]{2,1,0:T(8,128)(2,1)}), bf16[8,128,1024]{2,1,0:T(8,128)(2,1)S(1)}, u32[]{:S(2)}, u32[]{:S(2)}) async-start(bf16[8,128,1024]{2,1,0:T(8,128)(2,1)} %bitcast.116), calls=%async_computation.4 | async-start | bytes 4194304 | tf_op jit(solution)/shard_map/all_to_all | solution.py:176
  127.8 4.0 collective-permute-start.1
  133.0 34.9 %copy-start.37 = (s32[1,1024]{1,0:T(1,128)S(1)}, s32[1,1024]{1,0:T(1,128)}, u32[]{:S(2)}) copy-start(s32[1,1024]{1,0:T(1,128)} %get-tuple-element.1826) | copy-start | bytes 12292
  133.1 34.9 %copy-start.39 = (s32[1,1024]{1,0:T(1,128)S(1)}, s32[1,1024]{1,0:T(1,128)}, u32[]{:S(2)}) copy-start(s32[1,1024]{1,0:T(1,128)} %get-tuple-element.1828) | copy-start | bytes 12292
  169.3 64.0 %copy-start.41 = (s32[1024]{0:T(1024)}, s32[1024]{0:T(1024)S(1)}, u32[]{:S(2)}) copy-start(s32[1024]{0:T(1024)S(1)} %get-tuple-element.1903) | copy-start | bytes 12292
  238.1 52.4 %all-to-all-start.5 = ((bf16[8,128,1024]{2,1,0:T(8,128)(2,1)}), bf16[8,128,1024]{2,1,0:T(8,128)(2,1)}, u32[]{:S(2)}, u32[]{:S(2)}) async-start(bf16[8,128,1024]{2,1,0:T(8,128)(2,1)} %bitcast.35), calls=%async_computation.5 | async-start | bytes 4194304 | tf_op jit(solution)/shard_map/all_to_all | solution.py:176
  243.9 247.5 %reduce-scatter.3.cloned.1.call-start = ((), (), s32[]{:S(2)}) async-start(), calls=%async_computation.8 | async-start | bytes 10485760 | tf_op jit(solution)/shard_map/reduce_scatter | solution.py:1397
  243.9 19.3 %copy-start.14 = (s32[8,1536]{1,0:T(8,128)S(1)}, s32[8,1536]{1,0:T(8,128)}, u32[]{:S(2)}) copy-start(s32[8,1536]{1,0:T(8,128)} %copy-done.13) | copy-start | bytes 147460
  243.9 19.3 %copy-start.17 = (s32[1024,8]{1,0:T(8,128)S(1)}, s32[1024,8]{1,0:T(8,128)}, u32[]{:S(2)}) copy-start(s32[1024,8]{1,0:T(8,128)} %copy-done.16) | copy-start | bytes 98308
  290.6 200.8 %reduce-scatter.5.cloned.1.call-start = ((), (), s32[]{:S(2)}) async-start(), calls=%async_computation.9 | async-start | bytes 10485760 | tf_op jit(solution)/shard_map/reduce_scatter | solution.py:1398
  291.4 8.0 %copy-start.6 = (bf16[1024,1024]{1,0:T(8,128)(2,1)S(1)}, bf16[1024,1024]{1,0:T(8,128)(2,1)}, u32[]{:S(2)}) copy-start(bf16[1024,1024]{1,0:T(8,128)(2,1)} %copy-done.5) | copy-start | bytes 6291460
  303.1 188.3 %copy-start.38 = (s32[1,1024]{1,0:T(1,128)S(1)}, s32[1,1024]{1,0:T(1,128)}, u32[]{:S(2)}) copy-start(s32[1,1024]{1,0:T(1,128)} %get-tuple-element.1826) | copy-start | bytes 12292
  303.1 188.3 %copy-start.40 = (s32[1,1024]{1,0:T(1,128)S(1)}, s32[1,1024]{1,0:T(1,128)}, u32[]{:S(2)}) copy-start(s32[1,1024]{1,0:T(1,128)} %get-tuple-element.1828) | copy-start | bytes 12292
  303.1 188.3 %copy-start.42 = (s32[1024]{0:T(1024)S(1)}, s32[1024]{0:T(1024)}, u32[]{:S(2)}) copy-start(s32[1024]{0:T(1024)} %copy-done.41) | copy-start | bytes 12292
  (24 other events, 61.7 us)
Sparse Core Ops, SparseCore 0:
  9.6 59.2 all-gather.4
  70.5 58.3 all-gather.6
  290.7 106.7 reduce-scatter.2
  400.1 83.4 reduce-scatter.4

commit v5 on v4

--- a/solution.py
+++ b/solution.py
@@ -83,7 +83,7 @@
     length, width = mixed.shape[0], mixed.shape[1] // 3
     pairs = width // PAIR
     return pl.pallas_call(
-        functools.partial(attend_kernel, min(512, length)),
+        functools.partial(attend_kernel, min(1024, length)),
         grid=(pairs,),
         in_specs=[pair_columns(length, part * pairs) for part in range(3)],
         out_specs=[pair_columns(length, 0), pair_logs(length)],
@@ -525,6 +525,8 @@
 
 
 def later_rows(step, table, source, target, chunk, expert_count):
+    step, source, target = lax.optimization_barrier((step, source, target))
+    source, target = (tuple(rows[part] for part in (0, 2, 3)) for rows in (source, target))
     packed = pack(table, source, chunk, expert_count, step)
     return remote_column(target, chunk, step)[:, None], exchange(packed, expert_count)
 
@@ -1337,9 +1339,8 @@
     )
     rounds = (info[0, 0] + chunk - 1) // chunk
     token_places = tuple(token_rows[part] for part in (0, 2, 3))
-    slot_places = tuple(slot_rows[part] for part in (0, 2, 3))
-    token_side = (token_places, token_rows, token_columns)
-    slot_side = (slot_places, slot_rows, slot_columns)
+    token_side = (token_rows, token_columns)
+    slot_side = (slot_rows, slot_columns)
     device_starts, device_limits = info[1, :expert_count], info[2, :expert_count]
 
     def start(table):
@@ -1350,18 +1351,18 @@
         return exchange(packed, expert_count)
 
     def near_rows(table, source, target):
-        (rows,) = join(near_kernel, [target[2]], [source[1], table], (model_width,))
+        (rows,) = join(near_kernel, [target[1]], [source[0], table], (model_width,))
         return rows
 
     def sides(kept, table, source, target):
         kept = more_rounds(kept, table, source[0], target[0], chunk, expert_count, rounds)
-        return [target[2], kept]
+        return [target[1], kept]
 
     full_in = lax.all_gather(w_in[0], "dp", axis=0, tiled=True)
     full_out = lax.all_gather(w_out[0], "dp", axis=0, tiled=True)
 
     tokens_in, normed_low, normed_t, mixed_qkv = more_first_rounds(
-        first_rows, block_input[0], slot_places, token_places, chunk, expert_count, rounds,
+        first_rows, block_input[0], slot_rows, token_rows, chunk, expert_count, rounds,
         row(ln1_gain), row(ln1_bias), w_qkv,
     )
     context_low, log_totals = attend(mixed_qkv)
@@ -1431,9 +1432,11 @@
         )
         dense_sum = summed[3 * model_width :]
     arrived = arrived.reshape(-1, model_width)
-    columns, kept = sides(near, grad_tokens, token_side, slot_side)
     grad_input, grad_w_qkv, grad_w_o, grad_w_in, grad_w_out = finish_rows(
-        columns, kept, arrived, [mixed_sum, dense_sum, sum_in, sum_out]
+        slot_columns, near, arrived, [mixed_sum, dense_sum, sum_in, sum_out]
+    )
+    grad_input = more_rounds(
+        grad_input, grad_tokens, token_rows, slot_rows, chunk, expert_count, rounds
     )
     grad_ln1_gain, grad_ln1_bias, grad_ln2_gain, grad_ln2_bias = norms[:4]
     full_parts = bias_sums[:4].reshape(dp_count, -1)

time: 529 us -> 526 us (level)
  transfers between devices with their start and end apart: 8 -> 8, of which waited for: 2 -> 3; matrix products, arithmetic and copies ran while one was open for 16% -> 15% of each run, Pallas kernels for 57% -> 57%
where the time goes in v5:
time: 526 us; the launch traced here: 516 us
  Pallas kernels  379 us (72%)
  matrix products  67.5 us (13%)
  waiting for transfers between devices  21.4 us (4%)
  starting transfers between devices  17.1 us (3%)
  between operations  15.2 us (3%)
  local copies, waits for them, and re-layouts  13 us (2%)
    pallas_call x1, Pallas kernels, backward(): pl.pallas_call(functools.partial(backward_kernel, first, orders, along, c...  183 us
    pallas_call x1, Pallas kernels, begin(): pl.pallas_call(functools.partial(begin_kernel, count, chunk, dp_count), i...  65.3 us
    pallas_call x1, Pallas kernels, run_expert(): pl.pallas_call(expert_kernel, grid=(count // 256,), in_specs=[block_rows(...  64 us
    dot_general x3, matrix products, dot_first(): lax.dot_general(left, right, contract_first, preferred_element_type=f32)  41.5 us
    pallas_call x3, Pallas kernels, join(): pl.pallas_call(kernel, grid=(count // 256,), in_specs=[block_rows(array.s...  22 us
    pallas_call x1, Pallas kernels, attend(): pl.pallas_call(functools.partial(attend_kernel, min(1024, length)), grid=...  21.7 us
    dot_general x1, matrix products, dot_last(): lax.dot_general(left, right, contract_last, preferred_element_type=f32)  20 us
    all_to_all x2, waiting for transfers between devices, exchange(): lax.all_to_all(packed.reshape(expert_count, -1, packed.shape[-1]), 'exper...  17.3 us
  transfers between devices with their start and end apart: 8, of which 3 were waited for; matrix products, arithmetic and copies ran while one was open for 15% of the time, Pallas kernels for 57%

profile of v5, /device:TPU:24, one launch (start us, length us, event | category | flops | bytes accessed | tf_op | source)
XLA Modules:
  0.0 515.9 jit_solution(237107815508725870)
XLA Ops:
  8.7 65.3 %shard_map.220 = (s32[1024,8]{1,0:T(8,128)S(1)}, s32[1536,8]{1,0:T(8,128)S(1)}, s32[8,1024]{1,0:T(8,128)S(1)}, s32[8,1536]{1,0:T(8,128)S(1)}, s32[8,128]{1,0:T(8...) custom-call(s32[1,1024]{1,0:T(1,128)S(1)} %copy-done.12, ...), custom_call_target="tpu_custom_call" | custom-call | flops 19327352832 | bytes 12582912 | tf_op jit(solution)/shard_map/pallas_call | solution.py:1218
  76.5 21.7 %shard_map.221 = (bf16[1024,1024]{1,0:T(8,128)(2,1)S(1)}, f32[8,8,1024]{2,1,0:T(8,128)S(1)}) custom-call(bf16[1024,3072]{1,0:T(8,128)(2,1)} %get-tuple-element.599.q_ref.k_ref.v_ref, bf16[1024,3072]{1,0:T(8,128)(2,1)} %get-tuple-element.599.q_ref.k_ref.v_ref, bf16[1024,3072]{1,0:T(8,128)(2,1)} %get-tuple-element.599.q_ref.k_ref.v_ref), custom_call_target="tpu_custom_call" | custom-call | flops 4294967296 | bytes 8388608 | tf_op jit(solution)/shard_map/pallas_call | solution.py:85
  98.2 2.4 add_convert_fusion.table
  101.3 3.7 fusion.40
  105.0 2.1 broadcast_select_fusion.grad_y
  107.1 10.2 %all-to-all-start.4 = ((bf16[8,128,1024]{2,1,0:T(8,128)(2,1)}), bf16[8,128,1024]{2,1,0:T(8,128)(2,1)S(1)}, u32[]{:S(2)}, u32[]{:S(2)}) async-start(bf16[8,128,1024]{2,1,0:T(8,128)(2,1)} %bitcast.119), calls=%async_computation.4 | async-start | bytes 4194304 | tf_op jit(solution)/shard_map/all_to_all | solution.py:176
  117.3 7.1 %shard_map.222 = bf16[1536,1024]{1,0:T(8,128)(2,1)} custom-call(s32[1536,8]{1,0:T(8,128)S(1)} %get-tuple-element.591.columns.slot_columns.far, s32[8,1024]{1,0:T(8,128)S(1)} %get-tuple-element.1056, bf16[1024,1024]{1,0:T(8,128)(2,1)} %copy-done.34), custom_call_target="tpu_custom_call" | custom-call | flops 3221225472 | bytes 5242880 | tf_op jit(solution)/shard_map/pallas_call | solution.py:594
  124.4 1.6 collective-permute-start.1
  126.0 2.1 collective-permute-done.1
  129.3 20.0 %convolution_convert_fusion.grad_act = bf16[1536,4096]{1,0:T(8,128)(2,1)} fusion(bf16[1536,1024]{1,0:T(8,128)(2,1)} %broadcast_select_fusion.grad_y, bf16[1,4096,1024]{2,1,0:T(8,128)(2,1)} %all-gather.5.cloned.1.call-done), kind=kOutput, calls=%fused_computation.98 | convolution fusion | flops 12891193344 | bytes 24117248 | tf_op jit(solution)/shard_map/dot_general | solution.py:31
  149.3 15.2 %all-to-all-done.4 = bf16[8,128,1024]{2,1,0:T(8,128)(2,1)S(1)} async-done(((bf16[8,128,1024]{2,1,0:T(8,128)(2,1)}), bf16[8,128,1024]{2,1,0:T(8,128)(2,1)S(1)}, u32[]{:S(2)}, u32[]{:S(2)}) %all-to-all-start.4) | async-done | bytes 2097184 | tf_op jit(solution)/shard_map/all_to_all | solution.py:176
  165.9 64.0 %shard_map.223 = (bf16[1536,1024]{1,0:T(8,128)(2,1)}, bf16[1536,1024]{1,0:T(8,128)(2,1)}, bf16[1536,4096]{1,0:T(8,128)(2,1)}, bf16[1536,4096]{1,0:T(8,128)(2,1)}...) custom-call(s32[1536,8]{1,0:T(8,128)} %copy-done.3, bf16[1536,1024]{1,0:T(8,128)(2,1)} %get-tuple-element.604.kept, ...), custom_call_target="tpu_custom_call" | custom-call | flops 38654705664 | bytes 70254592 | tf_op jit(solution)/shard_map/pallas_call | solution.py:683
  229.9 6.5 %shard_map.224 = bf16[1024,1024]{1,0:T(8,128)(2,1)} custom-call(s32[8]{0:T(128)S(1)} %get-tuple-element.709.starts, s32[8]{0:T(128)S(1)} %get-tuple-element.708.limits, bf16[1536,1024]{1,0:T(8,128)(2,1)} %get-tuple-element.997.table_ref.table), custom_call_target="tpu_custom_call" | custom-call | flops 536870912 | bytes 3145728 | tf_op jit(solution)/shard_map/pallas_call | solution.py:208
  236.4 5.2 %all-to-all-start.5 = ((bf16[8,128,1024]{2,1,0:T(8,128)(2,1)}), bf16[8,128,1024]{2,1,0:T(8,128)(2,1)S(1)}, u32[]{:S(2)}, u32[]{:S(2)}) async-start(bf16[8,128,1024]{2,1,0:T(8,128)(2,1)} %bitcast.33), calls=%async_computation.5 | async-start | bytes 4194304 | tf_op jit(solution)/shard_map/all_to_all | solution.py:176
  241.6 19.3 %convolution_convert_fusion.1 = bf16[4096,1024]{1,0:T(8,128)(2,1)} fusion(bf16[1536,4096]{1,0:T(8,128)(2,1)} %get-tuple-element.614, bf16[1536,1024]{1,0:T(8,128)(2,1)} %broadcast_select_fusion.grad_y), kind=kOutput, calls=%fused_computation.99 | convolution fusion | flops 12889096192 | bytes 24117248 | tf_op jit(solution)/shard_map/dot_general | solution.py:35
  260.9 7.0 %shard_map.225 = bf16[1024,1024]{1,0:T(8,128)(2,1)} custom-call(s32[1024,8]{1,0:T(8,128)S(1)} %copy-done.14, s32[8,1536]{1,0:T(8,128)S(1)} %get-tuple-element.1060, bf16[1536,1024]{1,0:T(8,128)(2,1)} %get-tuple-element.997.table_ref.table), custom_call_target="tpu_custom_call" | custom-call | flops 3221225472 | bytes 5242880 | tf_op jit(solution)/shard_map/pallas_call | solution.py:594
  267.9 18.5 %convolution_convert_fusion.2 = bf16[4096,1024]{1,0:T(8,128)(2,1)} fusion(bf16[1536,4096]{1,0:T(8,128)(2,1)} %get-tuple-element.612, bf16[1536,1024]{1,0:T(8,128)(2,1)S(1)} %copy-done.35), kind=kOutput, calls=%fused_computation.100 | convolution fusion | flops 12889096192 | bytes 24117248 | tf_op jit(solution)/shard_map/dot_general | solution.py:35
  286.4 2.1 all-to-all-done.5
  291.4 7.9 %shard_map.226 = (bf16[1024,1024]{1,0:T(8,128)(2,1)S(1)}, bf16[1024,1024]{1,0:T(8,128)(2,1)S(1)}) custom-call(s32[1024,8]{1,0:T(8,128)S(1)} %copy-done.15, bf16[1024,1024]{1,0:T(8,128)(2,1)} %get-tuple-element.616.kept, bf16[1024,1024]{1,0:T(8,128)(2,1)} %bitcast.120, bf16[1024,1024]{1,0:T(8,128)(2,1)} %weight.1), custom_call_target="tpu_custom_call" | custom-call | flops 4294967296 | bytes 6291456 | tf_op jit(solution)/shard_map/pallas_call | solution.py:594
  299.4 3.7 convolution_convert_fusion.3.dense_ref
  303.2 182.9 %shard_map.227 = (bf16[1024,3072]{1,0:T(8,128)(2,1)}, bf16[1024,1024]{1,0:T(8,128)(2,1)}, f32[16,1024]{1,0:T(8,128)}, f32[8,1024]{1,0:T(8,128)}, bf16[8,128,1024...) custom-call(bf16[1024,3072]{1,0:T(8,128)(2,1)} %get-tuple-element.599.q_ref.k_ref.v_ref, ...), custom_call_target="tpu_custom_call" | custom-call | flops 10737418240 | bytes 33554432 | tf_op jit(solution)/shard_map/pallas_call | solution.py:1010
  489.5 1.6 copy-done.7
  491.1 1.6 copy-done.8
  492.7 16.2 %shard_map.228 = (bf16[1536,1024]{1,0:T(8,128)(2,1)}, f32[1024,3072]{1,0:T(8,128)}, f32[1024,1024]{1,0:T(8,128)}, f32[1024,1024]{1,0:T(8,128)}, f32[1024,1024]{1,0:T(8,128)}) custom-call(s32[1536,8]{1,0:T(8,128)S(1)} %copy-done.4, bf16[1536,1024]{1,0:T(8,128)(2,1)} %get-tuple-element.623.kept, bf16[1024,1024]{1,0:T(8,128)(2,1)S(1)} %bitcast.114, ...), custom_call_target="tpu_custom_call" | custom-call | flops 3221225472 | bytes 44040192 | tf_op jit(solution)/shard_map/pallas_call | solution.py:566
  (85 shorter events, 12.9 us)
Async XLA Ops:
  7.2 122.1 %all-gather.5.cloned.1.call-start = ((), (), s32[]{:S(2)}) async-start(), calls=%async_computation.10 | async-start | bytes 10485760 | tf_op jit(solution)/shard_map/all_gather | solution.py:1362
  7.9 156.6 %all-gather.7.cloned.1.call-start = ((), (), s32[]{:S(2)}) async-start(), calls=%async_computation.11 | async-start | bytes 10485760 | tf_op jit(solution)/shard_map/all_gather | solution.py:1361
  74.8 42.4 %copy-start.3 = (s32[1536,8]{1,0:T(8,128)}, s32[1536,8]{1,0:T(8,128)S(1)}, u32[]{:S(2)}) copy-start(s32[1536,8]{1,0:T(8,128)S(1)} %get-tuple-element.591.columns.slot_columns.far) | copy-start | bytes 147460
  76.5 21.7 %copy-start.20 = (bf16[1024,1024]{1,0:T(8,128)(2,1)S(1)}, bf16[1024,1024]{1,0:T(8,128)(2,1)}, u32[]{:S(2)}) copy-start(bf16[1024,1024]{1,0:T(8,128)(2,1)} %get-tuple-element.598.tokens_ref) | copy-start | bytes 6291460
  76.5 21.7 %copy-start.32 = (bf16[1024,1024]{1,0:T(8,128)(2,1)S(1)}, bf16[1024,1024]{1,0:T(8,128)(2,1)}, u32[]{:S(2)}) copy-start(bf16[1024,1024]{1,0:T(8,128)(2,1)} %weight.1) | copy-start | bytes 6291460
  98.2 2.4 copy-start.5
  98.2 2.4 copy-start.11
  98.2 2.4 copy-start.31
  100.6 4.4 copy-start.34
  100.7 23.7 %collective-permute-start = (bf16[1,1280]{1,0:T(2,128)(2,1)S(1)}, bf16[1,1280]{1,0:T(2,128)(2,1)S(1)}, u32[]{:S(2)}, u32[]{:S(2)}) collective-permute-start(bf16[1,1280]{1,0:T(2,128)(2,1)S(1)} %constant_dynamic-update-slice_fusion), channel_id=1, source_target_pairs={{0,1},{1,0},{2,3},{3,2},{4,5},{5,4},{6,7},{7,6},{8,9},{9,8},{10,11... | collective-permute-start | bytes 7688 | tf_op jit(solution)/shard_map/ppermute | solution.py:230
  101.3 3.7 copy-start.25
  107.1 57.5 %all-to-all-start.4 = ((bf16[8,128,1024]{2,1,0:T(8,128)(2,1)}), bf16[8,128,1024]{2,1,0:T(8,128)(2,1)S(1)}, u32[]{:S(2)}, u32[]{:S(2)}) async-start(bf16[8,128,1024]{2,1,0:T(8,128)(2,1)} %bitcast.119), calls=%async_computation.4 | async-start | bytes 4194304 | tf_op jit(solution)/shard_map/all_to_all | solution.py:176
  124.4 3.7 collective-permute-start.1
  236.4 52.1 %all-to-all-start.5 = ((bf16[8,128,1024]{2,1,0:T(8,128)(2,1)}), bf16[8,128,1024]{2,1,0:T(8,128)(2,1)S(1)}, u32[]{:S(2)}, u32[]{:S(2)}) async-start(bf16[8,128,1024]{2,1,0:T(8,128)(2,1)} %bitcast.33), calls=%async_computation.5 | async-start | bytes 4194304 | tf_op jit(solution)/shard_map/all_to_all | solution.py:176
  241.6 247.9 %reduce-scatter.3.cloned.1.call-start = ((), (), s32[]{:S(2)}) async-start(), calls=%async_computation.8 | async-start | bytes 10485760 | tf_op jit(solution)/shard_map/reduce_scatter | solution.py:1398
  241.6 19.3 %copy-start.14 = (s32[1024,8]{1,0:T(8,128)S(1)}, s32[1024,8]{1,0:T(8,128)}, u32[]{:S(2)}) copy-start(s32[1024,8]{1,0:T(8,128)} %copy-done.13) | copy-start | bytes 98308
  260.9 7.0 %copy-start.35 = (bf16[1536,1024]{1,0:T(8,128)(2,1)S(1)}, bf16[1536,1024]{1,0:T(8,128)(2,1)}, u32[]{:S(2)}) copy-start(bf16[1536,1024]{1,0:T(8,128)(2,1)} %get-tuple-element.613) | copy-start | bytes 9437188
  289.8 199.7 %reduce-scatter.5.cloned.1.call-start = ((), (), s32[]{:S(2)}) async-start(), calls=%async_computation.9 | async-start | bytes 10485760 | tf_op jit(solution)/shard_map/reduce_scatter | solution.py:1399
  291.4 8.0 %copy-start.6 = (bf16[1024,1024]{1,0:T(8,128)(2,1)S(1)}, bf16[1024,1024]{1,0:T(8,128)(2,1)}, u32[]{:S(2)}) copy-start(bf16[1024,1024]{1,0:T(8,128)(2,1)} %copy-done.5) | copy-start | bytes 6291460
  299.4 3.8 copy-start.9
  299.4 3.8 copy-start.10
  299.4 3.7 copy-start.21
  299.4 3.7 copy-start.29
  303.1 186.4 %copy-start.4 = (s32[1536,8]{1,0:T(8,128)S(1)}, s32[1536,8]{1,0:T(8,128)}, u32[]{:S(2)}) copy-start(s32[1536,8]{1,0:T(8,128)} %copy-done.3) | copy-start | bytes 147460
  (10 other events, 14.7 us)
Sparse Core Ops, SparseCore 0:
  9.6 59.2 all-gather.4
  70.5 58.3 all-gather.6
  288.6 104.3 reduce-scatter.2
  395.7 85.1 reduce-scatter.4

commit v6 on v5

--- a/solution.py
+++ b/solution.py
@@ -20,6 +20,7 @@
 bf16 = jnp.bfloat16
 PAIR = 2 * HEAD_DIM
 BIG_VMEM = 48 << 20
+FULL_VMEM = 60 << 20
 f32 = jnp.float32
 
 
@@ -570,7 +571,7 @@
         out_specs=[blocks(kept)] + [blocks(array) for array in sums],
         out_shape=[jax.ShapeDtypeStruct(kept.shape, bf16)]
         + [jax.ShapeDtypeStruct(array.shape, f32) for array in sums],
-        compiler_params=pltpu.CompilerParams(vmem_limit_bytes=BIG_VMEM),
+        compiler_params=pltpu.CompilerParams(vmem_limit_bytes=FULL_VMEM),
         cost_estimate=pl.CostEstimate(
             flops=2 * count * width * arrived.shape[0],
             bytes_accessed=4 * count * width + 6 * sum(array.size for array in sums),
@@ -600,7 +601,7 @@
         + [pl.BlockSpec((size, 256), lambda step: (0, step)) for size in turned],
         out_shape=[jax.ShapeDtypeStruct((count, size), bf16) for size in widths]
         + [jax.ShapeDtypeStruct((size, count), bf16) for size in turned],
-        compiler_params=pltpu.CompilerParams(vmem_limit_bytes=BIG_VMEM),
+        compiler_params=pltpu.CompilerParams(vmem_limit_bytes=FULL_VMEM if len(widths) > 1 else BIG_VMEM),
         cost_estimate=pl.CostEstimate(
             flops=2 * count * width * (inside + sum(widths) - width),
             bytes_accessed=2 * (inside * width + count * sum(widths)),
@@ -692,7 +693,7 @@
         + [jax.ShapeDtypeStruct((16, width), f32)],
         scratch_shapes=[pltpu.VMEM((hidden, width), bf16)] * 2
         + [pltpu.SemaphoreType.DMA((hidden // width, 2))],
-        compiler_params=pltpu.CompilerParams(vmem_limit_bytes=58 << 20),
+        compiler_params=pltpu.CompilerParams(vmem_limit_bytes=FULL_VMEM),
         cost_estimate=pl.CostEstimate(
             flops=6 * count * width * hidden,
             bytes_accessed=2 * count * (5 * width + 3 * hidden) + 4 * width * hidden,

time: 526 us -> 523 us (level)
  no operation moved by 1% of the time
where the time goes in v6:
time: 523 us; the launch traced here: 515 us
  Pallas kernels  380 us (73%)
  matrix products  69.7 us (13%)
  waiting for transfers between devices  21.8 us (4%)
  starting transfers between devices  16.7 us (3%)
  between operations  15.2 us (3%)
  local copies, waits for them, and re-layouts  8.79 us (2%)
    pallas_call x1, Pallas kernels, backward(): pl.pallas_call(functools.partial(backward_kernel, first, orders, along, c...  181 us
    pallas_call x1, Pallas kernels, begin(): pl.pallas_call(functools.partial(begin_kernel, count, chunk, dp_count), i...  65.4 us
    pallas_call x1, Pallas kernels, run_expert(): pl.pallas_call(expert_kernel, grid=(count // 256,), in_specs=[block_rows(...  64 us
    dot_general x3, matrix products, dot_first(): lax.dot_general(left, right, contract_first, preferred_element_type=f32)  43.7 us
    pallas_call x3, Pallas kernels, join(): pl.pallas_call(kernel, grid=(count // 256,), in_specs=[block_rows(array.s...  22.9 us
    pallas_call x1, Pallas kernels, attend(): pl.pallas_call(functools.partial(attend_kernel, min(1024, length)), grid=...  22.2 us
    dot_general x1, matrix products, dot_last(): lax.dot_general(left, right, contract_last, preferred_element_type=f32)  20 us
    pallas_call x1, Pallas kernels, finish_rows(): pl.pallas_call(last_kernel, grid=(steps,), in_specs=[blocks(far), blocks(...  18.1 us
  transfers between devices with their start and end apart: 8, of which 3 were waited for; matrix products, arithmetic and copies ran while one was open for 15% of the time, Pallas kernels for 57%

profile of v6, /device:TPU:24, one launch (start us, length us, event | category | flops | bytes accessed | tf_op | source)
XLA Modules:
  0.0 515.4 jit_solution(18107312351309340175)
XLA Ops:
  8.7 65.4 %shard_map.220 = (s32[1024,8]{1,0:T(8,128)S(1)}, s32[1536,8]{1,0:T(8,128)S(1)}, s32[8,1024]{1,0:T(8,128)S(1)}, s32[8,1536]{1,0:T(8,128)S(1)}, s32[8,128]{1,0:T(8...) custom-call(s32[1,1024]{1,0:T(1,128)S(1)} %copy-done.7, ...), custom_call_target="tpu_custom_call" | custom-call | flops 19327352832 | bytes 12582912 | tf_op jit(solution)/shard_map/pallas_call | solution.py:1219
  76.6 22.2 %shard_map.221 = (bf16[1024,1024]{1,0:T(8,128)(2,1)S(1)}, f32[8,8,1024]{2,1,0:T(8,128)S(1)}) custom-call(bf16[1024,3072]{1,0:T(8,128)(2,1)} %get-tuple-element.599.q_ref.k_ref.v_ref, bf16[1024,3072]{1,0:T(8,128)(2,1)} %get-tuple-element.599.q_ref.k_ref.v_ref, bf16[1024,3072]{1,0:T(8,128)(2,1)} %get-tuple-element.599.q_ref.k_ref.v_ref), custom_call_target="tpu_custom_call" | custom-call | flops 4294967296 | bytes 8388608 | tf_op jit(solution)/shard_map/pallas_call | solution.py:86
  98.9 2.3 add_convert_fusion.table
  101.9 3.7 fusion.40
  105.6 2.1 broadcast_select_fusion.grad_y
  107.7 10.2 %all-to-all-start.4 = ((bf16[8,128,1024]{2,1,0:T(8,128)(2,1)}), bf16[8,128,1024]{2,1,0:T(8,128)(2,1)S(1)}, u32[]{:S(2)}, u32[]{:S(2)}) async-start(bf16[8,128,1024]{2,1,0:T(8,128)(2,1)} %bitcast.120), calls=%async_computation.4 | async-start | bytes 4194304 | tf_op jit(solution)/shard_map/all_to_all | solution.py:177
  117.9 7.1 %shard_map.222 = bf16[1536,1024]{1,0:T(8,128)(2,1)} custom-call(s32[1536,8]{1,0:T(8,128)S(1)} %get-tuple-element.591.columns.slot_columns.far, s32[8,1024]{1,0:T(8,128)S(1)} %get-tuple-element.1058, bf16[1024,1024]{1,0:T(8,128)(2,1)} %copy-done.26), custom_call_target="tpu_custom_call" | custom-call | flops 3221225472 | bytes 5242880 | tf_op jit(solution)/shard_map/pallas_call | solution.py:595
  126.1 2.6 collective-permute-done.1
  130.0 20.0 %convolution_convert_fusion.grad_act = bf16[1536,4096]{1,0:T(8,128)(2,1)} fusion(bf16[1536,1024]{1,0:T(8,128)(2,1)} %broadcast_select_fusion.grad_y, bf16[1,4096,1024]{2,1,0:T(8,128)(2,1)} %all-gather.5.cloned.1.call-done), kind=kOutput, calls=%fused_computation.98 | convolution fusion | flops 12891193344 | bytes 24117248 | tf_op jit(solution)/shard_map/dot_general | solution.py:32
  150.0 15.2 %all-to-all-done.4 = bf16[8,128,1024]{2,1,0:T(8,128)(2,1)S(1)} async-done(((bf16[8,128,1024]{2,1,0:T(8,128)(2,1)}), bf16[8,128,1024]{2,1,0:T(8,128)(2,1)S(1)}, u32[]{:S(2)}, u32[]{:S(2)}) %all-to-all-start.4) | async-done | bytes 2097184 | tf_op jit(solution)/shard_map/all_to_all | solution.py:177
  165.2 1.4 copy-done.18
  166.6 64.0 %shard_map.223 = (bf16[1536,1024]{1,0:T(8,128)(2,1)}, bf16[1536,1024]{1,0:T(8,128)(2,1)}, bf16[1536,4096]{1,0:T(8,128)(2,1)}, bf16[1536,4096]{1,0:T(8,128)(2,1)}...) custom-call(s32[1536,8]{1,0:T(8,128)} %copy-done.3, bf16[1536,1024]{1,0:T(8,128)(2,1)} %get-tuple-element.604.kept, ...), custom_call_target="tpu_custom_call" | custom-call | flops 38654705664 | bytes 70254592 | tf_op jit(solution)/shard_map/pallas_call | solution.py:684
  230.6 6.5 %shard_map.224 = bf16[1024,1024]{1,0:T(8,128)(2,1)} custom-call(s32[8]{0:T(128)S(1)} %get-tuple-element.709.starts, s32[8]{0:T(128)S(1)} %get-tuple-element.708.limits, bf16[1536,1024]{1,0:T(8,128)(2,1)} %get-tuple-element.997.table_ref.table), custom_call_target="tpu_custom_call" | custom-call | flops 536870912 | bytes 3145728 | tf_op jit(solution)/shard_map/pallas_call | solution.py:209
  237.1 5.2 %all-to-all-start.5 = ((bf16[8,128,1024]{2,1,0:T(8,128)(2,1)}), bf16[8,128,1024]{2,1,0:T(8,128)(2,1)S(1)}, u32[]{:S(2)}, u32[]{:S(2)}) async-start(bf16[8,128,1024]{2,1,0:T(8,128)(2,1)} %bitcast.33), calls=%async_computation.5 | async-start | bytes 4194304 | tf_op jit(solution)/shard_map/all_to_all | solution.py:177
  242.3 19.3 %convolution_convert_fusion.1 = bf16[4096,1024]{1,0:T(8,128)(2,1)} fusion(bf16[1536,4096]{1,0:T(8,128)(2,1)} %get-tuple-element.614, bf16[1536,1024]{1,0:T(8,128)(2,1)} %broadcast_select_fusion.grad_y), kind=kOutput, calls=%fused_computation.99 | convolution fusion | flops 12889096192 | bytes 24117248 | tf_op jit(solution)/shard_map/dot_general | solution.py:36
  261.6 7.0 %shard_map.225 = bf16[1024,1024]{1,0:T(8,128)(2,1)} custom-call(s32[1024,8]{1,0:T(8,128)S(1)} %copy-done.9, s32[8,1536]{1,0:T(8,128)S(1)} %get-tuple-element.1062, bf16[1536,1024]{1,0:T(8,128)(2,1)} %get-tuple-element.997.table_ref.table), custom_call_target="tpu_custom_call" | custom-call | flops 3221225472 | bytes 5242880 | tf_op jit(solution)/shard_map/pallas_call | solution.py:595
  268.6 18.5 %convolution_convert_fusion.2 = bf16[4096,1024]{1,0:T(8,128)(2,1)} fusion(bf16[1536,4096]{1,0:T(8,128)(2,1)} %get-tuple-element.612, bf16[1536,1024]{1,0:T(8,128)(2,1)S(1)} %copy-done.27), kind=kOutput, calls=%fused_computation.100 | convolution fusion | flops 12889096192 | bytes 24117248 | tf_op jit(solution)/shard_map/dot_general | solution.py:36
  287.1 2.1 all-to-all-done.5
  289.2 1.3 copy-done.19
  291.1 8.9 %shard_map.226 = (bf16[1024,1024]{1,0:T(8,128)(2,1)}, bf16[1024,1024]{1,0:T(8,128)(2,1)}) custom-call(s32[1024,8]{1,0:T(8,128)} %copy-done.8, bf16[1024,1024]{1,0:T(8,128)(2,1)} %get-tuple-element.616.kept, bf16[1024,1024]{1,0:T(8,128)(2,1)} %bitcast.121, bf16[1024,1024]{1,0:T(8,128)(2,1)} %weight.1), custom_call_target="tpu_custom_call" | custom-call | flops 4294967296 | bytes 6291456 | tf_op jit(solution)/shard_map/pallas_call | solution.py:595
  300.0 5.8 %convolution_convert_fusion.3.dense_ref = bf16[1024,1024]{1,0:T(8,128)(2,1)} fusion(bf16[1024,1024]{1,0:T(8,128)(2,1)S(1)} %copy-done.5, bf16[1024,1024]{1,0:T(8,128)(2,1)} %get-tuple-element.620.hidden_ref), kind=kOutput, calls=%fused_computation.107 | convolution fusion | flops 2148532224 | bytes 6291456 | tf_op jit(solution)/shard_map/dot_general | solution.py:36
  305.9 181.0 %shard_map.227 = (bf16[1024,3072]{1,0:T(8,128)(2,1)}, bf16[1024,1024]{1,0:T(8,128)(2,1)}, f32[16,1024]{1,0:T(8,128)}, f32[8,1024]{1,0:T(8,128)}, bf16[8,128,1024...) custom-call(bf16[1024,3072]{1,0:T(8,128)(2,1)} %get-tuple-element.599.q_ref.k_ref.v_ref, ...), custom_call_target="tpu_custom_call" | custom-call | flops 10737418240 | bytes 33554432 | tf_op jit(solution)/shard_map/pallas_call | solution.py:1011
  487.6 1.5 fusion.44
  490.4 18.1 %shard_map.228 = (bf16[1536,1024]{1,0:T(8,128)(2,1)}, f32[1024,3072]{1,0:T(8,128)}, f32[1024,1024]{1,0:T(8,128)}, f32[1024,1024]{1,0:T(8,128)}, f32[1024,1024]{1,0:T(8,128)}) custom-call(s32[1536,8]{1,0:T(8,128)} %copy-done.3, bf16[1536,1024]{1,0:T(8,128)(2,1)} %get-tuple-element.623.kept, bf16[1024,1024]{1,0:T(8,128)(2,1)} %bitcast.118, ...), custom_call_target="tpu_custom_call" | custom-call | flops 3221225472 | bytes 44040192 | tf_op jit(solution)/shard_map/pallas_call | solution.py:567
  (71 shorter events, 8.8 us)
Async XLA Ops:
  7.2 1.5 copy-start.25
  7.2 1.5 copy-start.20
  7.2 1.5 copy-start.7
  7.2 122.8 %all-gather.5.cloned.1.call-start = ((), (), s32[]{:S(2)}) async-start(), calls=%async_computation.10 | async-start | bytes 10485760 | tf_op jit(solution)/shard_map/all_gather | solution.py:1363
  7.9 157.2 %all-gather.7.cloned.1.call-start = ((), (), s32[]{:S(2)}) async-start(), calls=%async_computation.11 | async-start | bytes 10485760 | tf_op jit(solution)/shard_map/all_gather | solution.py:1362
  74.9 43.0 %copy-start.3 = (s32[1536,8]{1,0:T(8,128)}, s32[1536,8]{1,0:T(8,128)S(1)}, u32[]{:S(2)}) copy-start(s32[1536,8]{1,0:T(8,128)S(1)} %get-tuple-element.591.columns.slot_columns.far) | copy-start | bytes 147460
  76.5 22.3 %copy-start.14 = (bf16[1024,1024]{1,0:T(8,128)(2,1)}, bf16[1024,1024]{1,0:T(8,128)(2,1)S(1)}, u32[]{:S(2)}) copy-start(bf16[1024,1024]{1,0:T(8,128)(2,1)S(1)} %get-tuple-element.598.tokens_ref) | copy-start | bytes 6291460
  76.5 22.3 %copy-start.24 = (bf16[1024,1024]{1,0:T(8,128)(2,1)S(1)}, bf16[1024,1024]{1,0:T(8,128)(2,1)}, u32[]{:S(2)}) copy-start(bf16[1024,1024]{1,0:T(8,128)(2,1)} %weight.1) | copy-start | bytes 6291460
  98.8 2.4 copy-start.4
  98.8 2.4 copy-start.6
  98.8 2.4 copy-start.22
  98.9 2.4 copy-start.23
  101.2 4.4 copy-start.26
  101.3 23.7 %collective-permute-start = (bf16[1,1280]{1,0:T(2,128)(2,1)S(1)}, bf16[1,1280]{1,0:T(2,128)(2,1)S(1)}, u32[]{:S(2)}, u32[]{:S(2)}) collective-permute-start(bf16[1,1280]{1,0:T(2,128)(2,1)S(1)} %constant_dynamic-update-slice_fusion), channel_id=1, source_target_pairs={{0,1},{1,0},{2,3},{3,2},{4,5},{5,4},{6,7},{7,6},{8,9},{9,8},{10,11... | collective-permute-start | bytes 7688 | tf_op jit(solution)/shard_map/ppermute | solution.py:231
  101.9 3.7 copy-start.17
  107.7 57.5 %all-to-all-start.4 = ((bf16[8,128,1024]{2,1,0:T(8,128)(2,1)}), bf16[8,128,1024]{2,1,0:T(8,128)(2,1)S(1)}, u32[]{:S(2)}, u32[]{:S(2)}) async-start(bf16[8,128,1024]{2,1,0:T(8,128)(2,1)} %bitcast.120), calls=%async_computation.4 | async-start | bytes 4194304 | tf_op jit(solution)/shard_map/all_to_all | solution.py:177
  125.0 3.7 collective-permute-start.1
  237.1 52.1 %all-to-all-start.5 = ((bf16[8,128,1024]{2,1,0:T(8,128)(2,1)}), bf16[8,128,1024]{2,1,0:T(8,128)(2,1)S(1)}, u32[]{:S(2)}, u32[]{:S(2)}) async-start(bf16[8,128,1024]{2,1,0:T(8,128)(2,1)} %bitcast.33), calls=%async_computation.5 | async-start | bytes 4194304 | tf_op jit(solution)/shard_map/all_to_all | solution.py:177
  242.3 248.0 %reduce-scatter.3.cloned.1.call-start = ((), (), s32[]{:S(2)}) async-start(), calls=%async_computation.8 | async-start | bytes 10485760 | tf_op jit(solution)/shard_map/reduce_scatter | solution.py:1399
  242.3 19.3 %copy-start.9 = (s32[1024,8]{1,0:T(8,128)S(1)}, s32[1024,8]{1,0:T(8,128)}, u32[]{:S(2)}) copy-start(s32[1024,8]{1,0:T(8,128)} %copy-done.8) | copy-start | bytes 98308
  261.6 7.0 %copy-start.27 = (bf16[1536,1024]{1,0:T(8,128)(2,1)S(1)}, bf16[1536,1024]{1,0:T(8,128)(2,1)}, u32[]{:S(2)}) copy-start(bf16[1536,1024]{1,0:T(8,128)(2,1)} %get-tuple-element.613) | copy-start | bytes 9437188
  290.5 199.8 %reduce-scatter.5.cloned.1.call-start = ((), (), s32[]{:S(2)}) async-start(), calls=%async_computation.9 | async-start | bytes 10485760 | tf_op jit(solution)/shard_map/reduce_scatter | solution.py:1400
  291.1 8.9 %copy-start.5 = (bf16[1024,1024]{1,0:T(8,128)(2,1)S(1)}, bf16[1024,1024]{1,0:T(8,128)(2,1)}, u32[]{:S(2)}) copy-start(bf16[1024,1024]{1,0:T(8,128)(2,1)} %copy-done.4) | copy-start | bytes 6291460
  300.0 5.8 %copy-start.21 = (f32[1024]{0:T(1024)S(1)}, f32[1024]{0:T(1024)}, u32[]{:S(2)}) copy-start(f32[1024]{0:T(1024)} %param.23) | copy-start | bytes 12292
  (3 other events, 3.5 us)
Sparse Core Ops, SparseCore 0:
  9.6 59.2 all-gather.4
  70.5 58.2 all-gather.6
  289.4 101.8 reduce-scatter.2
  393.9 86.4 reduce-scatter.4
